TPU v7x, 32 devices: a whole 2x2x4 slice. The times are simulated.
32 devices in a mesh: parts: 2 (over y), tok: 8 (over z, x), hid: 2 (over core).
Axes of the slice: x: 2, y: 2, z: 4, core: 2. Of those that a mesh axis runs over, the one named last changes fastest.
Arguments:
- inputs: bfloat16 [2048, 3072], P(('parts', 'tok')), parts along dimension 0
- hidden_grads: bfloat16 [2048, 8192], P(('parts', 'tok')), parts along dimension 0
- routes: int32 [2048, 2], P(('parts', 'tok')), parts along dimension 0, may hold values from 0 to 7, as said below
Outputs:
- input_tiles: float32 [32, 768, 768], P(('parts', 'tok', 'hid')), parts along dimension 0
- grad_tiles: float32 [32, 2048, 2048], P(('parts', 'tok', 'hid')), parts along dimension 0
There are 2 independent parts, one for each index of `parts`. A program takes and returns all parts, laid end to end along the dimension named above; each array names one. Nothing has to cross between parts.
Inputs may be any that keep to these rules, and one draw needn't show every extreme that they name: `routes`: each row names two different experts. Of the 128 rows of one device at most 40 name expert 0, and on some device exactly 40 do.
All inputs are finite; a program needn't handle non-finite values.
Results may differ from a plain program's by a relative error of at most 0.0003.
Values may be sent and summed in bfloat16 or wider, within the bound.
No kernel may reach another device: no remote copies, remote signals or barrier semaphores. Data moves between devices by JAX's collectives and lax.ppermute only.
A program may use at most 128 MiB of HBM per device.

v0:
```python
import math

import jax
import jax.numpy as jnp
import numpy as np
from jax import lax
from jax.sharding import PartitionSpec as P


def block_table(side):
    first_list = []
    second_list = []
    for owner_chip in range(side * side // 2):
        stripe = owner_chip // side
        column = owner_chip % side
        if column == side - 1:
            first_list.append(stripe)
            second_list.append(side - 1 - stripe)
        elif column < side - 1 - stripe:
            first_list.append(stripe)
            second_list.append(stripe + 1 + column)
        else:
            first_list.append(side - 1 - stripe)
            second_list.append(column + 1)
    return (np.array(first_list, np.int32), np.array(second_list, np.int32))


def compact(values, chosen, capacity):
    ranking = jnp.cumsum(chosen) - 1
    slot_ids = jnp.arange(capacity, dtype=jnp.int32)
    picker = ((ranking[None, :] == slot_ids[:, None]) & (chosen[None, :] == 1)).astype(jnp.bfloat16)
    return jnp.dot(picker, values, preferred_element_type=jnp.float32).astype(jnp.bfloat16)


def outgoing(packed, side, first_ids, second_ids):
    slot_count, feature_count = packed.shape
    blocks = packed.reshape(slot_count, side, feature_count // side)
    return jnp.concatenate([blocks[:, first_ids], blocks[:, second_ids]], axis=2)


def product(flat_data, left_start, right_start, width):
    left = lax.dynamic_slice_in_dim(flat_data, left_start, width, 1)
    right = lax.dynamic_slice_in_dim(flat_data, right_start, width, 1)
    return lax.dot_general(
        left, right, (((0,), (0,)), ((), ())), preferred_element_type=jnp.float32
    )


def shards(inputs, hidden_grads, routes):
    chosen = jnp.any(routes == 0, axis=1).astype(jnp.int32)
    core_index = lax.axis_index("hid")
    chip_index = lax.axis_index("tok")
    device_count = lax.axis_size("tok")
    side = math.isqrt(2 * device_count)
    first_ids, second_ids = block_table(side)
    diagonal = chip_index % side == side - 1
    capacity = chosen.shape[0] * 5 // 16
    packed_inputs = compact(inputs, chosen, capacity)
    packed_grads = compact(hidden_grads, chosen, capacity)
    send_inputs = outgoing(packed_inputs, side, first_ids, second_ids)
    send_grads = outgoing(packed_grads, side, first_ids, second_ids)
    local_count = jnp.sum(chosen)
    got_inputs = lax.all_to_all(send_inputs, "tok", split_axis=1, concat_axis=1, tiled=True)
    total = lax.psum(local_count.astype(jnp.float32), "tok")
    got_grads = lax.all_to_all(send_grads, "tok", split_axis=1, concat_axis=1, tiled=True)
    flat_inputs = got_inputs.reshape(-1, got_inputs.shape[2])
    flat_grads = got_grads.reshape(-1, got_grads.shape[2])
    input_width = flat_inputs.shape[1] // 2
    grad_width = flat_grads.shape[1] // 2
    right_pick = jnp.where(diagonal, core_index, 1 - core_index)
    input_sum = product(
        flat_inputs, core_index * input_width, right_pick * input_width, input_width
    )
    grad_sum = product(flat_grads, core_index * grad_width, right_pick * grad_width, grad_width)
    return ((input_sum / total)[None], (grad_sum / total)[None])


def solution(mesh):
    placed = (P(("parts", "tok"), None), P(("parts", "tok"), None), P(("parts", "tok"), None))
    return jax.shard_map(
        shards,
        mesh=mesh,
        in_specs=placed,
        out_specs=(P(("parts", "tok", "hid"), None, None), P(("parts", "tok", "hid"), None, None)),
        check_vma=False,
    )
```

profile of v0, /device:TPU:8, one launch (start us, length us, event | category | flops | bytes accessed | tf_op | source)
XLA Modules:
  0.0 125.9 jit_solution(7119536039668148183)
XLA Ops:
  0.6 0.0 copy-start
  0.6 0.8 compare_reduce_fusion
  1.5 0.1 copy.17
  1.6 0.2 reduce-window.8
  1.8 0.1 add_reduce_fusion
  1.9 0.7 pad_clamp_fusion.1
  2.6 0.7 pad_clamp_fusion
  3.2 1.4 %convolution_convert_fusion.1 = bf16[40,3072]{1,0:T(8,128)(2,1)S(1)} fusion(bf16[128,3072]{1,0:T(8,128)(2,1)} %param.9, s32[128]{0:T(128)S(1)} %add_reduce_fusion, pred[128]{0:T(512)(128)(4,1)S(1)} %get-tuple-element.2), kind=kOutput, calls=%fused_computation.6 | convolution fusion | flops 31590400 | bytes 1032832 | tf_op jit(solution)/shard_map/dot_general | solution.py:32
  4.6 0.6 gather_fusion
  5.2 0.6 gather_fusion.1
  5.8 1.0 pad_maximum_fusion.1
  6.8 6.3 %all-to-all-start = ((bf16[40,8,1536]{2,0,1:T(8,128)(2,1)}), bf16[40,8,1536]{2,0,1:T(8,128)(2,1)}, u32[]{:S(2)}, u32[]{:S(2)}) async-start(bf16[40,8,1536]{2,0,1:T(8,128)(2,1)} %pad_maximum_fusion.1), calls=%async_computation | async-start | bytes 1966080 | tf_op jit(solution)/shard_map/all_to_all | solution.py:63
  13.1 0.4 convolution_convert_fusion
  13.6 1.7 %gather_fusion.2 = bf16[8,40,2048]{2,1,0:T(8,128)(2,1)} fusion(bf16[40,4,2048]{2,0,1:T(8,128)(2,1)S(1)} %bitcast.26, s32[1024]{0:T(1024)S(1)} %pad_clamp_fusion.1), kind=kCustom, calls=%fused_computation.2 | custom fusion | bytes 2621472 | tf_op jit(solution)/shard_map/gather | solution.py:38
  15.3 1.7 %gather_fusion.3 = bf16[8,40,2048]{2,1,0:T(8,128)(2,1)} fusion(bf16[40,4,2048]{2,0,1:T(8,128)(2,1)S(1)} %bitcast.27, s32[1024]{0:T(1024)S(1)} %pad_clamp_fusion), kind=kCustom, calls=%fused_computation.3 | custom fusion | bytes 2621472 | tf_op jit(solution)/shard_map/gather | solution.py:38
  16.9 3.5 %pad_maximum_fusion = bf16[40,8,4096]{2,0,1:T(8,128)(2,1)} fusion(bf16[40,8,2048]{2,0,1:T(8,128)(2,1)} %bitcast.31, bf16[40,8,2048]{2,0,1:T(8,128)(2,1)} %bitcast.30), kind=kLoop, calls=%fused_computation.7 | loop fusion | flops 5242880 | bytes 5242880 | tf_op jit(solution)/shard_map/concatenate | solution.py:38
  20.4 14.9 %all-to-all-done = bf16[40,8,1536]{2,0,1:T(8,128)(2,1)} async-done(((bf16[40,8,1536]{2,0,1:T(8,128)(2,1)}), bf16[40,8,1536]{2,0,1:T(8,128)(2,1)}, u32[]{:S(2)}, u32[]{:S(2)}) %all-to-all-start) | async-done | bytes 983072 | tf_op jit(solution)/shard_map/all_to_all | solution.py:63
  35.4 6.5 %all-to-all-start.1 = ((bf16[40,8,4096]{2,0,1:T(8,128)(2,1)}), bf16[40,8,4096]{2,0,1:T(8,128)(2,1)}, u32[]{:S(2)}, u32[]{:S(2)}) async-start(bf16[40,8,4096]{2,0,1:T(8,128)(2,1)} %pad_maximum_fusion), calls=%async_computation.1 | async-start | bytes 5242880 | tf_op jit(solution)/shard_map/all_to_all | solution.py:65
  41.9 0.6 convert_reduce_fusion
  43.1 66.0 %psum.7 = f32[]{:T(128)} all-reduce(f32[]{:T(128)S(6)} %convert_element_type.36), channel_id=1, replica_groups=mesh['parts'=2,'tok'=8,'hid'=2] {'tok'}, use_global_device_ids=true, to_apply=%region_3.4 | all-reduce | flops 1 | bytes 8 | tf_op jit(solution)/shard_map/psum | solution.py:64
  109.2 1.5 %copy.31 = bf16[40,8,1536]{2,1,0:T(8,128)(2,1)S(1)} copy(bf16[40,8,1536]{2,0,1:T(8,128)(2,1)} %all-to-all-done) | data formatting | bytes 1966080 | tf_op jit(solution)/shard_map/all_to_all | solution.py:63
  110.6 2.9 %divide_bitcast_fusion.1 = f32[1,768,768]{2,1,0:T(8,128)} fusion(f32[]{:T(128)} %psum.7, bf16[320,1536]{1,0:T(8,128)(2,1)S(1)} %bitcast.36, s32[]{:T(128)S(6)} %select_n.39, s32[]{:T(128)S(6)} %select_n.36), kind=kOutput, calls=%fused_computation.9 | convolution fusion | flops 378077184 | bytes 3342348 | tf_op jit(solution)/shard_map/dot_general | solution.py:44
  113.5 3.2 %copy.30 = bf16[40,8,4096]{2,1,0:T(8,128)(2,1)S(1)} copy(bf16[40,8,4096]{2,0,1:T(8,128)(2,1)} %all-to-all-done.1) | data formatting | bytes 5242880 | tf_op jit(solution)/shard_map/all_to_all | solution.py:65
  116.7 9.2 %divide_bitcast_fusion = f32[1,2048,2048]{2,1,0:T(8,128)} fusion(f32[]{:T(128)} %psum.7, bf16[320,4096]{1,0:T(8,128)(2,1)S(1)} %bitcast.33, s32[]{:T(128)S(6)} %select_n.43, s32[]{:T(128)S(6)} %select_n.42), kind=kOutput, calls=%fused_computation.4 | convolution fusion | flops 2688548864 | bytes 19398668 | tf_op jit(solution)/shard_map/dot_general | solution.py:44
  (5 shorter events, 0.1 us)
Async XLA Ops:
  0.6 12.5 %copy-start = (bf16[128,8192]{1,0:T(8,128)(2,1)S(1)}, bf16[128,8192]{1,0:T(8,128)(2,1)}, u32[]{:S(2)}) copy-start(bf16[128,8192]{1,0:T(8,128)(2,1)} %param.10) | copy-start | bytes 6291460
  6.8 28.5 %all-to-all-start = ((bf16[40,8,1536]{2,0,1:T(8,128)(2,1)}), bf16[40,8,1536]{2,0,1:T(8,128)(2,1)}, u32[]{:S(2)}, u32[]{:S(2)}) async-start(bf16[40,8,1536]{2,0,1:T(8,128)(2,1)} %pad_maximum_fusion.1), calls=%async_computation | async-start | bytes 1966080 | tf_op jit(solution)/shard_map/all_to_all | solution.py:63
  35.4 78.1 %all-to-all-start.1 = ((bf16[40,8,4096]{2,0,1:T(8,128)(2,1)}), bf16[40,8,4096]{2,0,1:T(8,128)(2,1)}, u32[]{:S(2)}, u32[]{:S(2)}) async-start(bf16[40,8,4096]{2,0,1:T(8,128)(2,1)} %pad_maximum_fusion), calls=%async_computation.1 | async-start | bytes 5242880 | tf_op jit(solution)/shard_map/all_to_all | solution.py:65
where the time goes:
time: 126 us
  blocking collectives  66 us (52%)
  waiting for transfers between devices  14.9 us (12%)
  matrix products  13.8 us (11%)
  starting transfers between devices  12.7 us (10%)
  local copies, waits for them, and re-layouts  9.39 us (7%)
  other arithmetic  7.63 us (6%)
  between operations  1.36 us (1%)
    psum x1, blocking collectives, shards(): total = lax.psum(local_count.astype(jnp.float32), 'tok')  66 us
    all_to_all x1, waiting for transfers between devices, shards(): lax.all_to_all(send_inputs, 'tok', split_axis=1, concat_axis=1, tiled=True)  14.9 us
    dot_general x2, matrix products, product(): lax.dot_general(left, right, (((0,), (0,)), ((), ())), preferred_element_...  12 us
    all_to_all x1, starting transfers between devices, shards(): lax.all_to_all(send_grads, 'tok', split_axis=1, concat_axis=1, tiled=True)  6.48 us
    all_to_all x1, starting transfers between devices, shards(): lax.all_to_all(send_inputs, 'tok', split_axis=1, concat_axis=1, tiled=True)  6.25 us
    concatenate x2, other arithmetic, outgoing(): jnp.concatenate([blocks[:, first_ids], blocks[:, second_ids]], axis=2)  4.54 us
    all_to_all x1, local copies, waits for them, and re-layouts, shards(): lax.all_to_all(send_grads, 'tok', split_axis=1, concat_axis=1, tiled=True)  3.18 us
  transfers between devices with their start and end apart: 2, of which 1 were waited for; matrix products, arithmetic and copies ran while one was open for 10% of the time, Pallas kernels for 0%

commit v1 on v0

--- a/solution.py
+++ b/solution.py
@@ -1,10 +1,16 @@
+import functools
 import math
 
 import jax
 import jax.numpy as jnp
 import numpy as np
 from jax import lax
+from jax.experimental import pallas as pl
+from jax.experimental.pallas import tpu as pltpu
 from jax.sharding import PartitionSpec as P
+
+VMEM_LIMIT = 56 * 1024 * 1024
+SLOT_ROWS = 48
 
 
 def block_table(side):
@@ -46,7 +52,7 @@
     )
 
 
-def shards(inputs, hidden_grads, routes):
+def shards_any(inputs, hidden_grads, routes):
     chosen = jnp.any(routes == 0, axis=1).astype(jnp.int32)
     core_index = lax.axis_index("hid")
     chip_index = lax.axis_index("tok")
@@ -75,10 +81,234 @@
     return ((input_sum / total)[None], (grad_sum / total)[None])
 
 
+N_X = 2
+N_Z = 4
+
+
+def slot_table():
+    first_ids, second_ids = block_table(4)
+    slots = np.zeros((N_Z, N_X, 3), np.int32)
+    for z in range(N_Z):
+        zero = {int(first_ids[z * N_X]), int(second_ids[z * N_X])}
+        one = {int(first_ids[z * N_X + 1]), int(second_ids[z * N_X + 1])}
+        common = max(zero & one)
+        (a,) = zero - {common}
+        (b,) = one - {common}
+        slots[z, 0] = (a, common, b)
+        slots[z, 1] = (b, common, a)
+    return slots
+
+
+def pack_kernel(mark, table_ref, routes_ref, values_ref, own_ref, x_ref, *rest):
+    z_refs, half_ref = rest[:-1], rest[-1]
+    capacity, half = x_ref.shape[1:]
+    width = 2 * half
+    chosen = (routes_ref[0:1, :] == 0) | (routes_ref[1:2, :] == 0)
+    tokens = chosen.shape[1]
+    flags = jnp.where(chosen, 1.0, 0.0)
+    before = (
+        lax.broadcasted_iota(jnp.int32, (tokens, tokens), 0)
+        <= lax.broadcasted_iota(jnp.int32, (tokens, tokens), 1)
+    )
+    rank = jnp.dot(
+        flags.astype(jnp.bfloat16),
+        jnp.where(before, 1.0, 0.0).astype(jnp.bfloat16),
+        preferred_element_type=jnp.float32,
+    )
+    count = jnp.sum(flags)
+    slot = lax.broadcasted_iota(jnp.int32, (capacity, tokens), 0).astype(jnp.float32) + 1.0
+    picker = jnp.where((rank == slot) & chosen, 1.0, 0.0).astype(jnp.bfloat16)
+    core = table_ref[0]
+    empty = (
+        (lax.broadcasted_iota(jnp.int32, (capacity, 128), 0).astype(jnp.float32) >= count)
+        & (lax.broadcasted_iota(jnp.int32, (capacity, 128), 1) == 0)
+    )
+
+    def pick(block, part):
+        start = pl.multiple_of(block * width + part * half, 128)
+        return jnp.dot(
+            picker, values_ref[:, pl.ds(start, half)], preferred_element_type=jnp.float32
+        )
+
+    def put(ref, row, column, block, part):
+        got = pick(block, part)
+        if mark:
+            head = jnp.where(empty & (part == 0), jnp.inf, got[:, :128])
+            ref[row, :, column : column + 128] = head.astype(jnp.bfloat16)
+            ref[row, :, column + 128 : column + half] = got[:, 128:].astype(jnp.bfloat16)
+        else:
+            ref[row, :, column : column + half] = got.astype(jnp.bfloat16)
+
+    for block in range(4):
+        put(half_ref, block, 0, block, core)
+    for i, ref in enumerate(z_refs):
+        for row in range(3):
+            ref[row] = half_ref[table_ref[4 + 3 * i + row]]
+    for row in range(2):
+        x_ref[row] = half_ref[table_ref[2 + row]]
+    for row in range(2):
+        for part in range(2):
+            put(own_ref, row, part * half, table_ref[1 + row], part)
+
+
+def pack(mark, table, routes_t, values, capacity):
+    half = values.shape[1] // 8
+    shapes = [(2, capacity, 2 * half), (2, capacity, half)] + [(3, capacity, half)] * 3
+    vmem = pl.BlockSpec(memory_space=pltpu.VMEM)
+    return pl.pallas_call(
+        functools.partial(pack_kernel, mark),
+        out_shape=[jax.ShapeDtypeStruct(s, jnp.bfloat16) for s in shapes],
+        in_specs=[pl.BlockSpec(memory_space=pltpu.SMEM), vmem, vmem],
+        out_specs=[vmem] * len(shapes),
+        scratch_shapes=[pltpu.VMEM((4, capacity, half), jnp.bfloat16)],
+        compiler_params=pltpu.CompilerParams(vmem_limit_bytes=VMEM_LIMIT),
+        cost_estimate=pl.CostEstimate(
+            flops=2 * capacity * values.size, bytes_accessed=2 * values.size, transcendentals=0
+        ),
+    )(table, routes_t, values)
+
+
+def tile_kernel(marked, table_ref, *refs):
+    refs = list(refs)
+    count_in = None if marked else refs.pop(0)
+    own_ref = refs.pop(0)
+    z_refs = [refs.pop(0) for _ in range(3)]
+    hz_refs = [refs.pop(0) for _ in range(3)]
+    x_refs = [refs.pop(0) for _ in range(4)]
+    hx_refs = [refs.pop(0) for _ in range(4)]
+    out_ref = refs.pop(0)
+    count_out = refs.pop(0) if marked else None
+    data_ref, scale_ref = refs
+    capacity, half = x_refs[0].shape[1:]
+    step = pl.program_id(0)
+    rows_out = out_ref.shape[1]
+    core = table_ref[0]
+    left = table_ref[1]
+    right = table_ref[2]
+
+    @pl.when(step == 0)
+    def _():
+        slots = data_ref.shape[1] // SLOT_ROWS
+        for block in range(2):
+            for slot in range(slots):
+                data_ref[block, slot * SLOT_ROWS + 32 : (slot + 1) * SLOT_ROWS, :] = jnp.zeros(
+                    (SLOT_ROWS - 32, 2 * half), jnp.bfloat16
+                )
+        mine = pl.multiple_of(core * half, 128)
+        other = pl.multiple_of((1 - core) * half, 128)
+        for block in range(2):
+            data_ref[block, 0:capacity, :] = own_ref[block]
+            for i in range(3):
+                rows = pl.ds((1 + i) * SLOT_ROWS, capacity)
+                data_ref[block, rows, pl.ds(mine, half)] = z_refs[i][block]
+                data_ref[block, rows, pl.ds(other, half)] = hz_refs[i][block]
+            for i in range(4):
+                rows = pl.ds((4 + i) * SLOT_ROWS, capacity)
+                data_ref[block, rows, pl.ds(mine, half)] = x_refs[i][1 - block]
+                data_ref[block, rows, pl.ds(other, half)] = hx_refs[i][1 - block]
+        if marked:
+            for block in range(2):
+                head = data_ref[block, :, 0:128].astype(jnp.float32)
+                gone = head == jnp.inf
+                if block == 0:
+                    count = capacity * slots - jnp.sum(jnp.where(gone, 1.0, 0.0))
+                    scale_ref[0] = 1.0 / count
+                    count_out[0] = 1.0 / count
+                data_ref[block, :, 0:128] = jnp.where(gone, 0.0, head).astype(jnp.bfloat16)
+        else:
+            scale_ref[0] = count_in[0]
+
+    start = pl.multiple_of(step * rows_out, rows_out)
+    product_ = lax.dot_general(
+        data_ref[left, :, pl.ds(start, rows_out)],
+        data_ref[right],
+        (((0,), (0,)), ((), ())),
+        preferred_element_type=jnp.float32,
+    )
+    out_ref[0] = product_ * scale_ref[0]
+
+
+def tile(table, scale, own, z_got, hz_got, x_got, hx_got, rows_out):
+    marked = scale is None
+    width = own.shape[2]
+    operands = [table] + ([] if marked else [scale]) + [own, *z_got, *hz_got, *x_got, *hx_got]
+    smem = pl.BlockSpec(memory_space=pltpu.SMEM)
+    vmem = pl.BlockSpec(memory_space=pltpu.VMEM)
+    n_smem = 1 if marked else 2
+    out_shape = [jax.ShapeDtypeStruct((1, width, width), jnp.float32)]
+    out_specs = [pl.BlockSpec((1, rows_out, width), lambda i: (0, i, 0))]
+    if marked:
+        out_shape.append(jax.ShapeDtypeStruct((1,), jnp.float32))
+        out_specs.append(smem)
+    slots = 8
+    return pl.pallas_call(
+        functools.partial(tile_kernel, marked),
+        grid=(width // rows_out,),
+        out_shape=out_shape,
+        in_specs=[smem] * n_smem + [vmem] * (len(operands) - n_smem),
+        out_specs=out_specs,
+        scratch_shapes=[
+            pltpu.VMEM((2, slots * SLOT_ROWS, width), jnp.bfloat16),
+            pltpu.SMEM((1,), jnp.float32),
+        ],
+        compiler_params=pltpu.CompilerParams(vmem_limit_bytes=VMEM_LIMIT),
+        cost_estimate=pl.CostEstimate(
+            flops=2 * slots * SLOT_ROWS * width * width,
+            bytes_accessed=4 * width * width,
+            transcendentals=0,
+        ),
+    )(*operands)
+
+
+def z_pairs(distance):
+    return [
+        (z * N_X + x, ((z + distance) % N_Z) * N_X + x) for z in range(N_Z) for x in range(N_X)
+    ]
+
+
+X_PAIRS = [(chip, chip ^ 1) for chip in range(N_Z * N_X)]
+CORE_PAIRS = [(0, 1), (1, 0)]
+
+
+def spread(own, x_send, z_sends):
+    z_got = [lax.ppermute(send, "tok", z_pairs(d)) for d, send in zip((1, 3, 2), z_sends)]
+    x_got = [lax.ppermute(x_send, "tok", X_PAIRS)]
+    x_got += [lax.ppermute(got[1:], "tok", X_PAIRS) for got in z_got]
+    hz_got = [lax.ppermute(got[:2], "hid", CORE_PAIRS) for got in z_got]
+    hx_got = [lax.ppermute(got, "hid", CORE_PAIRS) for got in x_got]
+    return own, z_got, hz_got, x_got, hx_got
+
+
+def shards_eight(inputs, hidden_grads, routes):
+    core = lax.axis_index("hid").astype(jnp.int32)
+    chip = lax.axis_index("tok").astype(jnp.int32)
+    plane, column = chip // N_X, chip % N_X
+    capacity = routes.shape[0] * 5 // 16
+    slots = jnp.asarray(slot_table())
+    entries = [core[None], slots[plane, column]]
+    entries += [slots[(plane + d) % N_Z, column] for d in (1, 3, 2)]
+    pack_table = jnp.concatenate(entries)
+    first_ids, second_ids = block_table(4)
+    keep = slot_table()[np.arange(8) // N_X, np.arange(8) % N_X, 0]
+    first_is_common = jnp.asarray((keep != first_ids).astype(np.int32))[chip]
+    diagonal = (chip % 4 == 3).astype(jnp.int32)
+    left = jnp.where(core == 0, first_is_common, 1 - first_is_common)
+    right = jnp.where(diagonal == 1, left, 1 - left)
+    tile_table = jnp.stack([core, left, right])
+    routes_t = routes.T
+    own, x_send, *z_sends = pack(True, pack_table, routes_t, hidden_grads, capacity)
+    own_i, x_send_i, *z_sends_i = pack(False, pack_table, routes_t, inputs, capacity)
+    grad_parts = spread(own, x_send, z_sends)
+    input_parts = spread(own_i, x_send_i, z_sends_i)
+    grad_tile, scale = tile(tile_table, None, *grad_parts, 256)
+    (input_tile,) = tile(tile_table, scale, *input_parts, 256)
+    return input_tile, grad_tile
+
+
 def solution(mesh):
     placed = (P(("parts", "tok"), None), P(("parts", "tok"), None), P(("parts", "tok"), None))
     return jax.shard_map(
-        shards,
+        shards_eight if mesh.shape["tok"] == N_X * N_Z else shards_any,
         mesh=mesh,
         in_specs=placed,
         out_specs=(P(("parts", "tok", "hid"), None, None), P(("parts", "tok", "hid"), None, None)),

time: 126 us -> 84.6 us (0.67)
  the two profiles are of different devices: /device:TPU:8 before, /device:TPU:11 now
where the time goes in v1:
time: 84.6 us; the launch traced here: 84.3 us
  starting transfers between devices  29.6 us (35%)
  waiting for transfers between devices  27.5 us (33%)
  Pallas kernels  21.5 us (25%)
  local copies, waits for them, and re-layouts  2.81 us (3%)
  between operations  2.39 us (3%)
    ppermute x6, waiting for transfers between devices, spread(): lax.ppermute(send, 'tok', z_pairs(d))  22.8 us
    pallas_call x2, Pallas kernels, tile(): pl.pallas_call(functools.partial(tile_kernel, marked), grid=(width // row...  16.1 us
    ppermute x8, starting transfers between devices, spread(): hx_got = [lax.ppermute(got, 'hid', CORE_PAIRS) for got in x_got]  10.9 us
    ppermute x6, starting transfers between devices, spread(): lax.ppermute(send, 'tok', z_pairs(d))  7.09 us
    ppermute x6, starting transfers between devices, spread(): hz_got = [lax.ppermute(got[:2], 'hid', CORE_PAIRS) for got in z_got]  6.76 us
    pallas_call x2, Pallas kernels, pack(): pl.pallas_call(functools.partial(pack_kernel, mark), out_shape=[jax.Shape...  5.41 us
    ppermute x6, starting transfers between devices, spread(): x_got += [lax.ppermute(got[1:], 'tok', X_PAIRS) for got in z_got]  4.41 us
    ppermute x2, waiting for transfers between devices, spread(): x_got = [lax.ppermute(x_send, 'tok', X_PAIRS)]  3.01 us
  transfers between devices with their start and end apart: 28, of which 5 were waited for; matrix products, arithmetic and copies ran while one was open for 1% of the time, Pallas kernels for 17%

profile of v1, /device:TPU:11, one launch (start us, length us, event | category | flops | bytes accessed | tf_op | source)
XLA Modules:
  0.0 84.3 jit_solution(7065456997677275977)
XLA Ops:
  0.7 0.7 fusion.3
  1.5 0.6 concatenate.3.table_ref
  2.0 2.3 %shard_map.70 = (bf16[2,40,768]{2,1,0:T(8,128)(2,1)}, bf16[2,40,384]{2,1,0:T(8,128)(2,1)}, bf16[3,40,384]{2,1,0:T(8,128)(2,1)}, bf16[3,40,384]{2,1,0:T(8,128)(2,1)}, bf16[3,40,384]{2,1,0:T(8,128)(2,1)}) custom-call(s32[13]{0:T(128)} %concatenate.3.table_ref, s32[2,128]{1,0:T(2,128)} %bitcast.13, bf16[128,3072]{1,0:T(8,128)(2,1)} %values_ref.3), custom_call_target="tpu_custom_call" | custom-call | flops 31457280 | bytes 786432 | tf_op jit(solution)/shard_map/pallas_call | solution.py:158
  4.4 1.3 %collective-permute-start.14 = (bf16[3,40,384]{2,1,0:T(8,128)(2,1)}, bf16[3,40,384]{2,1,0:T(8,128)(2,1)S(1)}, u32[]{:S(2)}, u32[]{:S(2)}) collective-permute-start(bf16[3,40,384]{2,1,0:T(8,128)(2,1)} %get-tuple-element.21), channel_id=1, source_target_pairs={{0,4},{2,6},{4,8},{6,10},{8,12},{10,14},{12,0},{14,2},{1,5},{3,7},... | collective-permute-start | bytes 276488 | tf_op jit(solution)/shard_map/ppermute | solution.py:274
  5.7 3.1 %shard_map.68 = (bf16[2,40,2048]{2,1,0:T(8,128)(2,1)}, bf16[2,40,1024]{2,1,0:T(8,128)(2,1)}, bf16[3,40,1024]{2,1,0:T(8,128)(2,1)}, bf16[3,40,1024]{2,1,0:T(8,128)(2,1)}, bf16[3,40,1024]{2,1,0:T(8,128)(2,1)}) custom-call(s32[13]{0:T(128)} %concatenate.3.table_ref, s32[2,128]{1,0:T(2,128)} %bitcast.14, bf16[128,8192]{1,0:T(8,128)(2,1)} %values_ref.2), custom_call_target="tpu_custom_call" | custom-call | flops 83886080 | bytes 2097152 | tf_op jit(solution)/shard_map/pallas_call | solution.py:158
  8.8 1.3 %collective-permute-start = (bf16[3,40,1024]{2,1,0:T(8,128)(2,1)}, bf16[3,40,1024]{2,1,0:T(8,128)(2,1)S(1)}, u32[]{:S(2)}, u32[]{:S(2)}) collective-permute-start(bf16[3,40,1024]{2,1,0:T(8,128)(2,1)} %get-tuple-element.15), channel_id=1, source_target_pairs={{0,4},{2,6},{4,8},{6,10},{8,12},{10,14},{12,0},{14,2},{1,5},{3,7},... | collective-permute-start | bytes 737288 | tf_op jit(solution)/shard_map/ppermute | solution.py:274
  10.2 1.1 %collective-permute-start.2 = (bf16[3,40,1024]{2,1,0:T(8,128)(2,1)}, bf16[3,40,1024]{2,1,0:T(8,128)(2,1)S(1)}, u32[]{:S(2)}, u32[]{:S(2)}) collective-permute-start(bf16[3,40,1024]{2,1,0:T(8,128)(2,1)} %get-tuple-element.17), channel_id=1, source_target_pairs={{0,8},{2,10},{4,12},{6,14},{8,0},{10,2},{12,4},{14,6},{1,9},{3,11}... | collective-permute-start | bytes 737288 | tf_op jit(solution)/shard_map/ppermute | solution.py:274
  11.3 1.4 %collective-permute-start.15 = (bf16[3,40,384]{2,1,0:T(8,128)(2,1)}, bf16[3,40,384]{2,1,0:T(8,128)(2,1)S(1)}, u32[]{:S(2)}, u32[]{:S(2)}) collective-permute-start(bf16[3,40,384]{2,1,0:T(8,128)(2,1)} %get-tuple-element.22), channel_id=1, source_target_pairs={{0,12},{2,14},{4,0},{6,2},{8,4},{10,6},{12,8},{14,10},{1,13},{3,15... | collective-permute-start | bytes 276488 | tf_op jit(solution)/shard_map/ppermute | solution.py:274
  12.7 1.9 %collective-permute-start.16 = (bf16[3,40,384]{2,1,0:T(8,128)(2,1)}, bf16[3,40,384]{2,1,0:T(8,128)(2,1)S(1)}, u32[]{:S(2)}, u32[]{:S(2)}) collective-permute-start(bf16[3,40,384]{2,1,0:T(8,128)(2,1)} %get-tuple-element.23), channel_id=1, source_target_pairs={{0,8},{2,10},{4,12},{6,14},{8,0},{10,2},{12,4},{14,6},{1,9},{3,11}... | collective-permute-start | bytes 276488 | tf_op jit(solution)/shard_map/ppermute | solution.py:274
  14.6 22.8 %collective-permute-done.15.refs_3_ = bf16[3,40,384]{2,1,0:T(8,128)(2,1)S(1)} collective-permute-done((bf16[3,40,384]{2,1,0:T(8,128)(2,1)}, bf16[3,40,384]{2,1,0:T(8,128)(2,1)S(1)}, u32[]{:S(2)}, u32[]{:S(2)}) %collective-permute-start.15) | collective-permute-done | bytes 92192 | tf_op jit(solution)/shard_map/ppermute | solution.py:274
  37.7 3.0 %collective-permute-done.20.refs_8_ = bf16[2,40,384]{2,1,0:T(8,128)(2,1)S(1)} collective-permute-done((bf16[2,40,384]{2,1,0:T(8,128)(2,1)}, bf16[2,40,384]{2,1,0:T(8,128)(2,1)S(1)}, u32[]{:S(2)}, u32[]{:S(2)}) %collective-permute-start.20) | collective-permute-done | bytes 61472 | tf_op jit(solution)/shard_map/ppermute | solution.py:275
  40.9 2.0 %collective-permute-start.24 = (bf16[2,40,384]{2,1,0:T(8,128)(2,1)S(1)}, bf16[2,40,384]{2,1,0:T(8,128)(2,1)S(1)}, u32[]{:S(2)}, u32[]{:S(2)}) collective-permute-start(bf16[2,40,384]{2,1,0:T(8,128)(2,1)S(1)} %collective-permute-done.20.refs_8_), channel_id=1, source_target_pairs={{0,1},{1,0},{2,3},{3,2},{4,5},{5,4},{6,7},{7,6},{8,9},{9,8},{10,11... | collective-permute-start | bytes 184328 | tf_op jit(solution)/shard_map/ppermute | solution.py:278
  43.0 1.3 %collective-permute-start.21 = (bf16[2,40,384]{2,1,0:T(8,128)(2,1)S(1)}, bf16[2,40,384]{2,1,0:T(8,128)(2,1)S(1)}, u32[]{:S(2)}, u32[]{:S(2)}) collective-permute-start(bf16[2,40,384]{2,1,0:T(8,128)(2,1)S(1)} %get-tuple-element.36), channel_id=1, source_target_pairs={{0,2},{2,0},{4,6},{6,4},{8,10},{10,8},{12,14},{14,12},{1,3},{3,1},... | collective-permute-start | bytes 184328 | tf_op jit(solution)/shard_map/ppermute | solution.py:276
  44.7 1.3 %collective-permute-start.23 = (bf16[2,40,384]{2,1,0:T(8,128)(2,1)S(1)}, bf16[2,40,384]{2,1,0:T(8,128)(2,1)S(1)}, u32[]{:S(2)}, u32[]{:S(2)}) collective-permute-start(bf16[2,40,384]{2,1,0:T(8,128)(2,1)S(1)} %get-tuple-element.32), channel_id=1, source_target_pairs={{0,2},{2,0},{4,6},{6,4},{8,10},{10,8},{12,14},{14,12},{1,3},{3,1},... | collective-permute-start | bytes 184328 | tf_op jit(solution)/shard_map/ppermute | solution.py:276
  46.0 0.9 %collective-permute-start.17 = (bf16[2,40,384]{2,1,0:T(8,128)(2,1)S(1)}, bf16[2,40,384]{2,1,0:T(8,128)(2,1)S(1)}, u32[]{:S(2)}, u32[]{:S(2)}) collective-permute-start(bf16[2,40,384]{2,1,0:T(8,128)(2,1)S(1)} %get-tuple-element.37), channel_id=1, source_target_pairs={{0,1},{1,0},{2,3},{3,2},{4,5},{5,4},{6,7},{7,6},{8,9},{9,8},{10,11... | collective-permute-start | bytes 184328 | tf_op jit(solution)/shard_map/ppermute | solution.py:277
  46.9 2.8 %collective-permute-start.10 = (bf16[2,40,1024]{2,1,0:T(8,128)(2,1)S(1)}, bf16[2,40,1024]{2,1,0:T(8,128)(2,1)S(1)}, u32[]{:S(2)}, u32[]{:S(2)}) collective-permute-start(bf16[2,40,1024]{2,1,0:T(8,128)(2,1)S(1)} %collective-permute-done.6.refs_7_), channel_id=1, source_target_pairs={{0,1},{1,0},{2,3},{3,2},{4,5},{5,4},{6,7},{7,6},{8,9},{9,8},{10,11... | collective-permute-start | bytes 491528 | tf_op jit(solution)/shard_map/ppermute | solution.py:278
  49.6 1.4 %collective-permute-start.8 = (bf16[2,40,1024]{2,1,0:T(8,128)(2,1)S(1)}, bf16[2,40,1024]{2,1,0:T(8,128)(2,1)S(1)}, u32[]{:S(2)}, u32[]{:S(2)}) collective-permute-start(bf16[2,40,1024]{2,1,0:T(8,128)(2,1)S(1)} %get-tuple-element.28), channel_id=1, source_target_pairs={{0,2},{2,0},{4,6},{6,4},{8,10},{10,8},{12,14},{14,12},{1,3},{3,1},... | collective-permute-start | bytes 491528 | tf_op jit(solution)/shard_map/ppermute | solution.py:276
  51.2 2.0 %collective-permute-start.3 = (bf16[2,40,1024]{2,1,0:T(8,128)(2,1)S(1)}, bf16[2,40,1024]{2,1,0:T(8,128)(2,1)S(1)}, u32[]{:S(2)}, u32[]{:S(2)}) collective-permute-start(bf16[2,40,1024]{2,1,0:T(8,128)(2,1)S(1)} %get-tuple-element.31), channel_id=1, source_target_pairs={{0,1},{1,0},{2,3},{3,2},{4,5},{5,4},{6,7},{7,6},{8,9},{9,8},{10,11... | collective-permute-start | bytes 491528 | tf_op jit(solution)/shard_map/ppermute | solution.py:277
  53.3 1.1 %collective-permute-done.7.refs_8_ = bf16[2,40,1024]{2,1,0:T(8,128)(2,1)S(1)} collective-permute-done((bf16[2,40,1024]{2,1,0:T(8,128)(2,1)S(1)}, bf16[2,40,1024]{2,1,0:T(8,128)(2,1)S(1)}, u32[]{:S(2)}, u32[]{:S(2)}) %collective-permute-start.7) | collective-permute-done | bytes 163872 | tf_op jit(solution)/shard_map/ppermute | solution.py:276
  54.4 3.3 %collective-permute-start.5 = (bf16[2,40,1024]{2,1,0:T(8,128)(2,1)S(1)}, bf16[2,40,1024]{2,1,0:T(8,128)(2,1)S(1)}, u32[]{:S(2)}, u32[]{:S(2)}) collective-permute-start(bf16[2,40,1024]{2,1,0:T(8,128)(2,1)S(1)} %get-tuple-element.27), channel_id=1, source_target_pairs={{0,1},{1,0},{2,3},{3,2},{4,5},{5,4},{6,7},{7,6},{8,9},{9,8},{10,11... | collective-permute-start | bytes 491528 | tf_op jit(solution)/shard_map/ppermute | solution.py:277
  57.9 3.3 %collective-permute-start.11 = (bf16[2,40,1024]{2,1,0:T(8,128)(2,1)S(1)}, bf16[2,40,1024]{2,1,0:T(8,128)(2,1)S(1)}, u32[]{:S(2)}, u32[]{:S(2)}) collective-permute-start(bf16[2,40,1024]{2,1,0:T(8,128)(2,1)S(1)} %collective-permute-done.7.refs_8_), channel_id=1, source_target_pairs={{0,1},{1,0},{2,3},{3,2},{4,5},{5,4},{6,7},{7,6},{8,9},{9,8},{10,11... | collective-permute-start | bytes 491528 | tf_op jit(solution)/shard_map/ppermute | solution.py:278
  61.4 1.8 %collective-permute-start.12 = (bf16[2,40,1024]{2,1,0:T(8,128)(2,1)S(1)}, bf16[2,40,1024]{2,1,0:T(8,128)(2,1)S(1)}, u32[]{:S(2)}, u32[]{:S(2)}) collective-permute-start(bf16[2,40,1024]{2,1,0:T(8,128)(2,1)S(1)} %collective-permute-done.8.refs_9_), channel_id=1, source_target_pairs={{0,1},{1,0},{2,3},{3,2},{4,5},{5,4},{6,7},{7,6},{8,9},{9,8},{10,11... | collective-permute-start | bytes 491528 | tf_op jit(solution)/shard_map/ppermute | solution.py:278
  67.4 11.5 %shard_map.69 = (f32[1,2048,2048]{2,1,0:T(8,128)}, f32[1]{0:T(128)}) custom-call(s32[3]{0:T(128)} %pad_add_fusion.table_ref, bf16[2,40,2048]{2,1,0:T(8,128)(2,1)} %get-tuple-element.14.refs_0_, bf16[3,40,1024]{2,1,0:T(8,128)(2,1)} %copy-done.3, bf16[3,40,1024]{2,1,0:T(8,128)(2,1)} %copy-done.4, bf16[3,40,1024]{2,1,0:T(8,128)(2,1)} %copy-done.5, ...), custom_call_target="tpu_custom_call" | custom-call | flops 3221225472 | bytes 16777216 | tf_op jit(solution)/shard_map/pallas_call | solution.py:244
  79.7 4.6 %shard_map.71 = f32[1,768,768]{2,1,0:T(8,128)} custom-call(s32[3]{0:T(128)} %pad_add_fusion.table_ref, f32[1]{0:T(128)} %get-tuple-element.19.refs_0_, bf16[2,40,768]{2,1,0:T(8,128)(2,1)} %get-tuple-element.20.refs_1_, bf16[3,40,384]{2,1,0:T(8,128)(2,1)} %copy-done, bf16[3,40,384]{2,1,0:T(8,128)(2,1)} %copy-done.1, bf16[3,40,384]{2,1,0:T(8,128)(2,1)} %copy-done.2, ...), custom_call_target="tpu_custom_call" | custom-call | flops 452984832 | bytes 2359296 | tf_op jit(solution)/shard_map/pallas_call | solution.py:244
  (102 shorter events, 5.3 us)
Async XLA Ops:
  4.4 8.3 %collective-permute-start.14 = (bf16[3,40,384]{2,1,0:T(8,128)(2,1)}, bf16[3,40,384]{2,1,0:T(8,128)(2,1)S(1)}, u32[]{:S(2)}, u32[]{:S(2)}) collective-permute-start(bf16[3,40,384]{2,1,0:T(8,128)(2,1)} %get-tuple-element.21), channel_id=1, source_target_pairs={{0,4},{2,6},{4,8},{6,10},{8,12},{10,14},{12,0},{14,2},{1,5},{3,7},... | collective-permute-start | bytes 276488 | tf_op jit(solution)/shard_map/ppermute | solution.py:274
  8.8 34.2 %collective-permute-start = (bf16[3,40,1024]{2,1,0:T(8,128)(2,1)}, bf16[3,40,1024]{2,1,0:T(8,128)(2,1)S(1)}, u32[]{:S(2)}, u32[]{:S(2)}) collective-permute-start(bf16[3,40,1024]{2,1,0:T(8,128)(2,1)} %get-tuple-element.15), channel_id=1, source_target_pairs={{0,4},{2,6},{4,8},{6,10},{8,12},{10,14},{12,0},{14,2},{1,5},{3,7},... | collective-permute-start | bytes 737288 | tf_op jit(solution)/shard_map/ppermute | solution.py:274
  10.1 34.2 %collective-permute-start.1 = (bf16[3,40,1024]{2,1,0:T(8,128)(2,1)}, bf16[3,40,1024]{2,1,0:T(8,128)(2,1)S(1)}, u32[]{:S(2)}, u32[]{:S(2)}) collective-permute-start(bf16[3,40,1024]{2,1,0:T(8,128)(2,1)} %get-tuple-element.16), channel_id=1, source_target_pairs={{0,12},{2,14},{4,0},{6,2},{8,4},{10,6},{12,8},{14,10},{1,13},{3,15... | collective-permute-start | bytes 737288 | tf_op jit(solution)/shard_map/ppermute | solution.py:274
  10.2 35.7 %collective-permute-start.2 = (bf16[3,40,1024]{2,1,0:T(8,128)(2,1)}, bf16[3,40,1024]{2,1,0:T(8,128)(2,1)S(1)}, u32[]{:S(2)}, u32[]{:S(2)}) collective-permute-start(bf16[3,40,1024]{2,1,0:T(8,128)(2,1)} %get-tuple-element.17), channel_id=1, source_target_pairs={{0,8},{2,10},{4,12},{6,14},{8,0},{10,2},{12,4},{14,6},{1,9},{3,11}... | collective-permute-start | bytes 737288 | tf_op jit(solution)/shard_map/ppermute | solution.py:274
  11.3 26.1 %collective-permute-start.15 = (bf16[3,40,384]{2,1,0:T(8,128)(2,1)}, bf16[3,40,384]{2,1,0:T(8,128)(2,1)S(1)}, u32[]{:S(2)}, u32[]{:S(2)}) collective-permute-start(bf16[3,40,384]{2,1,0:T(8,128)(2,1)} %get-tuple-element.22), channel_id=1, source_target_pairs={{0,12},{2,14},{4,0},{6,2},{8,4},{10,6},{12,8},{14,10},{1,13},{3,15... | collective-permute-start | bytes 276488 | tf_op jit(solution)/shard_map/ppermute | solution.py:274
  12.7 28.2 %collective-permute-start.16 = (bf16[3,40,384]{2,1,0:T(8,128)(2,1)}, bf16[3,40,384]{2,1,0:T(8,128)(2,1)S(1)}, u32[]{:S(2)}, u32[]{:S(2)}) collective-permute-start(bf16[3,40,384]{2,1,0:T(8,128)(2,1)} %get-tuple-element.23), channel_id=1, source_target_pairs={{0,8},{2,10},{4,12},{6,14},{8,0},{10,2},{12,4},{14,6},{1,9},{3,11}... | collective-permute-start | bytes 276488 | tf_op jit(solution)/shard_map/ppermute | solution.py:274
  40.7 6.2 %collective-permute-start.6 = (bf16[2,40,1024]{2,1,0:T(8,128)(2,1)}, bf16[2,40,1024]{2,1,0:T(8,128)(2,1)S(1)}, u32[]{:S(2)}, u32[]{:S(2)}) collective-permute-start(bf16[2,40,1024]{2,1,0:T(8,128)(2,1)} %get-tuple-element.18), channel_id=1, source_target_pairs={{0,2},{2,0},{4,6},{6,4},{8,10},{10,8},{12,14},{14,12},{1,3},{3,1},... | collective-permute-start | bytes 491528 | tf_op jit(solution)/shard_map/ppermute | solution.py:275
  43.0 6.6 %collective-permute-start.21 = (bf16[2,40,384]{2,1,0:T(8,128)(2,1)S(1)}, bf16[2,40,384]{2,1,0:T(8,128)(2,1)S(1)}, u32[]{:S(2)}, u32[]{:S(2)}) collective-permute-start(bf16[2,40,384]{2,1,0:T(8,128)(2,1)S(1)} %get-tuple-element.36), channel_id=1, source_target_pairs={{0,2},{2,0},{4,6},{6,4},{8,10},{10,8},{12,14},{14,12},{1,3},{3,1},... | collective-permute-start | bytes 184328 | tf_op jit(solution)/shard_map/ppermute | solution.py:276
  44.3 5.3 %collective-permute-start.22 = (bf16[2,40,384]{2,1,0:T(8,128)(2,1)S(1)}, bf16[2,40,384]{2,1,0:T(8,128)(2,1)S(1)}, u32[]{:S(2)}, u32[]{:S(2)}) collective-permute-start(bf16[2,40,384]{2,1,0:T(8,128)(2,1)S(1)} %get-tuple-element.34), channel_id=1, source_target_pairs={{0,2},{2,0},{4,6},{6,4},{8,10},{10,8},{12,14},{14,12},{1,3},{3,1},... | collective-permute-start | bytes 184328 | tf_op jit(solution)/shard_map/ppermute | solution.py:276
  44.7 6.4 %collective-permute-start.23 = (bf16[2,40,384]{2,1,0:T(8,128)(2,1)S(1)}, bf16[2,40,384]{2,1,0:T(8,128)(2,1)S(1)}, u32[]{:S(2)}, u32[]{:S(2)}) collective-permute-start(bf16[2,40,384]{2,1,0:T(8,128)(2,1)S(1)} %get-tuple-element.32), channel_id=1, source_target_pairs={{0,2},{2,0},{4,6},{6,4},{8,10},{10,8},{12,14},{14,12},{1,3},{3,1},... | collective-permute-start | bytes 184328 | tf_op jit(solution)/shard_map/ppermute | solution.py:276
  46.0 5.2 %collective-permute-start.17 = (bf16[2,40,384]{2,1,0:T(8,128)(2,1)S(1)}, bf16[2,40,384]{2,1,0:T(8,128)(2,1)S(1)}, u32[]{:S(2)}, u32[]{:S(2)}) collective-permute-start(bf16[2,40,384]{2,1,0:T(8,128)(2,1)S(1)} %get-tuple-element.37), channel_id=1, source_target_pairs={{0,1},{1,0},{2,3},{3,2},{4,5},{5,4},{6,7},{7,6},{8,9},{9,8},{10,11... | collective-permute-start | bytes 184328 | tf_op jit(solution)/shard_map/ppermute | solution.py:277
  46.9 6.4 %collective-permute-start.10 = (bf16[2,40,1024]{2,1,0:T(8,128)(2,1)S(1)}, bf16[2,40,1024]{2,1,0:T(8,128)(2,1)S(1)}, u32[]{:S(2)}, u32[]{:S(2)}) collective-permute-start(bf16[2,40,1024]{2,1,0:T(8,128)(2,1)S(1)} %collective-permute-done.6.refs_7_), channel_id=1, source_target_pairs={{0,1},{1,0},{2,3},{3,2},{4,5},{5,4},{6,7},{7,6},{8,9},{9,8},{10,11... | collective-permute-start | bytes 491528 | tf_op jit(solution)/shard_map/ppermute | solution.py:278
  49.6 8.3 %collective-permute-start.8 = (bf16[2,40,1024]{2,1,0:T(8,128)(2,1)S(1)}, bf16[2,40,1024]{2,1,0:T(8,128)(2,1)S(1)}, u32[]{:S(2)}, u32[]{:S(2)}) collective-permute-start(bf16[2,40,1024]{2,1,0:T(8,128)(2,1)S(1)} %get-tuple-element.28), channel_id=1, source_target_pairs={{0,2},{2,0},{4,6},{6,4},{8,10},{10,8},{12,14},{14,12},{1,3},{3,1},... | collective-permute-start | bytes 491528 | tf_op jit(solution)/shard_map/ppermute | solution.py:276
  51.1 10.3 %collective-permute-start.9 = (bf16[2,40,1024]{2,1,0:T(8,128)(2,1)S(1)}, bf16[2,40,1024]{2,1,0:T(8,128)(2,1)S(1)}, u32[]{:S(2)}, u32[]{:S(2)}) collective-permute-start(bf16[2,40,1024]{2,1,0:T(8,128)(2,1)S(1)} %get-tuple-element.26), channel_id=1, source_target_pairs={{0,2},{2,0},{4,6},{6,4},{8,10},{10,8},{12,14},{14,12},{1,3},{3,1},... | collective-permute-start | bytes 491528 | tf_op jit(solution)/shard_map/ppermute | solution.py:276
  51.2 12.1 %collective-permute-start.3 = (bf16[2,40,1024]{2,1,0:T(8,128)(2,1)S(1)}, bf16[2,40,1024]{2,1,0:T(8,128)(2,1)S(1)}, u32[]{:S(2)}, u32[]{:S(2)}) collective-permute-start(bf16[2,40,1024]{2,1,0:T(8,128)(2,1)S(1)} %get-tuple-element.31), channel_id=1, source_target_pairs={{0,1},{1,0},{2,3},{3,2},{4,5},{5,4},{6,7},{7,6},{8,9},{9,8},{10,11... | collective-permute-start | bytes 491528 | tf_op jit(solution)/shard_map/ppermute | solution.py:277
  53.2 12.6 %collective-permute-start.4 = (bf16[2,40,1024]{2,1,0:T(8,128)(2,1)S(1)}, bf16[2,40,1024]{2,1,0:T(8,128)(2,1)S(1)}, u32[]{:S(2)}, u32[]{:S(2)}) collective-permute-start(bf16[2,40,1024]{2,1,0:T(8,128)(2,1)S(1)} %get-tuple-element.29), channel_id=1, source_target_pairs={{0,1},{1,0},{2,3},{3,2},{4,5},{5,4},{6,7},{7,6},{8,9},{9,8},{10,11... | collective-permute-start | bytes 491528 | tf_op jit(solution)/shard_map/ppermute | solution.py:277
  54.4 11.8 %collective-permute-start.5 = (bf16[2,40,1024]{2,1,0:T(8,128)(2,1)S(1)}, bf16[2,40,1024]{2,1,0:T(8,128)(2,1)S(1)}, u32[]{:S(2)}, u32[]{:S(2)}) collective-permute-start(bf16[2,40,1024]{2,1,0:T(8,128)(2,1)S(1)} %get-tuple-element.27), channel_id=1, source_target_pairs={{0,1},{1,0},{2,3},{3,2},{4,5},{5,4},{6,7},{7,6},{8,9},{9,8},{10,11... | collective-permute-start | bytes 491528 | tf_op jit(solution)/shard_map/ppermute | solution.py:277
  57.9 8.4 %collective-permute-start.11 = (bf16[2,40,1024]{2,1,0:T(8,128)(2,1)S(1)}, bf16[2,40,1024]{2,1,0:T(8,128)(2,1)S(1)}, u32[]{:S(2)}, u32[]{:S(2)}) collective-permute-start(bf16[2,40,1024]{2,1,0:T(8,128)(2,1)S(1)} %collective-permute-done.7.refs_8_), channel_id=1, source_target_pairs={{0,1},{1,0},{2,3},{3,2},{4,5},{5,4},{6,7},{7,6},{8,9},{9,8},{10,11... | collective-permute-start | bytes 491528 | tf_op jit(solution)/shard_map/ppermute | solution.py:278
  61.4 5.3 %collective-permute-start.12 = (bf16[2,40,1024]{2,1,0:T(8,128)(2,1)S(1)}, bf16[2,40,1024]{2,1,0:T(8,128)(2,1)S(1)}, u32[]{:S(2)}, u32[]{:S(2)}) collective-permute-start(bf16[2,40,1024]{2,1,0:T(8,128)(2,1)S(1)} %collective-permute-done.8.refs_9_), channel_id=1, source_target_pairs={{0,1},{1,0},{2,3},{3,2},{4,5},{5,4},{6,7},{7,6},{8,9},{9,8},{10,11... | collective-permute-start | bytes 491528 | tf_op jit(solution)/shard_map/ppermute | solution.py:278
  65.8 13.2 %collective-permute-start.18 = (bf16[2,40,384]{2,1,0:T(8,128)(2,1)S(1)}, bf16[2,40,384]{2,1,0:T(8,128)(2,1)S(1)}, u32[]{:S(2)}, u32[]{:S(2)}) collective-permute-start(bf16[2,40,384]{2,1,0:T(8,128)(2,1)S(1)} %get-tuple-element.35), channel_id=1, source_target_pairs={{0,1},{1,0},{2,3},{3,2},{4,5},{5,4},{6,7},{7,6},{8,9},{9,8},{10,11... | collective-permute-start | bytes 184328 | tf_op jit(solution)/shard_map/ppermute | solution.py:277
  66.2 12.8 %collective-permute-start.19 = (bf16[2,40,384]{2,1,0:T(8,128)(2,1)S(1)}, bf16[2,40,384]{2,1,0:T(8,128)(2,1)S(1)}, u32[]{:S(2)}, u32[]{:S(2)}) collective-permute-start(bf16[2,40,384]{2,1,0:T(8,128)(2,1)S(1)} %get-tuple-element.33), channel_id=1, source_target_pairs={{0,1},{1,0},{2,3},{3,2},{4,5},{5,4},{6,7},{7,6},{8,9},{9,8},{10,11... | collective-permute-start | bytes 184328 | tf_op jit(solution)/shard_map/ppermute | solution.py:277
  66.3 12.7 %collective-permute-start.25 = (bf16[2,40,384]{2,1,0:T(8,128)(2,1)S(1)}, bf16[2,40,384]{2,1,0:T(8,128)(2,1)S(1)}, u32[]{:S(2)}, u32[]{:S(2)}) collective-permute-start(bf16[2,40,384]{2,1,0:T(8,128)(2,1)S(1)} %collective-permute-done.21.refs_9_), channel_id=1, source_target_pairs={{0,1},{1,0},{2,3},{3,2},{4,5},{5,4},{6,7},{7,6},{8,9},{9,8},{10,11... | collective-permute-start | bytes 184328 | tf_op jit(solution)/shard_map/ppermute | solution.py:278
  66.8 12.3 %collective-permute-start.26 = (bf16[2,40,384]{2,1,0:T(8,128)(2,1)S(1)}, bf16[2,40,384]{2,1,0:T(8,128)(2,1)S(1)}, u32[]{:S(2)}, u32[]{:S(2)}) collective-permute-start(bf16[2,40,384]{2,1,0:T(8,128)(2,1)S(1)} %collective-permute-done.22.refs_10_), channel_id=1, source_target_pairs={{0,1},{1,0},{2,3},{3,2},{4,5},{5,4},{6,7},{7,6},{8,9},{9,8},{10,11... | collective-permute-start | bytes 184328 | tf_op jit(solution)/shard_map/ppermute | solution.py:278
  66.8 12.2 %collective-permute-start.27 = (bf16[2,40,384]{2,1,0:T(8,128)(2,1)S(1)}, bf16[2,40,384]{2,1,0:T(8,128)(2,1)S(1)}, u32[]{:S(2)}, u32[]{:S(2)}) collective-permute-start(bf16[2,40,384]{2,1,0:T(8,128)(2,1)S(1)} %collective-permute-done.23.refs_11_), channel_id=1, source_target_pairs={{0,1},{1,0},{2,3},{3,2},{4,5},{5,4},{6,7},{7,6},{8,9},{9,8},{10,11... | collective-permute-start | bytes 184328 | tf_op jit(solution)/shard_map/ppermute | solution.py:278
  (32 other events, 550.0 us)

commit v2 on v0

--- a/solution.py
+++ b/solution.py
@@ -1,10 +1,15 @@
+import functools
 import math
 
 import jax
 import jax.numpy as jnp
 import numpy as np
 from jax import lax
+from jax.experimental import pallas as pl
+from jax.experimental.pallas import tpu as pltpu
 from jax.sharding import PartitionSpec as P
+
+SLOT_ROWS = 48
 
 
 def block_table(side):
@@ -46,7 +51,7 @@
     )
 
 
-def shards(inputs, hidden_grads, routes):
+def shards_any(inputs, hidden_grads, routes):
     chosen = jnp.any(routes == 0, axis=1).astype(jnp.int32)
     core_index = lax.axis_index("hid")
     chip_index = lax.axis_index("tok")
@@ -75,10 +80,276 @@
     return ((input_sum / total)[None], (grad_sum / total)[None])
 
 
+N_X = 2
+N_Z = 4
+
+
+def slot_table():
+    first_ids, second_ids = block_table(4)
+    slots = np.zeros((N_Z, N_X, 3), np.int32)
+    for z in range(N_Z):
+        zero = {int(first_ids[z * N_X]), int(second_ids[z * N_X])}
+        one = {int(first_ids[z * N_X + 1]), int(second_ids[z * N_X + 1])}
+        common = max(zero & one)
+        (a,) = zero - {common}
+        (b,) = one - {common}
+        slots[z, 0] = (a, common, b)
+        slots[z, 1] = (b, common, a)
+    return slots
+
+
+def lookup(values, index):
+    found = jnp.int32(int(values[0]))
+    for i in range(1, len(values)):
+        found = jnp.where(index == i, jnp.int32(int(values[i])), found)
+    return found
+
+
+def place():
+    chip = lax.axis_index("tok").astype(jnp.int32)
+    return lax.div(chip, N_X), lax.rem(chip, N_X), lax.axis_index("hid").astype(jnp.int32)
+
+
+def pack_kernel(mark, routes_ref, values_ref, p1_ref, p2_ref, x0_ref, own_ref, held, packed, sems):
+    plane, column, core = place()
+    capacity, half = p2_ref.shape[1:]
+    width = 2 * half
+    copies = [
+        pltpu.make_async_copy(
+            values_ref.at[:, block * width : (block + 1) * width], held.at[block], sems.at[block]
+        )
+        for block in range(4)
+    ]
+    for copy in copies:
+        copy.start()
+    chosen = (routes_ref[0:1, :] == 0) | (routes_ref[1:2, :] == 0)
+    tokens = chosen.shape[1]
+    flags = jnp.where(chosen, 1.0, 0.0)
+    before = (
+        lax.broadcasted_iota(jnp.int32, (tokens, tokens), 0)
+        <= lax.broadcasted_iota(jnp.int32, (tokens, tokens), 1)
+    )
+    rank = jnp.dot(
+        flags.astype(jnp.bfloat16),
+        jnp.where(before, 1.0, 0.0).astype(jnp.bfloat16),
+        preferred_element_type=jnp.float32,
+    )
+    slot = lax.broadcasted_iota(jnp.int32, (capacity, tokens), 0).astype(jnp.float32) + 1.0
+    picker = jnp.where((rank == slot) & chosen, 1.0, 0.0)
+    empty = (jnp.sum(picker, axis=1, keepdims=True) == 0.0) & (
+        lax.broadcasted_iota(jnp.int32, (capacity, 128), 1) == 0
+    )
+    picker = picker.astype(jnp.bfloat16)
+    for block in range(4):
+        copies[block].wait()
+        got = jnp.dot(picker, held[block], preferred_element_type=jnp.float32)
+        if mark:
+            head = jnp.where(empty, jnp.inf, got[:, :128])
+            packed[block, :, :128] = head.astype(jnp.bfloat16)
+            packed[block, :, 128:] = got[:, 128:].astype(jnp.bfloat16)
+        else:
+            packed[block] = got.astype(jnp.bfloat16)
+
+    table = slot_table().reshape(-1, 3)
+
+    def block_at(to_plane, row):
+        return lookup(table[:, row], to_plane * N_X + column)
+
+    to_plane = lax.rem(plane + jnp.where(core == 0, 1, 3), N_Z)
+    for row in range(3):
+        p1_ref[row] = packed[block_at(to_plane, row)]
+    start = pl.multiple_of(core * half, 128)
+    for row in range(2):
+        x0_ref[row] = packed[block_at(plane, row + 1), :, pl.ds(start, half)]
+    to_plane = lax.rem(plane + 2, N_Z)
+    for row in range(3):
+        p2_ref[row] = packed[block_at(to_plane, row), :, pl.ds(start, half)]
+    for row in range(2):
+        own_ref[row] = packed[block_at(plane, row)]
+
+
+def pack(mark, routes_t, values, capacity):
+    tokens = values.shape[0]
+    width = values.shape[1] // 4
+    half = width // 2
+    shapes = [(3, capacity, width), (3, capacity, half), (2, capacity, half), (2, capacity, width)]
+    vmem = pl.BlockSpec(memory_space=pltpu.VMEM)
+    return pl.pallas_call(
+        functools.partial(pack_kernel, mark),
+        out_shape=[jax.ShapeDtypeStruct(s, jnp.bfloat16) for s in shapes],
+        in_specs=[vmem, pl.BlockSpec(memory_space=pl.ANY)],
+        out_specs=[vmem] * len(shapes),
+        scratch_shapes=[
+            pltpu.VMEM((4, tokens, width), jnp.bfloat16),
+            pltpu.VMEM((4, capacity, width), jnp.bfloat16),
+            pltpu.SemaphoreType.DMA((4,)),
+        ],
+        compiler_params=pltpu.CompilerParams(vmem_limit_bytes=12 * 2**20),
+        cost_estimate=pl.CostEstimate(
+            flops=2 * capacity * values.size, bytes_accessed=2 * values.size, transcendentals=0
+        ),
+    )(routes_t, values)
+
+
+def tile_kernel(marked, *refs):
+    refs = list(refs)
+    scale_in = None if marked else refs.pop(0)
+    own, p1, hp1, p2, hp2, x0, hx0, x1, hx1, x2, hx2 = (refs.pop(0) for _ in range(11))
+    out_ref = refs.pop(0)
+    scale_out = refs.pop(0) if marked else None
+    data, stage, sems = refs
+    plane, column, core = place()
+    chip = plane * N_X + column
+    capacity, half = p2.shape[1:]
+    width = 2 * half
+    rows_out = width // sems.shape[0]
+    slots = data.shape[1] // SLOT_ROWS
+    first_ids, _ = block_table(4)
+    first_is_common = lookup(
+        (slot_table().reshape(-1, 3)[:, 0] != first_ids).astype(np.int32), chip
+    )
+    left = jnp.where(core == 0, first_is_common, 1 - first_is_common)
+    right = jnp.where(lax.rem(chip, 4) == 3, left, 1 - left)
+
+    mine = pl.multiple_of(core * half, 128)
+    other = pl.multiple_of((1 - core) * half, 128)
+    for block in range(2):
+        for slot in range(slots):
+            data[block, slot * SLOT_ROWS + 32 : (slot + 1) * SLOT_ROWS, :] = jnp.zeros(
+                (SLOT_ROWS - 32, width), jnp.bfloat16
+            )
+        whole = (own.at[block], p1.at[block], hp1.at[block], x1.at[1 - block], hx1.at[1 - block])
+        for slot, ref in enumerate(whole):
+            data[block, slot * SLOT_ROWS : slot * SLOT_ROWS + capacity, :] = ref[...]
+        halves = (
+            (p2.at[block], hp2.at[block]),
+            (x0.at[1 - block], hx0.at[1 - block]),
+            (x2.at[1 - block], hx2.at[1 - block]),
+        )
+        for slot, (ref, far_ref) in enumerate(halves, len(whole)):
+            rows = pl.ds(slot * SLOT_ROWS, capacity)
+            data[block, rows, pl.ds(mine, half)] = ref[...]
+            data[block, rows, pl.ds(other, half)] = far_ref[...]
+    if marked:
+        for block in range(2):
+            head = data[block, :, 0:128].astype(jnp.float32)
+            gone = head == jnp.inf
+            if block == 0:
+                scale = 1.0 / (capacity * slots - jnp.sum(jnp.where(gone, 1.0, 0.0)))
+                scale_out[0] = scale
+            data[block, :, 0:128] = jnp.where(gone, 0.0, head).astype(jnp.bfloat16)
+    else:
+        scale = scale_in[0]
+
+    copies = []
+    for i in range(sems.shape[0]):
+        rows = pl.ds(i * rows_out, rows_out)
+        stage[rows, :] = scale * lax.dot_general(
+            data[left, :, rows],
+            data[right],
+            (((0,), (0,)), ((), ())),
+            preferred_element_type=jnp.float32,
+        )
+        copies.append(pltpu.make_async_copy(stage.at[rows], out_ref.at[0, rows], sems.at[i]))
+        copies[-1].start()
+    for copy in copies:
+        copy.wait()
+
+
+def tile(scale, parts, steps, limit):
+    marked = scale is None
+    width = parts[0].shape[2]
+    smem = pl.BlockSpec(memory_space=pltpu.SMEM)
+    vmem = pl.BlockSpec(memory_space=pltpu.VMEM)
+    out_shape = [jax.ShapeDtypeStruct((1, width, width), jnp.float32)]
+    out_specs = [pl.BlockSpec(memory_space=pl.ANY)]
+    if marked:
+        out_shape.append(jax.ShapeDtypeStruct((1,), jnp.float32))
+        out_specs.append(smem)
+    slots = 8
+    return pl.pallas_call(
+        functools.partial(tile_kernel, marked),
+        out_shape=out_shape,
+        in_specs=([] if marked else [smem]) + [vmem] * len(parts),
+        out_specs=out_specs,
+        scratch_shapes=[
+            pltpu.VMEM((2, slots * SLOT_ROWS, width), jnp.bfloat16),
+            pltpu.VMEM((width, width), jnp.float32),
+            pltpu.SemaphoreType.DMA((steps,)),
+        ],
+        compiler_params=pltpu.CompilerParams(vmem_limit_bytes=limit),
+        cost_estimate=pl.CostEstimate(
+            flops=2 * slots * SLOT_ROWS * width * width,
+            bytes_accessed=4 * width * width,
+            transcendentals=0,
+        ),
+    )(*([] if marked else [scale]), *parts)
+
+
+def moves(step):
+    pairs = []
+    for z in range(N_Z):
+        for x in range(N_X):
+            for core in range(2):
+                to_z, to_x, to_core = step(z, x, core)
+                source = (z * N_X + x) * 2 + core
+                pairs.append((source, (to_z % N_Z * N_X + to_x) * 2 + to_core))
+    return pairs
+
+
+ALONG_Z = moves(lambda z, x, core: (z + (1, 3)[core], x, core))
+ACROSS_Z = moves(lambda z, x, core: (z + 2, x, core))
+ALONG_X = moves(lambda z, x, core: (z, 1 - x, core))
+CORES = moves(lambda z, x, core: (z, x, 1 - core))
+
+
+def send(array, pairs, after=()):
+    if after:
+        array = lax.optimization_barrier((array, *after))[0]
+    return lax.ppermute(array, ("tok", "hid"), pairs)
+
+
+def shards_eight(inputs, hidden_grads, routes):
+    capacity = routes.shape[0] * 5 // 16
+    routes_t = routes.T
+    p1, p2, x0, own = pack(True, routes_t, hidden_grads, capacity)
+    p1 = send(p1, ALONG_Z)
+    x0 = send(x0, ALONG_X)
+    p1_i, p2_i, x0_i, own_i = pack(False, routes_t, inputs, capacity)
+    x0_i = send(x0_i, ALONG_X)
+    p2 = send(p2, ACROSS_Z, [x0, x0_i])
+    hx0 = send(x0, CORES)
+    hx0_i = send(x0_i, CORES)
+    x1 = send(p1[1:], ALONG_X)
+    hp1 = send(p1[:2], CORES)
+    p1_i = send(p1_i, ALONG_Z, [p1])
+    hx1 = send(x1, CORES)
+    x2 = send(p2[1:], ALONG_X)
+    hp2 = send(p2[:2], CORES)
+    p2_i = send(p2_i, ACROSS_Z, [p2])
+    hx2 = send(x2, CORES)
+    x1_i = send(p1_i[1:], ALONG_X, [x2])
+    hp1_i = send(p1_i[:2], CORES)
+    hx1_i = send(x1_i, CORES)
+    x2_i = send(p2_i[1:], ALONG_X)
+    hp2_i = send(p2_i[:2], CORES)
+    hx2_i = send(x2_i, CORES)
+    grad_tile, scale = tile(
+        None, (own, p1, hp1, p2, hp2, x0, hx0, x1, hx1, x2, hx2), 8, 28 * 2**20
+    )
+    (input_tile,) = tile(
+        scale,
+        (own_i, p1_i, hp1_i, p2_i, hp2_i, x0_i, hx0_i, x1_i, hx1_i, x2_i, hx2_i),
+        3,
+        12 * 2**20,
+    )
+    return input_tile, grad_tile
+
+
 def solution(mesh):
     placed = (P(("parts", "tok"), None), P(("parts", "tok"), None), P(("parts", "tok"), None))
     return jax.shard_map(
-        shards,
+        shards_eight if mesh.shape["tok"] == N_X * N_Z else shards_any,
         mesh=mesh,
         in_specs=placed,
         out_specs=(P(("parts", "tok", "hid"), None, None), P(("parts", "tok", "hid"), None, None)),

time: 126 us -> 64.5 us (0.51)
  the two profiles are of different devices: /device:TPU:8 before, /device:TPU:0 now
where the time goes in v2:
time: 64.5 us; the launch traced here: 64.3 us
  waiting for transfers between devices  33.5 us (52%)
  starting transfers between devices  14.9 us (23%)
  Pallas kernels  12.8 us (20%)
  local copies, waits for them, and re-layouts  2.36 us (4%)
  between operations  0.76 us (1%)
    ppermute x20, waiting for transfers between devices, send(): return lax.ppermute(array, ('tok', 'hid'), pairs)  33.5 us
    ppermute x20, starting transfers between devices, send(): return lax.ppermute(array, ('tok', 'hid'), pairs)  14.9 us
    pallas_call x2, Pallas kernels, tile(): pl.pallas_call(functools.partial(tile_kernel, marked), out_shape=out_shap...  10.4 us
    pallas_call x2, Pallas kernels, pack(): pl.pallas_call(functools.partial(pack_kernel, mark), out_shape=[jax.Shape...  2.35 us
    unnamed x6, local copies, waits for them, and re-layouts  2.27 us
  transfers between devices with their start and end apart: 20, of which 6 were waited for; matrix products, arithmetic and copies ran while one was open for 0% of the time, Pallas kernels for 14%

profile of v2, /device:TPU:0, one launch (start us, length us, event | category | flops | bytes accessed | tf_op | source)
XLA Modules:
  0.0 64.3 jit_solution(2360722045139314494)
XLA Ops:
  0.6 1.6 %copy-done = bf16[128,8192]{1,0:T(8,128)(2,1)S(1)} copy-done((bf16[128,8192]{1,0:T(8,128)(2,1)S(1)}, bf16[128,8192]{1,0:T(8,128)(2,1)}, u32[]{:S(2)}) %copy-start) | copy-done | bytes 2097176
  2.2 0.7 %copy-done.2 = s32[128,2]{0,1:T(2,128)S(1)} copy-done((s32[128,2]{0,1:T(2,128)S(1)}, s32[128,2]{0,1:T(2,128)}, u32[]{:S(2)}) %copy-start.2) | copy-done | bytes 1048
  2.9 1.4 %shard_map.50 = (bf16[3,40,2048]{2,1,0:T(8,128)(2,1)S(1)}, bf16[3,40,1024]{2,1,0:T(8,128)(2,1)S(1)}, bf16[2,40,1024]{2,1,0:T(8,128)(2,1)S(1)}, bf16[2,40,2048]{2,1,0:T(8,128)(2,1)S(1)}) custom-call(s32[2,128]{1,0:T(2,128)S(1)} %bitcast.1, bf16[128,8192]{1,0:T(8,128)(2,1)S(1)} %copy-done), custom_call_target="tpu_custom_call" | custom-call | flops 83886080 | bytes 2097152 | tf_op jit(solution)/shard_map/pallas_call | solution.py:177
  4.3 3.1 %collective-permute-start = (bf16[3,40,2048]{2,1,0:T(8,128)(2,1)S(1)}, bf16[3,40,2048]{2,1,0:T(8,128)(2,1)S(1)}, u32[]{:S(2)}, u32[]{:S(2)}) collective-permute-start(bf16[3,40,2048]{2,1,0:T(8,128)(2,1)S(1)} %get-tuple-element.17), channel_id=1, source_target_pairs={{0,4},{1,13},{2,6},{3,15},{4,8},{5,1},{6,10},{7,3},{8,12},{9,5},{1... | collective-permute-start | bytes 1474568 | tf_op jit(solution)/shard_map/ppermute | solution.py:309
  7.3 1.5 %collective-permute-start.2 = (bf16[2,40,1024]{2,1,0:T(8,128)(2,1)S(1)}, bf16[2,40,1024]{2,1,0:T(8,128)(2,1)S(1)}, u32[]{:S(2)}, u32[]{:S(2)}) collective-permute-start(bf16[2,40,1024]{2,1,0:T(8,128)(2,1)S(1)} %get-tuple-element.19), channel_id=1, source_target_pairs={{0,2},{1,3},{2,0},{3,1},{4,6},{5,7},{6,4},{7,5},{8,10},{9,11},{10,... | collective-permute-start | bytes 491528 | tf_op jit(solution)/shard_map/ppermute | solution.py:309
  8.8 1.0 %shard_map.51 = (bf16[3,40,768]{2,1,0:T(8,128)(2,1)S(1)}, bf16[3,40,384]{2,1,0:T(8,128)(2,1)S(1)}, bf16[2,40,384]{2,1,0:T(8,128)(2,1)S(1)}, bf16[2,40,768]{2,1,0:T(8,128)(2,1)S(1)}) custom-call(s32[2,128]{1,0:T(2,128)S(1)} %bitcast.2, bf16[128,3072]{1,0:T(8,128)(2,1)S(1)} %copy-done.1), custom_call_target="tpu_custom_call" | custom-call | flops 31457280 | bytes 786432 | tf_op jit(solution)/shard_map/pallas_call | solution.py:177
  9.8 0.6 collective-permute-start.3
  10.4 4.7 %collective-permute-done.3.refs_6_ = bf16[2,40,384]{2,1,0:T(8,128)(2,1)S(1)} collective-permute-done((bf16[2,40,384]{2,1,0:T(8,128)(2,1)S(1)}, bf16[2,40,384]{2,1,0:T(8,128)(2,1)S(1)}, u32[]{:S(2)}, u32[]{:S(2)}) %collective-permute-start.3) | collective-permute-done | bytes 61472 | tf_op jit(solution)/shard_map/ppermute | solution.py:309
  15.2 1.5 %collective-permute-start.4 = (bf16[3,40,1024]{2,1,0:T(8,128)(2,1)S(1)}, bf16[3,40,1024]{2,1,0:T(8,128)(2,1)S(1)}, u32[]{:S(2)}, u32[]{:S(2)}) collective-permute-start(bf16[3,40,1024]{2,1,0:T(8,128)(2,1)S(1)} %get-tuple-element.21), channel_id=1, source_target_pairs={{0,8},{1,9},{2,10},{3,11},{4,12},{5,13},{6,14},{7,15},{8,0},{9,1},... | collective-permute-start | bytes 737288 | tf_op jit(solution)/shard_map/ppermute | solution.py:309
  16.7 14.2 %collective-permute-done.4.refs_3_ = bf16[3,40,1024]{2,1,0:T(8,128)(2,1)S(1)} collective-permute-done((bf16[3,40,1024]{2,1,0:T(8,128)(2,1)S(1)}, bf16[3,40,1024]{2,1,0:T(8,128)(2,1)S(1)}, u32[]{:S(2)}, u32[]{:S(2)}) %collective-permute-start.4) | collective-permute-done | bytes 245792 | tf_op jit(solution)/shard_map/ppermute | solution.py:309
  31.0 1.7 %collective-permute-start.7 = (bf16[2,40,2048]{2,1,0:T(8,128)(2,1)S(1)}, bf16[2,40,2048]{2,1,0:T(8,128)(2,1)S(1)}, u32[]{:S(2)}, u32[]{:S(2)}) collective-permute-start(bf16[2,40,2048]{2,1,0:T(8,128)(2,1)S(1)} %get-tuple-element.30), channel_id=1, source_target_pairs={{0,2},{1,3},{2,0},{3,1},{4,6},{5,7},{6,4},{7,5},{8,10},{9,11},{10,... | collective-permute-start | bytes 983048 | tf_op jit(solution)/shard_map/ppermute | solution.py:309
  32.7 0.5 collective-permute-start.9
  33.2 4.2 %collective-permute-done.13.refs_4_ = bf16[3,40,384]{2,1,0:T(8,128)(2,1)S(1)} collective-permute-done((bf16[3,40,384]{2,1,0:T(8,128)(2,1)S(1)}, bf16[3,40,384]{2,1,0:T(8,128)(2,1)S(1)}, u32[]{:S(2)}, u32[]{:S(2)}) %collective-permute-start.13) | collective-permute-done | bytes 92192 | tf_op jit(solution)/shard_map/ppermute | solution.py:309
  37.4 1.2 %collective-permute-start.1 = (bf16[2,40,2048]{2,1,0:T(8,128)(2,1)S(1)}, bf16[2,40,2048]{2,1,0:T(8,128)(2,1)S(1)}, u32[]{:S(2)}, u32[]{:S(2)}) collective-permute-start(bf16[2,40,2048]{2,1,0:T(8,128)(2,1)S(1)} %get-tuple-element.31), channel_id=1, source_target_pairs={{0,1},{1,0},{2,3},{3,2},{4,5},{5,4},{6,7},{7,6},{8,9},{9,8},{10,11... | collective-permute-start | bytes 983048 | tf_op jit(solution)/shard_map/ppermute | solution.py:309
  38.5 5.6 %collective-permute-done.9.refs_9_ = bf16[2,40,1024]{2,1,0:T(8,128)(2,1)S(1)} collective-permute-done((bf16[2,40,1024]{2,1,0:T(8,128)(2,1)S(1)}, bf16[2,40,1024]{2,1,0:T(8,128)(2,1)S(1)}, u32[]{:S(2)}, u32[]{:S(2)}) %collective-permute-start.9) | collective-permute-done | bytes 163872 | tf_op jit(solution)/shard_map/ppermute | solution.py:309
  44.1 1.6 %collective-permute-start.18 = (bf16[2,40,384]{2,1,0:T(8,128)(2,1)S(1)}, bf16[2,40,384]{2,1,0:T(8,128)(2,1)S(1)}, u32[]{:S(2)}, u32[]{:S(2)}) collective-permute-start(bf16[2,40,384]{2,1,0:T(8,128)(2,1)S(1)} %get-tuple-element.36), channel_id=1, source_target_pairs={{0,2},{1,3},{2,0},{3,1},{4,6},{5,7},{6,4},{7,5},{8,10},{9,11},{10,... | collective-permute-start | bytes 184328 | tf_op jit(solution)/shard_map/ppermute | solution.py:309
  45.8 0.5 collective-permute-start.8
  46.3 2.1 %collective-permute-done.18.refs_10_ = bf16[2,40,384]{2,1,0:T(8,128)(2,1)S(1)} collective-permute-done((bf16[2,40,384]{2,1,0:T(8,128)(2,1)S(1)}, bf16[2,40,384]{2,1,0:T(8,128)(2,1)S(1)}, u32[]{:S(2)}, u32[]{:S(2)}) %collective-permute-start.18) | collective-permute-done | bytes 61472 | tf_op jit(solution)/shard_map/ppermute | solution.py:309
  48.3 1.6 %collective-permute-start.16 = (bf16[2,40,768]{2,1,0:T(8,128)(2,1)S(1)}, bf16[2,40,768]{2,1,0:T(8,128)(2,1)S(1)}, u32[]{:S(2)}, u32[]{:S(2)}) collective-permute-start(bf16[2,40,768]{2,1,0:T(8,128)(2,1)S(1)} %get-tuple-element.28), channel_id=1, source_target_pairs={{0,2},{1,3},{2,0},{3,1},{4,6},{5,7},{6,4},{7,5},{8,10},{9,11},{10,... | collective-permute-start | bytes 368648 | tf_op jit(solution)/shard_map/ppermute | solution.py:309
  50.0 0.5 collective-permute-start.14
  50.5 2.7 %collective-permute-done.16.refs_8_ = bf16[2,40,768]{2,1,0:T(8,128)(2,1)S(1)} collective-permute-done((bf16[2,40,768]{2,1,0:T(8,128)(2,1)S(1)}, bf16[2,40,768]{2,1,0:T(8,128)(2,1)S(1)}, u32[]{:S(2)}, u32[]{:S(2)}) %collective-permute-start.16) | collective-permute-done | bytes 122912 | tf_op jit(solution)/shard_map/ppermute | solution.py:309
  53.2 0.5 collective-permute-start.12
  53.8 7.9 %shard_map.52 = (f32[1,2048,2048]{2,1,0:T(8,128)}, f32[1]{0:T(128)}) custom-call(bf16[2,40,2048]{2,1,0:T(8,128)(2,1)S(1)} %get-tuple-element.16.refs_0_, bf16[3,40,2048]{2,1,0:T(8,128)(2,1)S(1)} %collective-permute-done.refs_1_, bf16[2,40,2048]{2,1,0:T(8,128)(2,1)S(1)} %collective-permute-done.1.refs_2_, ...), custom_call_target="tpu_custom_call" | custom-call | flops 3221225472 | bytes 16777216 | tf_op jit(solution)/shard_map/pallas_call | solution.py:270
  61.8 2.5 %shard_map.53 = f32[1,768,768]{2,1,0:T(8,128)} custom-call(f32[1]{0:T(128)} %get-tuple-element.22.refs_0_, bf16[2,40,768]{2,1,0:T(8,128)(2,1)S(1)} %get-tuple-element.23.refs_1_, bf16[3,40,768]{2,1,0:T(8,128)(2,1)S(1)} %collective-permute-done.11.refs_2_, bf16[2,40,768]{2,1,0:T(8,128)(2,1)S(1)} %collective-permute-done.12.refs_3_, ...), custom_call_target="tpu_custom_call" | custom-call | flops 452984832 | bytes 2359296 | tf_op jit(solution)/shard_map/pallas_call | solution.py:270
  (30 shorter events, 0.2 us)
Async XLA Ops:
  0.6 1.6 %copy-start = (bf16[128,8192]{1,0:T(8,128)(2,1)S(1)}, bf16[128,8192]{1,0:T(8,128)(2,1)}, u32[]{:S(2)}) copy-start(bf16[128,8192]{1,0:T(8,128)(2,1)} %values_ref.2) | copy-start | bytes 6291460
  2.2 0.7 %copy-start.2 = (s32[128,2]{0,1:T(2,128)S(1)}, s32[128,2]{0,1:T(2,128)}, u32[]{:S(2)}) copy-start(s32[128,2]{0,1:T(2,128)} %param.5) | copy-start | bytes 3076
  2.9 5.9 %copy-start.1 = (bf16[128,3072]{1,0:T(8,128)(2,1)S(1)}, bf16[128,3072]{1,0:T(8,128)(2,1)}, u32[]{:S(2)}) copy-start(bf16[128,3072]{1,0:T(8,128)(2,1)} %values_ref.3) | copy-start | bytes 2359300
  4.3 26.6 %collective-permute-start = (bf16[3,40,2048]{2,1,0:T(8,128)(2,1)S(1)}, bf16[3,40,2048]{2,1,0:T(8,128)(2,1)S(1)}, u32[]{:S(2)}, u32[]{:S(2)}) collective-permute-start(bf16[3,40,2048]{2,1,0:T(8,128)(2,1)S(1)} %get-tuple-element.17), channel_id=1, source_target_pairs={{0,4},{1,13},{2,6},{3,15},{4,8},{5,1},{6,10},{7,3},{8,12},{9,5},{1... | collective-permute-start | bytes 1474568 | tf_op jit(solution)/shard_map/ppermute | solution.py:309
  7.3 7.8 %collective-permute-start.2 = (bf16[2,40,1024]{2,1,0:T(8,128)(2,1)S(1)}, bf16[2,40,1024]{2,1,0:T(8,128)(2,1)S(1)}, u32[]{:S(2)}, u32[]{:S(2)}) collective-permute-start(bf16[2,40,1024]{2,1,0:T(8,128)(2,1)S(1)} %get-tuple-element.19), channel_id=1, source_target_pairs={{0,2},{1,3},{2,0},{3,1},{4,6},{5,7},{6,4},{7,5},{8,10},{9,11},{10,... | collective-permute-start | bytes 491528 | tf_op jit(solution)/shard_map/ppermute | solution.py:309
  9.8 5.3 %collective-permute-start.3 = (bf16[2,40,384]{2,1,0:T(8,128)(2,1)S(1)}, bf16[2,40,384]{2,1,0:T(8,128)(2,1)S(1)}, u32[]{:S(2)}, u32[]{:S(2)}) collective-permute-start(bf16[2,40,384]{2,1,0:T(8,128)(2,1)S(1)} %get-tuple-element.20), channel_id=1, source_target_pairs={{0,2},{1,3},{2,0},{3,1},{4,6},{5,7},{6,4},{7,5},{8,10},{9,11},{10,... | collective-permute-start | bytes 184328 | tf_op jit(solution)/shard_map/ppermute | solution.py:309
  15.2 15.7 %collective-permute-start.4 = (bf16[3,40,1024]{2,1,0:T(8,128)(2,1)S(1)}, bf16[3,40,1024]{2,1,0:T(8,128)(2,1)S(1)}, u32[]{:S(2)}, u32[]{:S(2)}) collective-permute-start(bf16[3,40,1024]{2,1,0:T(8,128)(2,1)S(1)} %get-tuple-element.21), channel_id=1, source_target_pairs={{0,8},{1,9},{2,10},{3,11},{4,12},{5,13},{6,14},{7,15},{8,0},{9,1},... | collective-permute-start | bytes 737288 | tf_op jit(solution)/shard_map/ppermute | solution.py:309
  16.7 20.6 %collective-permute-start.6 = (bf16[2,40,1024]{2,1,0:T(8,128)(2,1)S(1)}, bf16[2,40,1024]{2,1,0:T(8,128)(2,1)S(1)}, u32[]{:S(2)}, u32[]{:S(2)}) collective-permute-start(bf16[2,40,1024]{2,1,0:T(8,128)(2,1)S(1)} %collective-permute-done.2.refs_5_), channel_id=1, source_target_pairs={{0,1},{1,0},{2,3},{3,2},{4,5},{5,4},{6,7},{7,6},{8,9},{9,8},{10,11... | collective-permute-start | bytes 491528 | tf_op jit(solution)/shard_map/ppermute | solution.py:309
  30.9 6.4 %collective-permute-start.13 = (bf16[3,40,384]{2,1,0:T(8,128)(2,1)S(1)}, bf16[3,40,384]{2,1,0:T(8,128)(2,1)S(1)}, u32[]{:S(2)}, u32[]{:S(2)}) collective-permute-start(bf16[3,40,384]{2,1,0:T(8,128)(2,1)S(1)} %get-tuple-element.27), channel_id=1, source_target_pairs={{0,8},{1,9},{2,10},{3,11},{4,12},{5,13},{6,14},{7,15},{8,0},{9,1},... | collective-permute-start | bytes 276488 | tf_op jit(solution)/shard_map/ppermute | solution.py:309
  31.0 14.8 %collective-permute-start.7 = (bf16[2,40,2048]{2,1,0:T(8,128)(2,1)S(1)}, bf16[2,40,2048]{2,1,0:T(8,128)(2,1)S(1)}, u32[]{:S(2)}, u32[]{:S(2)}) collective-permute-start(bf16[2,40,2048]{2,1,0:T(8,128)(2,1)S(1)} %get-tuple-element.30), channel_id=1, source_target_pairs={{0,2},{1,3},{2,0},{3,1},{4,6},{5,7},{6,4},{7,5},{8,10},{9,11},{10,... | collective-permute-start | bytes 983048 | tf_op jit(solution)/shard_map/ppermute | solution.py:309
  32.7 11.4 %collective-permute-start.9 = (bf16[2,40,1024]{2,1,0:T(8,128)(2,1)S(1)}, bf16[2,40,1024]{2,1,0:T(8,128)(2,1)S(1)}, u32[]{:S(2)}, u32[]{:S(2)}) collective-permute-start(bf16[2,40,1024]{2,1,0:T(8,128)(2,1)S(1)} %get-tuple-element.32), channel_id=1, source_target_pairs={{0,2},{1,3},{2,0},{3,1},{4,6},{5,7},{6,4},{7,5},{8,10},{9,11},{10,... | collective-permute-start | bytes 491528 | tf_op jit(solution)/shard_map/ppermute | solution.py:309
  33.2 16.8 %collective-permute-start.5 = (bf16[2,40,1024]{2,1,0:T(8,128)(2,1)S(1)}, bf16[2,40,1024]{2,1,0:T(8,128)(2,1)S(1)}, u32[]{:S(2)}, u32[]{:S(2)}) collective-permute-start(bf16[2,40,1024]{2,1,0:T(8,128)(2,1)S(1)} %get-tuple-element.33), channel_id=1, source_target_pairs={{0,1},{1,0},{2,3},{3,2},{4,5},{5,4},{6,7},{7,6},{8,9},{9,8},{10,11... | collective-permute-start | bytes 491528 | tf_op jit(solution)/shard_map/ppermute | solution.py:309
  37.3 8.4 %collective-permute-start.11 = (bf16[3,40,768]{2,1,0:T(8,128)(2,1)S(1)}, bf16[3,40,768]{2,1,0:T(8,128)(2,1)S(1)}, u32[]{:S(2)}, u32[]{:S(2)}) collective-permute-start(bf16[3,40,768]{2,1,0:T(8,128)(2,1)S(1)} %get-tuple-element.25), channel_id=1, source_target_pairs={{0,4},{1,13},{2,6},{3,15},{4,8},{5,1},{6,10},{7,3},{8,12},{9,5},{1... | collective-permute-start | bytes 552968 | tf_op jit(solution)/shard_map/ppermute | solution.py:309
  37.4 15.9 %collective-permute-start.1 = (bf16[2,40,2048]{2,1,0:T(8,128)(2,1)S(1)}, bf16[2,40,2048]{2,1,0:T(8,128)(2,1)S(1)}, u32[]{:S(2)}, u32[]{:S(2)}) collective-permute-start(bf16[2,40,2048]{2,1,0:T(8,128)(2,1)S(1)} %get-tuple-element.31), channel_id=1, source_target_pairs={{0,1},{1,0},{2,3},{3,2},{4,5},{5,4},{6,7},{7,6},{8,9},{9,8},{10,11... | collective-permute-start | bytes 983048 | tf_op jit(solution)/shard_map/ppermute | solution.py:309
  44.1 4.2 %collective-permute-start.18 = (bf16[2,40,384]{2,1,0:T(8,128)(2,1)S(1)}, bf16[2,40,384]{2,1,0:T(8,128)(2,1)S(1)}, u32[]{:S(2)}, u32[]{:S(2)}) collective-permute-start(bf16[2,40,384]{2,1,0:T(8,128)(2,1)S(1)} %get-tuple-element.36), channel_id=1, source_target_pairs={{0,2},{1,3},{2,0},{3,1},{4,6},{5,7},{6,4},{7,5},{8,10},{9,11},{10,... | collective-permute-start | bytes 184328 | tf_op jit(solution)/shard_map/ppermute | solution.py:309
  45.7 4.2 %collective-permute-start.10 = (bf16[2,40,1024]{2,1,0:T(8,128)(2,1)S(1)}, bf16[2,40,1024]{2,1,0:T(8,128)(2,1)S(1)}, u32[]{:S(2)}, u32[]{:S(2)}) collective-permute-start(bf16[2,40,1024]{2,1,0:T(8,128)(2,1)S(1)} %collective-permute-done.9.refs_9_), channel_id=1, source_target_pairs={{0,1},{1,0},{2,3},{3,2},{4,5},{5,4},{6,7},{7,6},{8,9},{9,8},{10,11... | collective-permute-start | bytes 491528 | tf_op jit(solution)/shard_map/ppermute | solution.py:309
  45.8 8.0 %collective-permute-start.8 = (bf16[2,40,2048]{2,1,0:T(8,128)(2,1)S(1)}, bf16[2,40,2048]{2,1,0:T(8,128)(2,1)S(1)}, u32[]{:S(2)}, u32[]{:S(2)}) collective-permute-start(bf16[2,40,2048]{2,1,0:T(8,128)(2,1)S(1)} %collective-permute-done.7.refs_7_), channel_id=1, source_target_pairs={{0,1},{1,0},{2,3},{3,2},{4,5},{5,4},{6,7},{7,6},{8,9},{9,8},{10,11... | collective-permute-start | bytes 983048 | tf_op jit(solution)/shard_map/ppermute | solution.py:309
  48.3 4.9 %collective-permute-start.16 = (bf16[2,40,768]{2,1,0:T(8,128)(2,1)S(1)}, bf16[2,40,768]{2,1,0:T(8,128)(2,1)S(1)}, u32[]{:S(2)}, u32[]{:S(2)}) collective-permute-start(bf16[2,40,768]{2,1,0:T(8,128)(2,1)S(1)} %get-tuple-element.28), channel_id=1, source_target_pairs={{0,2},{1,3},{2,0},{3,1},{4,6},{5,7},{6,4},{7,5},{8,10},{9,11},{10,... | collective-permute-start | bytes 368648 | tf_op jit(solution)/shard_map/ppermute | solution.py:309
  50.0 11.8 %collective-permute-start.15 = (bf16[2,40,384]{2,1,0:T(8,128)(2,1)S(1)}, bf16[2,40,384]{2,1,0:T(8,128)(2,1)S(1)}, u32[]{:S(2)}, u32[]{:S(2)}) collective-permute-start(bf16[2,40,384]{2,1,0:T(8,128)(2,1)S(1)} %collective-permute-done.3.refs_6_), channel_id=1, source_target_pairs={{0,1},{1,0},{2,3},{3,2},{4,5},{5,4},{6,7},{7,6},{8,9},{9,8},{10,11... | collective-permute-start | bytes 184328 | tf_op jit(solution)/shard_map/ppermute | solution.py:309
  50.0 11.8 %collective-permute-start.14 = (bf16[2,40,384]{2,1,0:T(8,128)(2,1)S(1)}, bf16[2,40,384]{2,1,0:T(8,128)(2,1)S(1)}, u32[]{:S(2)}, u32[]{:S(2)}) collective-permute-start(bf16[2,40,384]{2,1,0:T(8,128)(2,1)S(1)} %get-tuple-element.37), channel_id=1, source_target_pairs={{0,1},{1,0},{2,3},{3,2},{4,5},{5,4},{6,7},{7,6},{8,9},{9,8},{10,11... | collective-permute-start | bytes 184328 | tf_op jit(solution)/shard_map/ppermute | solution.py:309
  53.2 8.5 %collective-permute-start.19 = (bf16[2,40,384]{2,1,0:T(8,128)(2,1)S(1)}, bf16[2,40,384]{2,1,0:T(8,128)(2,1)S(1)}, u32[]{:S(2)}, u32[]{:S(2)}) collective-permute-start(bf16[2,40,384]{2,1,0:T(8,128)(2,1)S(1)} %collective-permute-done.18.refs_10_), channel_id=1, source_target_pairs={{0,1},{1,0},{2,3},{3,2},{4,5},{5,4},{6,7},{7,6},{8,9},{9,8},{10,11... | collective-permute-start | bytes 184328 | tf_op jit(solution)/shard_map/ppermute | solution.py:309
  53.2 8.5 %collective-permute-start.12 = (bf16[2,40,768]{2,1,0:T(8,128)(2,1)S(1)}, bf16[2,40,768]{2,1,0:T(8,128)(2,1)S(1)}, u32[]{:S(2)}, u32[]{:S(2)}) collective-permute-start(bf16[2,40,768]{2,1,0:T(8,128)(2,1)S(1)} %get-tuple-element.35), channel_id=1, source_target_pairs={{0,1},{1,0},{2,3},{3,2},{4,5},{5,4},{6,7},{7,6},{8,9},{9,8},{10,11... | collective-permute-start | bytes 368648 | tf_op jit(solution)/shard_map/ppermute | solution.py:309
  53.7 8.0 %collective-permute-start.17 = (bf16[2,40,768]{2,1,0:T(8,128)(2,1)S(1)}, bf16[2,40,768]{2,1,0:T(8,128)(2,1)S(1)}, u32[]{:S(2)}, u32[]{:S(2)}) collective-permute-start(bf16[2,40,768]{2,1,0:T(8,128)(2,1)S(1)} %collective-permute-done.16.refs_8_), channel_id=1, source_target_pairs={{0,1},{1,0},{2,3},{3,2},{4,5},{5,4},{6,7},{7,6},{8,9},{9,8},{10,11... | collective-permute-start | bytes 368648 | tf_op jit(solution)/shard_map/ppermute | solution.py:309

commit v3 on v0

--- a/solution.py
+++ b/solution.py
@@ -1,10 +1,15 @@
+import functools
 import math
 
 import jax
 import jax.numpy as jnp
 import numpy as np
 from jax import lax
+from jax.experimental import pallas as pl
+from jax.experimental.pallas import tpu as pltpu
 from jax.sharding import PartitionSpec as P
+
+SLOT_ROWS = 48
 
 
 def block_table(side):
@@ -38,7 +43,7 @@
     return jnp.concatenate([blocks[:, first_ids], blocks[:, second_ids]], axis=2)
 
 
-def product(flat_data, left_start, right_start, width):
+def block_product(flat_data, left_start, right_start, width):
     left = lax.dynamic_slice_in_dim(flat_data, left_start, width, 1)
     right = lax.dynamic_slice_in_dim(flat_data, right_start, width, 1)
     return lax.dot_general(
@@ -46,7 +51,7 @@
     )
 
 
-def shards(inputs, hidden_grads, routes):
+def shards_any(inputs, hidden_grads, routes):
     chosen = jnp.any(routes == 0, axis=1).astype(jnp.int32)
     core_index = lax.axis_index("hid")
     chip_index = lax.axis_index("tok")
@@ -68,17 +73,306 @@
     input_width = flat_inputs.shape[1] // 2
     grad_width = flat_grads.shape[1] // 2
     right_pick = jnp.where(diagonal, core_index, 1 - core_index)
-    input_sum = product(
+    input_sum = block_product(
         flat_inputs, core_index * input_width, right_pick * input_width, input_width
     )
-    grad_sum = product(flat_grads, core_index * grad_width, right_pick * grad_width, grad_width)
+    grad_sum = block_product(flat_grads, core_index * grad_width, right_pick * grad_width, grad_width)
     return ((input_sum / total)[None], (grad_sum / total)[None])
+
+
+N_X = 2
+N_Z = 4
+SLOTS = N_X * N_Z
+SMEM = pl.BlockSpec(memory_space=pltpu.SMEM)
+VMEM = pl.BlockSpec(memory_space=pltpu.VMEM)
+ANY = pl.BlockSpec(memory_space=pl.ANY)
+
+
+def slot_table():
+    first_ids, second_ids = block_table(4)
+    slots = np.zeros((N_Z, N_X, 3), np.int32)
+    for z in range(N_Z):
+        zero = {int(first_ids[z * N_X]), int(second_ids[z * N_X])}
+        one = {int(first_ids[z * N_X + 1]), int(second_ids[z * N_X + 1])}
+        common = max(zero & one)
+        (a,) = zero - {common}
+        (b,) = one - {common}
+        slots[z, 0] = (a, common, b)
+        slots[z, 1] = (b, common, a)
+    return slots
+
+
+def lookup(values, index):
+    found = jnp.int32(int(values[0]))
+    for i in range(1, len(values)):
+        found = jnp.where(index == i, jnp.int32(int(values[i])), found)
+    return found
+
+
+def place():
+    chip = lax.axis_index("tok").astype(jnp.int32)
+    return lax.div(chip, N_X), lax.rem(chip, N_X), lax.axis_index("hid").astype(jnp.int32)
+
+
+def block_at(plane, column, row):
+    return lookup(slot_table().reshape(-1, 3)[:, row], plane * N_X + column)
+
+
+def pack_kernel(far_routes, grads, inputs, p1_ref, p2_ref, p2_i_ref, x0_ref, own_ref, *scratch):
+    routes_ref, held, held_i, packed, sems = scratch
+    plane, column, core = place()
+    capacity, total = x0_ref.shape
+    width = held.shape[2]
+    sources = [(grads, held, 0), (inputs, held_i, width)]
+    copies = []
+    for n, (source, buffer, _) in enumerate(sources):
+        size = buffer.shape[2]
+        for block in range(4):
+            copies.append(
+                pltpu.make_async_copy(
+                    source.at[:, block * size : (block + 1) * size],
+                    buffer.at[block],
+                    sems.at[4 * n + block],
+                )
+            )
+    routes_copy = pltpu.make_async_copy(far_routes, routes_ref, sems.at[8])
+    routes_copy.start()
+    for copy in copies:
+        copy.start()
+    routes_copy.wait()
+    chosen = (routes_ref[0:1, :] == 0) | (routes_ref[1:2, :] == 0)
+    tokens = chosen.shape[1]
+    flags = jnp.where(chosen, 1.0, 0.0)
+    before = (
+        lax.broadcasted_iota(jnp.int32, (tokens, tokens), 0)
+        <= lax.broadcasted_iota(jnp.int32, (tokens, tokens), 1)
+    )
+    rank = jnp.dot(
+        flags.astype(BF16),
+        jnp.where(before, 1.0, 0.0).astype(BF16),
+        preferred_element_type=jnp.float32,
+    )
+    slot = lax.broadcasted_iota(jnp.int32, (capacity, tokens), 0).astype(jnp.float32) + 1.0
+    picker = jnp.where((rank == slot) & chosen, 1.0, 0.0)
+    empty = (jnp.sum(picker, axis=1, keepdims=True) == 0.0) & (
+        lax.broadcasted_iota(jnp.int32, (capacity, 128), 1) == 0
+    )
+    picker = picker.astype(BF16)
+    for n, (_, buffer, low) in enumerate(sources):
+        for block in range(4):
+            copies[4 * n + block].wait()
+            got = jnp.dot(picker, buffer[block], preferred_element_type=jnp.float32)
+            if n == 1:
+                head = jnp.where(empty, jnp.inf, got[:, :128])
+                packed[block, :, low : low + 128] = head.astype(BF16)
+                packed[block, :, low + 128 :] = got[:, 128:].astype(BF16)
+            else:
+                packed[block, :, :width] = got.astype(BF16)
+    to_plane = lax.rem(plane + jnp.where(core == 0, 1, 3), N_Z)
+    for row in range(3):
+        p1_ref[row] = packed[block_at(to_plane, column, row)]
+    x0_block = jnp.where(
+        core == 0, block_at(plane, 1 - column, 1), block_at(plane, 1 - column, 0)
+    )
+    x0_ref[...] = packed[x0_block]
+    to_plane = lax.rem(plane + 2, N_Z)
+    to_column = jnp.where(core == 0, column, 1 - column)
+    for row in range(2):
+        block = block_at(to_plane, to_column, row)
+        p2_ref[row] = packed[block, :, :width]
+        p2_i_ref[row] = packed[block, :, width:]
+        own_ref[row] = packed[block_at(plane, column, row)]
+
+
+BF16 = jnp.bfloat16
+
+
+def pack(routes_t, grads, inputs, capacity):
+    tokens = routes_t.shape[1]
+    width, width_i = grads.shape[1] // 4, inputs.shape[1] // 4
+    total = width + width_i
+    shapes = [(3, capacity, total), (2, capacity, width), (2, capacity, width_i)]
+    shapes += [(capacity, total), (2, capacity, total)]
+    operands = [pltpu.with_memory_space_constraint(a, pltpu.HBM) for a in (routes_t, grads, inputs)]
+    return pl.pallas_call(
+        pack_kernel,
+        out_shape=[jax.ShapeDtypeStruct(s, BF16) for s in shapes],
+        in_specs=[pl.BlockSpec(memory_space=pltpu.HBM)] * 3,
+        out_specs=[VMEM] * len(shapes),
+        scratch_shapes=[
+            pltpu.VMEM(routes_t.shape, jnp.int32),
+            pltpu.VMEM((4, tokens, width), BF16),
+            pltpu.VMEM((4, tokens, width_i), BF16),
+            pltpu.VMEM((4, capacity, total), BF16),
+            pltpu.SemaphoreType.DMA((9,)),
+        ],
+        compiler_params=pltpu.CompilerParams(vmem_limit_bytes=12 * 2**20),
+        cost_estimate=pl.CostEstimate(
+            flops=2 * 4 * capacity * tokens * total,
+            bytes_accessed=8 * tokens * total,
+            transcendentals=0,
+        ),
+    )(*operands)
+
+
+def assemble(data, pieces, start):
+    own, x0, hx0, p1, hp1, x1, hx1, p2, hp2 = pieces
+    core = lax.axis_index("hid")
+    capacity = own.shape[1]
+    size = data.shape[2]
+    span = pl.ds(start, size)
+    for block in range(2):
+        whole = [own.at[block], p1.at[block]]
+        whole = [ref[:, span] for ref in whole]
+        whole.append(jnp.where((core == 0) == (block == 1), x0[:, span], hx0[:, span]))
+        whole += [hp1[block], x1[1 - block], hx1[1 - block], p2[block], hp2[block]]
+        for slot, piece in enumerate(whole):
+            low = slot * SLOT_ROWS
+            data[block, low + 32 : low + SLOT_ROWS, :] = jnp.zeros((SLOT_ROWS - 32, size), BF16)
+            data[block, low : low + capacity, :] = piece
+
+
+def clear_marks(data, capacity, slots):
+    for block in range(2):
+        head = data[block, :, 0:128].astype(jnp.float32)
+        gone = head == jnp.inf
+        if block == 0:
+            count = capacity * slots - jnp.sum(jnp.where(gone, 1.0, 0.0))
+        data[block, :, 0:128] = jnp.where(gone, 0.0, head).astype(jnp.bfloat16)
+    return 1.0 / count
+
+
+def sides():
+    plane, column, core = place()
+    chip = plane * N_X + column
+    first_ids, _ = block_table(4)
+    first_is_common = lookup(
+        (slot_table().reshape(-1, 3)[:, 0] != first_ids).astype(np.int32), chip
+    )
+    left = jnp.where(core == 0, first_is_common, 1 - first_is_common)
+    return left, jnp.where(lax.rem(chip, 4) == 3, left, 1 - left)
+
+
+def product(scale, left, right):
+    return scale * lax.dot_general(
+        left, right, (((0,), (0,)), ((), ())), preferred_element_type=jnp.float32
+    )
+
+
+def multiply(scale, data, out_ref, stage, sems, start):
+    left, right = sides()
+    steps = sems.shape[0]
+    size = stage.shape[0] // steps
+    copies = []
+    for i in range(steps):
+        rows = pl.ds(i * size, size)
+        to = pl.ds(start + i * size, size)
+        stage[rows, :] = product(scale, data[left, :, to], data[right])
+        copies.append(pltpu.make_async_copy(stage.at[rows], out_ref.at[0, to], sems.at[i]))
+        copies[-1].start()
+    for copy in copies:
+        copy.wait()
+
+
+def cost(rows, width):
+    return pl.CostEstimate(
+        flops=2 * SLOTS * SLOT_ROWS * rows * width,
+        bytes_accessed=4 * rows * width,
+        transcendentals=0,
+    )
+
+
+def tile_kernel(marked, *refs):
+    refs = list(refs)
+    scale_in = None if marked else refs.pop(0)
+    data, stage, sems = refs[-3:]
+    pieces = refs[:9]
+    out_ref = refs[9]
+    assemble(data, pieces, pieces[0].shape[2] - data.shape[2] if marked else 0)
+    if marked:
+        scale = clear_marks(data, pieces[0].shape[1], SLOTS)
+        refs[10][0] = scale
+    else:
+        scale = scale_in[0]
+    multiply(scale, data, out_ref, stage, sems, 0)
+
+
+def tile(scale, pieces, steps, limit):
+    marked = scale is None
+    width = pieces[-1].shape[2]
+    out_shape = [jax.ShapeDtypeStruct((1, width, width), jnp.float32)]
+    if marked:
+        out_shape.append(jax.ShapeDtypeStruct((1,), jnp.float32))
+    return pl.pallas_call(
+        functools.partial(tile_kernel, marked),
+        out_shape=out_shape,
+        in_specs=([] if marked else [SMEM]) + [VMEM] * len(pieces),
+        out_specs=[ANY, SMEM] if marked else [ANY],
+        scratch_shapes=[
+            pltpu.VMEM((2, SLOTS * SLOT_ROWS, width), BF16),
+            pltpu.VMEM((width, width), jnp.float32),
+            pltpu.SemaphoreType.DMA((steps,)),
+        ],
+        compiler_params=pltpu.CompilerParams(vmem_limit_bytes=limit),
+        cost_estimate=cost(width, width),
+    )(*([] if marked else [scale]), *pieces)
+
+
+def moves(step):
+    pairs = []
+    for z in range(N_Z):
+        for x in range(N_X):
+            for core in range(2):
+                to_z, to_x, to_core = step(z, x, core)
+                source = (z * N_X + x) * 2 + core
+                pairs.append((source, (to_z % N_Z * N_X + to_x) * 2 + to_core))
+    return pairs
+
+
+ALONG_Z = moves(lambda z, x, core: (z + (1, 3)[core], x, core))
+ACROSS_Z = moves(lambda z, x, core: (z + 2, (x, 1 - x)[core], core))
+ALONG_X = moves(lambda z, x, core: (z, 1 - x, core))
+CORES = moves(lambda z, x, core: (z, x, 1 - core))
+
+
+def after(array, *done):
+    return lax.optimization_barrier((array, *done))[0]
+
+
+def send(array, pairs):
+    return lax.ppermute(array, ("tok", "hid"), pairs)
+
+
+def both(array):
+    return [array, send(array, CORES)]
+
+
+def shards_eight(inputs, hidden_grads, routes):
+    capacity = routes.shape[0] * 5 // 16
+    width = hidden_grads.shape[1] // 4
+    p1, p2, p2_i, x0, own = pack(routes.T, hidden_grads, inputs, capacity)
+    p1 = send(p1, ALONG_Z)
+    x0 = send(x0, ALONG_X)
+    hx0 = send(x0, CORES)
+    p1 = after(p1, x0)
+    p2_i = send(after(p2_i, p1), ACROSS_Z)
+    p2 = send(after(p2, p1), ACROSS_Z)
+    x1_i = send(p1[1:, :, width:], ALONG_X)
+    x1 = send(p1[1:, :, :width], ALONG_X)
+    x1_i = after(x1_i, p2_i)
+    hp1_i = send(p1[:2, :, width:], CORES)
+    hp1 = send(p1[:2, :, :width], CORES)
+    base = [own, x0, hx0, p1]
+    input_tile, scale = tile(None, base + [hp1_i, *both(x1_i), *both(p2_i)], 3, 12 * 2**20)
+    p2 = after(p2, scale)
+    (grad_tile,) = tile(scale, base + [hp1, *both(x1), *both(p2)], 8, 28 * 2**20)
+    return input_tile, grad_tile
 
 
 def solution(mesh):
     placed = (P(("parts", "tok"), None), P(("parts", "tok"), None), P(("parts", "tok"), None))
     return jax.shard_map(
-        shards,
+        shards_eight if mesh.shape["tok"] == N_X * N_Z else shards_any,
         mesh=mesh,
         in_specs=placed,
         out_specs=(P(("parts", "tok", "hid"), None, None), P(("parts", "tok", "hid"), None, None)),

time: 126 us -> 55.8 us (0.44)
  the two profiles are of different devices: /device:TPU:8 before, /device:TPU:0 now
where the time goes in v3:
time: 55.8 us; the launch traced here: 55.6 us
  waiting for transfers between devices  30.5 us (55%)
  Pallas kernels  12.8 us (23%)
  starting transfers between devices  11.6 us (21%)
  between operations  0.67 us (1%)
    ppermute x13, waiting for transfers between devices, send(): return lax.ppermute(array, ('tok', 'hid'), pairs)  30.5 us
    ppermute x13, starting transfers between devices, send(): return lax.ppermute(array, ('tok', 'hid'), pairs)  11.6 us
    pallas_call x2, Pallas kernels, tile(): pl.pallas_call(functools.partial(tile_kernel, marked), out_shape=out_shap...  10.1 us
    pallas_call x1, Pallas kernels, pack(): pl.pallas_call(pack_kernel, out_shape=[jax.ShapeDtypeStruct(s, BF16) for...  2.71 us
  transfers between devices with their start and end apart: 13, of which 8 were waited for; matrix products, arithmetic and copies ran while one was open for 0% of the time, Pallas kernels for 5%

profile of v3, /device:TPU:0, one launch (start us, length us, event | category | flops | bytes accessed | tf_op | source)
XLA Modules:
  0.0 55.6 jit_solution(12644611460806837288)
XLA Ops:
  0.6 2.7 %shard_map.50 = (bf16[3,40,2816]{2,1,0:T(8,128)(2,1)S(1)}, bf16[2,40,2048]{2,1,0:T(8,128)(2,1)S(1)}, bf16[2,40,768]{2,1,0:T(8,128)(2,1)S(1)}, bf16[40,2816]{1,0:T(8,128)(2,1)S(1)}, bf16[2,40,2816]{2,1,0:T(8,128)(2,1)S(1)}) custom-call(s32[2,128]{1,0:T(2,128)} %bitcast.1, bf16[128,8192]{1,0:T(8,128)(2,1)} %grads.1, bf16[128,3072]{1,0:T(8,128)(2,1)} %inputs.1), custom_call_target="tpu_custom_call" | custom-call | flops 115343360 | bytes 2883584 | tf_op jit(solution)/shard_map/pallas_call | solution.py:197
  3.4 3.1 %collective-permute-start.2 = (bf16[3,40,2816]{2,1,0:T(8,128)(2,1)S(1)}, bf16[3,40,2816]{2,1,0:T(8,128)(2,1)S(1)}, u32[]{:S(2)}, u32[]{:S(2)}) collective-permute-start(bf16[3,40,2816]{2,1,0:T(8,128)(2,1)S(1)} %get-tuple-element.16), channel_id=1, source_target_pairs={{0,4},{1,13},{2,6},{3,15},{4,8},{5,1},{6,10},{7,3},{8,12},{9,5},{1... | collective-permute-start | bytes 2027528 | tf_op jit(solution)/shard_map/ppermute | solution.py:343
  6.4 1.5 %collective-permute-start = (bf16[40,2816]{1,0:T(8,128)(2,1)S(1)}, bf16[40,2816]{1,0:T(8,128)(2,1)S(1)}, u32[]{:S(2)}, u32[]{:S(2)}) collective-permute-start(bf16[40,2816]{1,0:T(8,128)(2,1)S(1)} %get-tuple-element.15), channel_id=1, source_target_pairs={{0,2},{1,3},{2,0},{3,1},{4,6},{5,7},{6,4},{7,5},{8,10},{9,11},{10,... | collective-permute-start | bytes 675848 | tf_op jit(solution)/shard_map/ppermute | solution.py:343
  7.9 6.3 %collective-permute-done.refs_1_.refs_2_ = bf16[40,2816]{1,0:T(8,128)(2,1)S(1)} collective-permute-done((bf16[40,2816]{1,0:T(8,128)(2,1)S(1)}, bf16[40,2816]{1,0:T(8,128)(2,1)S(1)}, u32[]{:S(2)}, u32[]{:S(2)}) %collective-permute-start) | collective-permute-done | bytes 225312 | tf_op jit(solution)/shard_map/ppermute | solution.py:343
  14.3 0.7 %collective-permute-start.1 = (bf16[40,2816]{1,0:T(8,128)(2,1)S(1)}, bf16[40,2816]{1,0:T(8,128)(2,1)S(1)}, u32[]{:S(2)}, u32[]{:S(2)}) collective-permute-start(bf16[40,2816]{1,0:T(8,128)(2,1)S(1)} %collective-permute-done.refs_1_.refs_2_), channel_id=1, source_target_pairs={{0,1},{1,0},{2,3},{3,2},{4,5},{5,4},{6,7},{7,6},{8,9},{9,8},{10,11... | collective-permute-start | bytes 675848 | tf_op jit(solution)/shard_map/ppermute | solution.py:343
  14.9 8.9 %collective-permute-done.2.refs_3_.refs_4_ = bf16[3,40,2816]{2,1,0:T(8,128)(2,1)S(1)} collective-permute-done((bf16[3,40,2816]{2,1,0:T(8,128)(2,1)S(1)}, bf16[3,40,2816]{2,1,0:T(8,128)(2,1)S(1)}, u32[]{:S(2)}, u32[]{:S(2)}) %collective-permute-start.2) | collective-permute-done | bytes 675872 | tf_op jit(solution)/shard_map/ppermute | solution.py:343
  23.8 1.8 %collective-permute-start.5 = (bf16[2,40,768]{2,1,0:T(8,128)(2,1)S(1)}, bf16[2,40,768]{2,1,0:T(8,128)(2,1)S(1)}, u32[]{:S(2)}, u32[]{:S(2)}) collective-permute-start(bf16[2,40,768]{2,1,0:T(8,128)(2,1)S(1)} %get-tuple-element.19), channel_id=1, source_target_pairs={{0,8},{1,11},{2,10},{3,9},{4,12},{5,15},{6,14},{7,13},{8,0},{9,3},... | collective-permute-start | bytes 368648 | tf_op jit(solution)/shard_map/ppermute | solution.py:343
  25.6 1.2 %collective-permute-start.11 = (bf16[2,40,2048]{2,1,0:T(8,128)(2,1)S(1)}, bf16[2,40,2048]{2,1,0:T(8,128)(2,1)S(1)}, u32[]{:S(2)}, u32[]{:S(2)}) collective-permute-start(bf16[2,40,2048]{2,1,0:T(8,128)(2,1)S(1)} %get-tuple-element.24), channel_id=1, source_target_pairs={{0,8},{1,11},{2,10},{3,9},{4,12},{5,15},{6,14},{7,13},{8,0},{9,3},... | collective-permute-start | bytes 983048 | tf_op jit(solution)/shard_map/ppermute | solution.py:343
  26.8 1.5 %collective-permute-start.9 = (bf16[2,40,2048]{2,1,0:T(8,128)(2,1)S(1)}, bf16[2,40,2048]{2,1,0:T(8,128)(2,1)S(1)}, u32[]{:S(2)}, u32[]{:S(2)}) collective-permute-start(bf16[2,40,2048]{2,1,0:T(8,128)(2,1)S(1)} %get-tuple-element.26), channel_id=1, source_target_pairs={{0,2},{1,3},{2,0},{3,1},{4,6},{5,7},{6,4},{7,5},{8,10},{9,11},{10,... | collective-permute-start | bytes 983048 | tf_op jit(solution)/shard_map/ppermute | solution.py:343
  28.3 0.6 %collective-permute-start.4 = (bf16[2,40,768]{2,1,0:T(8,128)(2,1)S(1)}, bf16[2,40,768]{2,1,0:T(8,128)(2,1)S(1)}, u32[]{:S(2)}, u32[]{:S(2)}) collective-permute-start(bf16[2,40,768]{2,1,0:T(8,128)(2,1)S(1)} %get-tuple-element.28), channel_id=1, source_target_pairs={{0,2},{1,3},{2,0},{3,1},{4,6},{5,7},{6,4},{7,5},{8,10},{9,11},{10,... | collective-permute-start | bytes 368648 | tf_op jit(solution)/shard_map/ppermute | solution.py:343
  28.9 10.7 %collective-permute-done.5.refs_7_ = bf16[2,40,768]{2,1,0:T(8,128)(2,1)S(1)} collective-permute-done((bf16[2,40,768]{2,1,0:T(8,128)(2,1)S(1)}, bf16[2,40,768]{2,1,0:T(8,128)(2,1)S(1)}, u32[]{:S(2)}, u32[]{:S(2)}) %collective-permute-start.5) | collective-permute-done | bytes 122912 | tf_op jit(solution)/shard_map/ppermute | solution.py:343
  39.6 0.0 collective-permute-start.3
  39.6 0.5 collective-permute-start.7
  40.1 0.1 collective-permute-start.6
  40.2 0.7 %collective-permute-done.3.refs_4_ = bf16[2,40,768]{2,1,0:T(8,128)(2,1)S(1)} collective-permute-done((bf16[2,40,768]{2,1,0:T(8,128)(2,1)S(1)}, bf16[2,40,768]{2,1,0:T(8,128)(2,1)S(1)}, u32[]{:S(2)}, u32[]{:S(2)}) %collective-permute-start.3) | collective-permute-done | bytes 122912 | tf_op jit(solution)/shard_map/ppermute | solution.py:343
  40.9 0.1 collective-permute-start.8
  41.1 0.0 collective-permute-done.7.refs_8_
  41.1 0.3 collective-permute-done.6.refs_6_
  41.5 2.6 %shard_map.51 = (f32[1,768,768]{2,1,0:T(8,128)}, f32[1]{0:T(128)}) custom-call(bf16[2,40,2816]{2,1,0:T(8,128)(2,1)S(1)} %get-tuple-element.14.refs_0_.refs_1_, bf16[40,2816]{1,0:T(8,128)(2,1)S(1)} %collective-permute-done.refs_1_.refs_2_, bf16[40,2816]{1,0:T(8,128)(2,1)S(1)} %collective-permute-done.1.refs_2_.refs_3_, ...), custom_call_target="tpu_custom_call" | custom-call | flops 452984832 | bytes 2359296 | tf_op jit(solution)/shard_map/pallas_call | solution.py:306
  44.0 1.9 %collective-permute-done.11.refs_8_ = bf16[2,40,2048]{2,1,0:T(8,128)(2,1)S(1)} collective-permute-done((bf16[2,40,2048]{2,1,0:T(8,128)(2,1)S(1)}, bf16[2,40,2048]{2,1,0:T(8,128)(2,1)S(1)}, u32[]{:S(2)}, u32[]{:S(2)}) %collective-permute-start.11) | collective-permute-done | bytes 327712 | tf_op jit(solution)/shard_map/ppermute | solution.py:343
  46.0 0.5 collective-permute-start.12
  46.5 1.1 %collective-permute-done.10.refs_7_ = bf16[2,40,2048]{2,1,0:T(8,128)(2,1)S(1)} collective-permute-done((bf16[2,40,2048]{2,1,0:T(8,128)(2,1)S(1)}, bf16[2,40,2048]{2,1,0:T(8,128)(2,1)S(1)}, u32[]{:S(2)}, u32[]{:S(2)}) %collective-permute-start.10) | collective-permute-done | bytes 327712 | tf_op jit(solution)/shard_map/ppermute | solution.py:343
  47.6 0.5 collective-permute-done.12.refs_9_
  48.1 7.5 %shard_map.52 = f32[1,2048,2048]{2,1,0:T(8,128)} custom-call(f32[1]{0:T(128)} %get-tuple-element.22.refs_0_, bf16[2,40,2816]{2,1,0:T(8,128)(2,1)S(1)} %get-tuple-element.14.refs_0_.refs_1_, bf16[40,2816]{1,0:T(8,128)(2,1)S(1)} %collective-permute-done.refs_1_.refs_2_, bf16[40,2816]{1,0:T(8,128)(2,1)S(1)} %collective-permute-done.1.refs_2_.refs_3_, ...), custom_call_target="tpu_custom_call" | custom-call | flops 3221225472 | bytes 16777216 | tf_op jit(solution)/shard_map/pallas_call | solution.py:306
  (7 shorter events, 0.1 us)
Async XLA Ops:
  3.4 20.4 %collective-permute-start.2 = (bf16[3,40,2816]{2,1,0:T(8,128)(2,1)S(1)}, bf16[3,40,2816]{2,1,0:T(8,128)(2,1)S(1)}, u32[]{:S(2)}, u32[]{:S(2)}) collective-permute-start(bf16[3,40,2816]{2,1,0:T(8,128)(2,1)S(1)} %get-tuple-element.16), channel_id=1, source_target_pairs={{0,4},{1,13},{2,6},{3,15},{4,8},{5,1},{6,10},{7,3},{8,12},{9,5},{1... | collective-permute-start | bytes 2027528 | tf_op jit(solution)/shard_map/ppermute | solution.py:343
  6.4 7.8 %collective-permute-start = (bf16[40,2816]{1,0:T(8,128)(2,1)S(1)}, bf16[40,2816]{1,0:T(8,128)(2,1)S(1)}, u32[]{:S(2)}, u32[]{:S(2)}) collective-permute-start(bf16[40,2816]{1,0:T(8,128)(2,1)S(1)} %get-tuple-element.15), channel_id=1, source_target_pairs={{0,2},{1,3},{2,0},{3,1},{4,6},{5,7},{6,4},{7,5},{8,10},{9,11},{10,... | collective-permute-start | bytes 675848 | tf_op jit(solution)/shard_map/ppermute | solution.py:343
  14.3 25.9 %collective-permute-start.1 = (bf16[40,2816]{1,0:T(8,128)(2,1)S(1)}, bf16[40,2816]{1,0:T(8,128)(2,1)S(1)}, u32[]{:S(2)}, u32[]{:S(2)}) collective-permute-start(bf16[40,2816]{1,0:T(8,128)(2,1)S(1)} %collective-permute-done.refs_1_.refs_2_), channel_id=1, source_target_pairs={{0,1},{1,0},{2,3},{3,2},{4,5},{5,4},{6,7},{7,6},{8,9},{9,8},{10,11... | collective-permute-start | bytes 675848 | tf_op jit(solution)/shard_map/ppermute | solution.py:343
  23.8 15.8 %collective-permute-start.5 = (bf16[2,40,768]{2,1,0:T(8,128)(2,1)S(1)}, bf16[2,40,768]{2,1,0:T(8,128)(2,1)S(1)}, u32[]{:S(2)}, u32[]{:S(2)}) collective-permute-start(bf16[2,40,768]{2,1,0:T(8,128)(2,1)S(1)} %get-tuple-element.19), channel_id=1, source_target_pairs={{0,8},{1,11},{2,10},{3,9},{4,12},{5,15},{6,14},{7,13},{8,0},{9,3},... | collective-permute-start | bytes 368648 | tf_op jit(solution)/shard_map/ppermute | solution.py:343
  25.6 20.4 %collective-permute-start.11 = (bf16[2,40,2048]{2,1,0:T(8,128)(2,1)S(1)}, bf16[2,40,2048]{2,1,0:T(8,128)(2,1)S(1)}, u32[]{:S(2)}, u32[]{:S(2)}) collective-permute-start(bf16[2,40,2048]{2,1,0:T(8,128)(2,1)S(1)} %get-tuple-element.24), channel_id=1, source_target_pairs={{0,8},{1,11},{2,10},{3,9},{4,12},{5,15},{6,14},{7,13},{8,0},{9,3},... | collective-permute-start | bytes 983048 | tf_op jit(solution)/shard_map/ppermute | solution.py:343
  26.8 19.1 %collective-permute-start.9 = (bf16[2,40,2048]{2,1,0:T(8,128)(2,1)S(1)}, bf16[2,40,2048]{2,1,0:T(8,128)(2,1)S(1)}, u32[]{:S(2)}, u32[]{:S(2)}) collective-permute-start(bf16[2,40,2048]{2,1,0:T(8,128)(2,1)S(1)} %get-tuple-element.26), channel_id=1, source_target_pairs={{0,2},{1,3},{2,0},{3,1},{4,6},{5,7},{6,4},{7,5},{8,10},{9,11},{10,... | collective-permute-start | bytes 983048 | tf_op jit(solution)/shard_map/ppermute | solution.py:343
  28.3 11.3 %collective-permute-start.4 = (bf16[2,40,768]{2,1,0:T(8,128)(2,1)S(1)}, bf16[2,40,768]{2,1,0:T(8,128)(2,1)S(1)}, u32[]{:S(2)}, u32[]{:S(2)}) collective-permute-start(bf16[2,40,768]{2,1,0:T(8,128)(2,1)S(1)} %get-tuple-element.28), channel_id=1, source_target_pairs={{0,2},{1,3},{2,0},{3,1},{4,6},{5,7},{6,4},{7,5},{8,10},{9,11},{10,... | collective-permute-start | bytes 368648 | tf_op jit(solution)/shard_map/ppermute | solution.py:343
  39.6 1.3 %collective-permute-start.3 = (bf16[2,40,768]{2,1,0:T(8,128)(2,1)S(1)}, bf16[2,40,768]{2,1,0:T(8,128)(2,1)S(1)}, u32[]{:S(2)}, u32[]{:S(2)}) collective-permute-start(bf16[2,40,768]{2,1,0:T(8,128)(2,1)S(1)} %get-tuple-element.29), channel_id=1, source_target_pairs={{0,1},{1,0},{2,3},{3,2},{4,5},{5,4},{6,7},{7,6},{8,9},{9,8},{10,11... | collective-permute-start | bytes 368648 | tf_op jit(solution)/shard_map/ppermute | solution.py:343
  39.6 1.5 %collective-permute-start.7 = (bf16[2,40,768]{2,1,0:T(8,128)(2,1)S(1)}, bf16[2,40,768]{2,1,0:T(8,128)(2,1)S(1)}, u32[]{:S(2)}, u32[]{:S(2)}) collective-permute-start(bf16[2,40,768]{2,1,0:T(8,128)(2,1)S(1)} %collective-permute-done.5.refs_7_), channel_id=1, source_target_pairs={{0,1},{1,0},{2,3},{3,2},{4,5},{5,4},{6,7},{7,6},{8,9},{9,8},{10,11... | collective-permute-start | bytes 368648 | tf_op jit(solution)/shard_map/ppermute | solution.py:343
  40.1 1.3 %collective-permute-start.6 = (bf16[2,40,768]{2,1,0:T(8,128)(2,1)S(1)}, bf16[2,40,768]{2,1,0:T(8,128)(2,1)S(1)}, u32[]{:S(2)}, u32[]{:S(2)}) collective-permute-start(bf16[2,40,768]{2,1,0:T(8,128)(2,1)S(1)} %collective-permute-done.4.refs_5_), channel_id=1, source_target_pairs={{0,1},{1,0},{2,3},{3,2},{4,5},{5,4},{6,7},{7,6},{8,9},{9,8},{10,11... | collective-permute-start | bytes 368648 | tf_op jit(solution)/shard_map/ppermute | solution.py:343
  40.9 5.5 %collective-permute-start.8 = (bf16[2,40,2048]{2,1,0:T(8,128)(2,1)S(1)}, bf16[2,40,2048]{2,1,0:T(8,128)(2,1)S(1)}, u32[]{:S(2)}, u32[]{:S(2)}) collective-permute-start(bf16[2,40,2048]{2,1,0:T(8,128)(2,1)S(1)} %get-tuple-element.27), channel_id=1, source_target_pairs={{0,1},{1,0},{2,3},{3,2},{4,5},{5,4},{6,7},{7,6},{8,9},{9,8},{10,11... | collective-permute-start | bytes 983048 | tf_op jit(solution)/shard_map/ppermute | solution.py:343
  46.0 1.6 %collective-permute-start.10 = (bf16[2,40,2048]{2,1,0:T(8,128)(2,1)S(1)}, bf16[2,40,2048]{2,1,0:T(8,128)(2,1)S(1)}, u32[]{:S(2)}, u32[]{:S(2)}) collective-permute-start(bf16[2,40,2048]{2,1,0:T(8,128)(2,1)S(1)} %collective-permute-done.9.refs_6_), channel_id=1, source_target_pairs={{0,1},{1,0},{2,3},{3,2},{4,5},{5,4},{6,7},{7,6},{8,9},{9,8},{10,11... | collective-permute-start | bytes 983048 | tf_op jit(solution)/shard_map/ppermute | solution.py:343
  46.0 2.1 %collective-permute-start.12 = (bf16[2,40,2048]{2,1,0:T(8,128)(2,1)S(1)}, bf16[2,40,2048]{2,1,0:T(8,128)(2,1)S(1)}, u32[]{:S(2)}, u32[]{:S(2)}) collective-permute-start(bf16[2,40,2048]{2,1,0:T(8,128)(2,1)S(1)} %collective-permute-done.11.refs_8_), channel_id=1, source_target_pairs={{0,1},{1,0},{2,3},{3,2},{4,5},{5,4},{6,7},{7,6},{8,9},{9,8},{10,11... | collective-permute-start | bytes 983048 | tf_op jit(solution)/shard_map/ppermute | solution.py:343

commit v4 on v3

--- a/solution.py
+++ b/solution.py
@@ -102,6 +102,34 @@
     return slots
 
 
+FIRST_HOP = (2, 0, 3, 1)
+SECOND_HOP = (1, 0, 3, 2)
+ACROSS = (None, 2, 1, None)
+OUTWARD = (None, 3, 0, None)
+
+
+def first_slots():
+    slots = slot_table()
+    found = np.zeros((N_Z, N_X, 4), np.int32)
+    found[:, :, :3] = slots
+    for x in range(N_X):
+        assert slots[1, x, 0] == slots[1, x, 2]
+        found[1, x, 0] = slots[0, x, 0]
+        found[1, x, 3] = slots[0, x, 2]
+    return found.reshape(N_Z * N_X, 4)
+
+
+def relay_slots():
+    slots, first = slot_table(), first_slots().reshape(N_Z, N_X, 4)
+    found = np.zeros((N_Z, N_X, 3), np.int32)
+    for z in (1, 2):
+        for x in range(N_X):
+            held = [int(b) for b in first[z, x]]
+            for row in range(3):
+                found[z, x, row] = held.index(int(slots[SECOND_HOP[z], x, row]))
+    return found.reshape(N_Z * N_X, 3)
+
+
 def lookup(values, index):
     found = jnp.int32(int(values[0]))
     for i in range(1, len(values)):
@@ -118,14 +146,15 @@
     return lookup(slot_table().reshape(-1, 3)[:, row], plane * N_X + column)
 
 
-def pack_kernel(far_routes, grads, inputs, p1_ref, p2_ref, p2_i_ref, x0_ref, own_ref, *scratch):
-    routes_ref, held, held_i, packed, sems = scratch
+def pack_kernel(far_routes, grads, inputs, *refs):
+    first_ref, second_ref, across_ref, out_ref, x0_ref, own_ref = refs[:6]
+    routes_ref, held, held_i, packed, sems = refs[6:]
     plane, column, core = place()
     capacity, total = x0_ref.shape
     width = held.shape[2]
-    sources = [(grads, held, 0), (inputs, held_i, width)]
+    sources = [(grads, held), (inputs, held_i)]
     copies = []
-    for n, (source, buffer, _) in enumerate(sources):
+    for n, (source, buffer) in enumerate(sources):
         size = buffer.shape[2]
         for block in range(4):
             copies.append(
@@ -158,30 +187,40 @@
         lax.broadcasted_iota(jnp.int32, (capacity, 128), 1) == 0
     )
     picker = picker.astype(BF16)
-    for n, (_, buffer, low) in enumerate(sources):
+    for n, (_, buffer) in enumerate(sources):
         for block in range(4):
             copies[4 * n + block].wait()
             got = jnp.dot(picker, buffer[block], preferred_element_type=jnp.float32)
-            if n == 1:
+            if n == 0:
                 head = jnp.where(empty, jnp.inf, got[:, :128])
-                packed[block, :, low : low + 128] = head.astype(BF16)
-                packed[block, :, low + 128 :] = got[:, 128:].astype(BF16)
+                packed[block, :, :128] = head.astype(BF16)
+                packed[block, :, 128:width] = got[:, 128:].astype(BF16)
             else:
-                packed[block, :, :width] = got.astype(BF16)
-    to_plane = lax.rem(plane + jnp.where(core == 0, 1, 3), N_Z)
+                packed[block, :, width:] = got.astype(BF16)
+    bounds = (0, width, total)
+
+    def put_half(ref, row, block):
+        for low, high in zip(bounds[:-1], bounds[1:]):
+            half = (high - low) // 2
+            start = pl.multiple_of(low + core * half, 128)
+            ref[row, :, low // 2 : high // 2] = packed[block, :, pl.ds(start, half)]
+
+    firsts = first_slots()
+    to_plane = lookup(FIRST_HOP, plane)
+    for row in range(4):
+        put_half(first_ref, row, lookup(firsts[:, row], to_plane * N_X + column))
+    to_plane = lookup(SECOND_HOP, plane)
     for row in range(3):
-        p1_ref[row] = packed[block_at(to_plane, column, row)]
+        put_half(second_ref, row, block_at(to_plane, column, row))
     x0_block = jnp.where(
         core == 0, block_at(plane, 1 - column, 1), block_at(plane, 1 - column, 0)
     )
     x0_ref[...] = packed[x0_block]
-    to_plane = lax.rem(plane + 2, N_Z)
     to_column = jnp.where(core == 0, column, 1 - column)
     for row in range(2):
-        block = block_at(to_plane, to_column, row)
-        p2_ref[row] = packed[block, :, :width]
-        p2_i_ref[row] = packed[block, :, width:]
         own_ref[row] = packed[block_at(plane, column, row)]
+        across_ref[row] = packed[block_at(lookup((0, 2, 1, 0), plane), to_column, row)]
+        out_ref[row] = packed[block_at(lookup((0, 3, 0, 0), plane), to_column, row)]
 
 
 BF16 = jnp.bfloat16
@@ -191,8 +230,8 @@
     tokens = routes_t.shape[1]
     width, width_i = grads.shape[1] // 4, inputs.shape[1] // 4
     total = width + width_i
-    shapes = [(3, capacity, total), (2, capacity, width), (2, capacity, width_i)]
-    shapes += [(capacity, total), (2, capacity, total)]
+    shapes = [(4, capacity, total // 2), (3, capacity, total // 2), (2, capacity, total)]
+    shapes += [(2, capacity, total), (capacity, total), (2, capacity, total)]
     operands = [pltpu.with_memory_space_constraint(a, pltpu.HBM) for a in (routes_t, grads, inputs)]
     return pl.pallas_call(
         pack_kernel,
@@ -215,21 +254,57 @@
     )(*operands)
 
 
+def relay_kernel(got, own, keep_ref, forward_ref, second_ref):
+    plane, column, core = place()
+    chip = plane * N_X + column
+    table = relay_slots()
+    inner = (plane == 1) | (plane == 2)
+    keep_ref[0] = got[jnp.where(plane == 1, 2, 0)]
+    keep_ref[1] = got[1]
+    forward_ref[...] = got[1:3]
+    for row in range(3):
+        second_ref[row] = jnp.where(inner, got[lookup(table[:, row], chip)], own[row])
+
+
+def relay(got, own):
+    _, capacity, half = got.shape
+    return pl.pallas_call(
+        relay_kernel,
+        out_shape=[jax.ShapeDtypeStruct((n, capacity, half), BF16) for n in (2, 2, 3)],
+        in_specs=[VMEM] * 2,
+        out_specs=[VMEM] * 3,
+        compiler_params=pltpu.CompilerParams(vmem_limit_bytes=4 * 2**20),
+        cost_estimate=cost(1, 1),
+    )(got, own)
+
+
 def assemble(data, pieces, start):
-    own, x0, hx0, p1, hp1, x1, hx1, p2, hp2 = pieces
-    core = lax.axis_index("hid")
+    own, x0, hx0, across, far_across, *halves, out, far_out = pieces
+    plane, column, core = place()
+    inner = (plane == 1) | (plane == 2)
     capacity = own.shape[1]
     size = data.shape[2]
     span = pl.ds(start, size)
+    half = size // 2
+    half_span = pl.ds(start // 2, half)
+    mine = pl.ds(pl.multiple_of(core * half, 128), half)
+    far = pl.ds(pl.multiple_of((1 - core) * half, 128), half)
     for block in range(2):
-        whole = [own.at[block], p1.at[block]]
-        whole = [ref[:, span] for ref in whole]
+        whole = [own[block, :, span]]
         whole.append(jnp.where((core == 0) == (block == 1), x0[:, span], hx0[:, span]))
-        whole += [hp1[block], x1[1 - block], hx1[1 - block], p2[block], hp2[block]]
-        for slot, piece in enumerate(whole):
+        whole.append(jnp.where(inner, across[block, :, span], out[block, :, span]))
+        whole.append(jnp.where(inner, far_across[block, :, span], far_out[block, :, span]))
+        for slot in range(SLOTS):
             low = slot * SLOT_ROWS
             data[block, low + 32 : low + SLOT_ROWS, :] = jnp.zeros((SLOT_ROWS - 32, size), BF16)
-            data[block, low : low + capacity, :] = piece
+            if slot < len(whole):
+                data[block, low : low + capacity, :] = whole[slot]
+            else:
+                n = 2 * (slot - len(whole))
+                row = block if n < 4 else 1 - block
+                rows = pl.ds(low, capacity)
+                data[block, rows, mine] = halves[n][row, :, half_span]
+                data[block, rows, far] = halves[n + 1][row, :, half_span]
 
 
 def clear_marks(data, capacity, slots):
@@ -259,80 +334,85 @@
     )
 
 
-def multiply(scale, data, out_ref, stage, sems, start):
+def cost(rows, width):
+    return pl.CostEstimate(flops=0, bytes_accessed=0, transcendentals=0)
+
+
+def tiles_kernel(*refs):
+    pieces = refs[:15]
+    out_i, out, data, data_i, stage, stage_i, sems = refs[15:]
     left, right = sides()
-    steps = sems.shape[0]
-    size = stage.shape[0] // steps
+    width = data.shape[2]
     copies = []
-    for i in range(steps):
-        rows = pl.ds(i * size, size)
-        to = pl.ds(start + i * size, size)
-        stage[rows, :] = product(scale, data[left, :, to], data[right])
-        copies.append(pltpu.make_async_copy(stage.at[rows], out_ref.at[0, to], sems.at[i]))
+
+    def write(source, target):
+        copies.append(pltpu.make_async_copy(source, target, sems.at[len(copies)]))
         copies[-1].start()
+
+    def multiply(data, stage, out, steps):
+        size = data.shape[2] // steps
+        for i in range(steps):
+            rows = pl.ds(i * size, size)
+            stage[rows, :] = product(scale, data[left, :, rows], data[right])
+            write(stage.at[rows], out.at[0, rows])
+
+    assemble(data, pieces, 0)
+    scale = clear_marks(data, pieces[0].shape[1], SLOTS)
+    multiply(data, stage, out, 8)
+    assemble(data_i, pieces, width)
+    multiply(data_i, stage_i, out_i, 3)
     for copy in copies:
         copy.wait()
 
 
-def cost(rows, width):
-    return pl.CostEstimate(
-        flops=2 * SLOTS * SLOT_ROWS * rows * width,
-        bytes_accessed=4 * rows * width,
-        transcendentals=0,
-    )
-
-
-def tile_kernel(marked, *refs):
-    refs = list(refs)
-    scale_in = None if marked else refs.pop(0)
-    data, stage, sems = refs[-3:]
-    pieces = refs[:9]
-    out_ref = refs[9]
-    assemble(data, pieces, pieces[0].shape[2] - data.shape[2] if marked else 0)
-    if marked:
-        scale = clear_marks(data, pieces[0].shape[1], SLOTS)
-        refs[10][0] = scale
-    else:
-        scale = scale_in[0]
-    multiply(scale, data, out_ref, stage, sems, 0)
-
-
-def tile(scale, pieces, steps, limit):
-    marked = scale is None
-    width = pieces[-1].shape[2]
-    out_shape = [jax.ShapeDtypeStruct((1, width, width), jnp.float32)]
-    if marked:
-        out_shape.append(jax.ShapeDtypeStruct((1,), jnp.float32))
+def tiles(width, pieces):
+    width_i = pieces[0].shape[2] - width
     return pl.pallas_call(
-        functools.partial(tile_kernel, marked),
-        out_shape=out_shape,
-        in_specs=([] if marked else [SMEM]) + [VMEM] * len(pieces),
-        out_specs=[ANY, SMEM] if marked else [ANY],
-        scratch_shapes=[
-            pltpu.VMEM((2, SLOTS * SLOT_ROWS, width), BF16),
-            pltpu.VMEM((width, width), jnp.float32),
-            pltpu.SemaphoreType.DMA((steps,)),
-        ],
-        compiler_params=pltpu.CompilerParams(vmem_limit_bytes=limit),
+        tiles_kernel,
+        out_shape=[jax.ShapeDtypeStruct((1, w, w), jnp.float32) for w in (width_i, width)],
+        in_specs=[VMEM] * len(pieces),
+        out_specs=[ANY, ANY],
+        scratch_shapes=[pltpu.VMEM((2, SLOTS * SLOT_ROWS, w), BF16) for w in (width, width_i)]
+        + [pltpu.VMEM((w, w), jnp.float32) for w in (width, width_i)]
+        + [pltpu.SemaphoreType.DMA((11,))],
+        compiler_params=pltpu.CompilerParams(vmem_limit_bytes=32 * 2**20),
         cost_estimate=cost(width, width),
-    )(*([] if marked else [scale]), *pieces)
-
-
-def moves(step):
+    )(*pieces)
+
+
+def moves(step, turn=lambda x, core: (x, core)):
     pairs = []
     for z in range(N_Z):
         for x in range(N_X):
             for core in range(2):
-                to_z, to_x, to_core = step(z, x, core)
-                source = (z * N_X + x) * 2 + core
-                pairs.append((source, (to_z % N_Z * N_X + to_x) * 2 + to_core))
+                if step[z] is not None:
+                    to_x, to_core = turn(x, core)
+                    source = (z * N_X + x) * 2 + core
+                    pairs.append((source, (step[z] * N_X + to_x) * 2 + to_core))
     return pairs
 
 
-ALONG_Z = moves(lambda z, x, core: (z + (1, 3)[core], x, core))
-ACROSS_Z = moves(lambda z, x, core: (z + 2, (x, 1 - x)[core], core))
-ALONG_X = moves(lambda z, x, core: (z, 1 - x, core))
-CORES = moves(lambda z, x, core: (z, x, 1 - core))
+def to_both_columns(x, core):
+    return (x, 1 - x)[core], core
+
+
+def to_neighbour(x, core):
+    return 1 - x, core
+
+
+def to_other_core(x, core):
+    return x, 1 - core
+
+
+STAY = (0, 1, 2, 3)
+FIRST = moves(FIRST_HOP)
+SECOND = moves(SECOND_HOP)
+MIDDLE = moves(ACROSS, to_both_columns)
+ENDS = moves(OUTWARD, to_both_columns)
+ALONG_X = moves(STAY, to_neighbour)
+CORES = moves(STAY, to_other_core)
+INNER_CORES = moves((None, 1, 2, None), to_other_core)
+OUTER_CORES = moves((0, None, None, 3), to_other_core)
 
 
 def after(array, *done):
@@ -343,29 +423,30 @@
     return lax.ppermute(array, ("tok", "hid"), pairs)
 
 
-def both(array):
-    return [array, send(array, CORES)]
-
-
 def shards_eight(inputs, hidden_grads, routes):
     capacity = routes.shape[0] * 5 // 16
-    width = hidden_grads.shape[1] // 4
-    p1, p2, p2_i, x0, own = pack(routes.T, hidden_grads, inputs, capacity)
-    p1 = send(p1, ALONG_Z)
+    first, second, across, out, x0, own = pack(routes.T, hidden_grads, inputs, capacity)
+    first = send(first, FIRST)
     x0 = send(x0, ALONG_X)
     hx0 = send(x0, CORES)
-    p1 = after(p1, x0)
-    p2_i = send(after(p2_i, p1), ACROSS_Z)
-    p2 = send(after(p2, p1), ACROSS_Z)
-    x1_i = send(p1[1:, :, width:], ALONG_X)
-    x1 = send(p1[1:, :, :width], ALONG_X)
-    x1_i = after(x1_i, p2_i)
-    hp1_i = send(p1[:2, :, width:], CORES)
-    hp1 = send(p1[:2, :, :width], CORES)
-    base = [own, x0, hx0, p1]
-    input_tile, scale = tile(None, base + [hp1_i, *both(x1_i), *both(p2_i)], 3, 12 * 2**20)
-    p2 = after(p2, scale)
-    (grad_tile,) = tile(scale, base + [hp1, *both(x1), *both(p2)], 8, 28 * 2**20)
+    first = after(first, x0)
+    keep, forward, second = relay(first, second)
+    second = send(second, SECOND)
+    across = send(after(across, x0), MIDDLE)
+    out = send(after(out, keep), ENDS)
+    x1 = send(forward, ALONG_X)
+    far_keep = send(keep, CORES)
+    second = after(second, far_keep, hx0, across)
+    far_x1 = send(x1, CORES)
+    x2 = send(second[1:], ALONG_X)
+    far_second = send(second[:2], CORES)
+    far_across = send(across, INNER_CORES)
+    far_x2 = send(x2, CORES)
+    out = after(out, far_x1, far_second, far_across, far_x2)
+    far_out = send(out, OUTER_CORES)
+    pieces = [own, x0, hx0, across, far_across, keep, far_keep, second, far_second]
+    pieces += [x1, far_x1, x2, far_x2, out, far_out]
+    input_tile, grad_tile = tiles(hidden_grads.shape[1] // 4, pieces)
     return input_tile, grad_tile
 
 

time: 55.8 us -> 50.5 us (0.905)
  waiting for transfers between devices: 30.5 us -> 21.5 us
  starting transfers between devices: 11.6 us -> 16.9 us
  Pallas kernels: 12.8 us -> 11.2 us
    ppermute x13 -> x14, waiting for transfers between devices: 30.5 us -> 21.5 us  [send(): return lax.ppermute(array, ('tok', 'hid'), pairs)]
    ppermute x13 -> x14, starting transfers between devices: 11.6 us -> 16.9 us  [send(): return lax.ppermute(array, ('tok', 'hid'), pairs)]
    pallas_call x2, Pallas kernels: 10.1 us -> 8.4 us  [the longest x1 8.34 us: tiles(): pl.pallas_call(tiles_kernel, out_shape=[jax.ShapeDtypeStruct((1, w, w), j...]
  transfers between devices with their start and end apart: 13 -> 14, of which waited for: 8 -> 6; matrix products, arithmetic and copies ran while one was open for 0% -> 0% of each run, Pallas kernels for 5% -> 0%
where the time goes in v4:
time: 50.5 us; the launch traced here: 50.3 us
  waiting for transfers between devices  21.5 us (43%)
  starting transfers between devices  16.9 us (33%)
  Pallas kernels  11.2 us (22%)
  between operations  0.71 us (1%)
    ppermute x14, waiting for transfers between devices, send(): return lax.ppermute(array, ('tok', 'hid'), pairs)  21.5 us
    ppermute x14, starting transfers between devices, send(): return lax.ppermute(array, ('tok', 'hid'), pairs)  16.9 us
    pallas_call x1, Pallas kernels, tiles(): pl.pallas_call(tiles_kernel, out_shape=[jax.ShapeDtypeStruct((1, w, w), j...  8.34 us
    pallas_call x1, Pallas kernels, pack(): pl.pallas_call(pack_kernel, out_shape=[jax.ShapeDtypeStruct(s, BF16) for...  2.76 us
  transfers between devices with their start and end apart: 14, of which 6 were waited for; matrix products, arithmetic and copies ran while one was open for 0% of the time, Pallas kernels for 0%

profile of v4, /device:TPU:0, one launch (start us, length us, event | category | flops | bytes accessed | tf_op | source)
XLA Modules:
  0.0 50.3 jit_solution(16985978986338846439)
XLA Ops:
  0.6 2.8 %shard_map.50 = (bf16[4,40,1408]{2,1,0:T(8,128)(2,1)S(1)}, bf16[3,40,1408]{2,1,0:T(8,128)(2,1)S(1)}, bf16[2,40,2816]{2,1,0:T(8,128)(2,1)S(1)}, bf16[2,40,2816]{2...) custom-call(s32[2,128]{1,0:T(2,128)} %bitcast.1, bf16[128,8192]{1,0:T(8,128)(2,1)} %grads.1, ...), custom_call_target="tpu_custom_call" | custom-call | flops 115343360 | bytes 2883584 | tf_op jit(solution)/shard_map/pallas_call | solution.py:236
  3.4 4.1 %collective-permute-start.4 = (bf16[4,40,1408]{2,1,0:T(8,128)(2,1)S(1)}, bf16[4,40,1408]{2,1,0:T(8,128)(2,1)S(1)}, u32[]{:S(2)}, u32[]{:S(2)}) collective-permute-start(bf16[4,40,1408]{2,1,0:T(8,128)(2,1)S(1)} %get-tuple-element.20), channel_id=1, source_target_pairs={{0,8},{1,9},{2,10},{3,11},{4,0},{5,1},{6,2},{7,3},{8,12},{9,13},{1... | collective-permute-start | bytes 1351688 | tf_op jit(solution)/shard_map/ppermute | solution.py:423
  7.5 1.5 %collective-permute-start = (bf16[40,2816]{1,0:T(8,128)(2,1)S(1)}, bf16[40,2816]{1,0:T(8,128)(2,1)S(1)}, u32[]{:S(2)}, u32[]{:S(2)}) collective-permute-start(bf16[40,2816]{1,0:T(8,128)(2,1)S(1)} %get-tuple-element.17), channel_id=1, source_target_pairs={{0,2},{1,3},{2,0},{3,1},{4,6},{5,7},{6,4},{7,5},{8,10},{9,11},{10,... | collective-permute-start | bytes 675848 | tf_op jit(solution)/shard_map/ppermute | solution.py:423
  9.0 5.5 %collective-permute-done.refs_1_ = bf16[40,2816]{1,0:T(8,128)(2,1)S(1)} collective-permute-done((bf16[40,2816]{1,0:T(8,128)(2,1)S(1)}, bf16[40,2816]{1,0:T(8,128)(2,1)S(1)}, u32[]{:S(2)}, u32[]{:S(2)}) %collective-permute-start) | collective-permute-done | bytes 225312 | tf_op jit(solution)/shard_map/ppermute | solution.py:423
  14.5 0.7 %collective-permute-start.2 = (bf16[2,40,2816]{2,1,0:T(8,128)(2,1)S(1)}, bf16[2,40,2816]{2,1,0:T(8,128)(2,1)S(1)}, u32[]{:S(2)}, u32[]{:S(2)}) collective-permute-start(bf16[2,40,2816]{2,1,0:T(8,128)(2,1)S(1)} %get-tuple-element.19), channel_id=1, source_target_pairs={{4,8},{5,11},{6,10},{7,9},{8,4},{9,7},{10,6},{11,5},{20,24},{21,27... | collective-permute-start | bytes 1351688 | tf_op jit(solution)/shard_map/ppermute | solution.py:423
  15.2 1.9 %collective-permute-done.4.got = bf16[4,40,1408]{2,1,0:T(8,128)(2,1)S(1)} collective-permute-done((bf16[4,40,1408]{2,1,0:T(8,128)(2,1)S(1)}, bf16[4,40,1408]{2,1,0:T(8,128)(2,1)S(1)}, u32[]{:S(2)}, u32[]{:S(2)}) %collective-permute-start.4) | collective-permute-done | bytes 450592 | tf_op jit(solution)/shard_map/ppermute | solution.py:423
  17.1 0.1 shard_map.51
  17.2 2.5 %collective-permute-start.6 = (bf16[3,40,1408]{2,1,0:T(8,128)(2,1)S(1)}, bf16[3,40,1408]{2,1,0:T(8,128)(2,1)S(1)}, u32[]{:S(2)}, u32[]{:S(2)}) collective-permute-start(bf16[3,40,1408]{2,1,0:T(8,128)(2,1)S(1)} %get-tuple-element.24), channel_id=1, source_target_pairs={{0,4},{1,5},{2,6},{3,7},{4,0},{5,1},{6,2},{7,3},{8,12},{9,13},{10,... | collective-permute-start | bytes 1013768 | tf_op jit(solution)/shard_map/ppermute | solution.py:423
  19.7 0.5 %collective-permute-start.5 = (bf16[2,40,1408]{2,1,0:T(8,128)(2,1)S(1)}, bf16[2,40,1408]{2,1,0:T(8,128)(2,1)S(1)}, u32[]{:S(2)}, u32[]{:S(2)}) collective-permute-start(bf16[2,40,1408]{2,1,0:T(8,128)(2,1)S(1)} %get-tuple-element.23.refs_5_), channel_id=1, source_target_pairs={{0,1},{1,0},{2,3},{3,2},{4,5},{5,4},{6,7},{7,6},{8,9},{9,8},{10,11... | collective-permute-start | bytes 675848 | tf_op jit(solution)/shard_map/ppermute | solution.py:423
  20.2 1.5 %collective-permute-start.8 = (bf16[2,40,1408]{2,1,0:T(8,128)(2,1)S(1)}, bf16[2,40,1408]{2,1,0:T(8,128)(2,1)S(1)}, u32[]{:S(2)}, u32[]{:S(2)}) collective-permute-start(bf16[2,40,1408]{2,1,0:T(8,128)(2,1)S(1)} %get-tuple-element.26), channel_id=1, source_target_pairs={{0,2},{1,3},{2,0},{3,1},{4,6},{5,7},{6,4},{7,5},{8,10},{9,11},{10,... | collective-permute-start | bytes 675848 | tf_op jit(solution)/shard_map/ppermute | solution.py:423
  21.7 0.0 collective-permute-done.1.refs_2_
  21.7 1.3 %collective-permute-start.12 = (bf16[2,40,2816]{2,1,0:T(8,128)(2,1)S(1)}, bf16[2,40,2816]{2,1,0:T(8,128)(2,1)S(1)}, u32[]{:S(2)}, u32[]{:S(2)}) collective-permute-start(bf16[2,40,2816]{2,1,0:T(8,128)(2,1)S(1)} %get-tuple-element.28), channel_id=1, source_target_pairs={{4,12},{5,15},{6,14},{7,13},{8,0},{9,3},{10,2},{11,1},{20,28},{21,... | collective-permute-start | bytes 1351688 | tf_op jit(solution)/shard_map/ppermute | solution.py:423
  23.0 0.0 collective-permute-done.2.refs_3_
  23.0 0.7 %collective-permute-start.3 = (bf16[2,40,2816]{2,1,0:T(8,128)(2,1)S(1)}, bf16[2,40,2816]{2,1,0:T(8,128)(2,1)S(1)}, u32[]{:S(2)}, u32[]{:S(2)}) collective-permute-start(bf16[2,40,2816]{2,1,0:T(8,128)(2,1)S(1)} %collective-permute-done.2.refs_3_), channel_id=1, source_target_pairs={{4,5},{5,4},{6,7},{7,6},{8,9},{9,8},{10,11},{11,10},{20,21},{21,20... | collective-permute-start | bytes 1351688 | tf_op jit(solution)/shard_map/ppermute | solution.py:423
  23.7 0.0 collective-permute-done.5.refs_6_
  23.7 2.9 %collective-permute-done.6.refs_7_ = bf16[3,40,1408]{2,1,0:T(8,128)(2,1)S(1)} collective-permute-done((bf16[3,40,1408]{2,1,0:T(8,128)(2,1)S(1)}, bf16[3,40,1408]{2,1,0:T(8,128)(2,1)S(1)}, u32[]{:S(2)}, u32[]{:S(2)}) %collective-permute-start.6) | collective-permute-done | bytes 337952 | tf_op jit(solution)/shard_map/ppermute | solution.py:423
  26.7 1.6 %collective-permute-start.10 = (bf16[2,40,1408]{2,1,0:T(8,128)(2,1)S(1)}, bf16[2,40,1408]{2,1,0:T(8,128)(2,1)S(1)}, u32[]{:S(2)}, u32[]{:S(2)}) collective-permute-start(bf16[2,40,1408]{2,1,0:T(8,128)(2,1)S(1)} %get-tuple-element.30), channel_id=1, source_target_pairs={{0,2},{1,3},{2,0},{3,1},{4,6},{5,7},{6,4},{7,5},{8,10},{9,11},{10,... | collective-permute-start | bytes 675848 | tf_op jit(solution)/shard_map/ppermute | solution.py:423
  28.3 0.0 collective-permute-start.9
  28.3 0.5 %collective-permute-start.7 = (bf16[2,40,1408]{2,1,0:T(8,128)(2,1)S(1)}, bf16[2,40,1408]{2,1,0:T(8,128)(2,1)S(1)}, u32[]{:S(2)}, u32[]{:S(2)}) collective-permute-start(bf16[2,40,1408]{2,1,0:T(8,128)(2,1)S(1)} %get-tuple-element.31), channel_id=1, source_target_pairs={{0,1},{1,0},{2,3},{3,2},{4,5},{5,4},{6,7},{7,6},{8,9},{9,8},{10,11... | collective-permute-start | bytes 675848 | tf_op jit(solution)/shard_map/ppermute | solution.py:423
  28.8 7.3 %collective-permute-done.10.refs_11_ = bf16[2,40,1408]{2,1,0:T(8,128)(2,1)S(1)} collective-permute-done((bf16[2,40,1408]{2,1,0:T(8,128)(2,1)S(1)}, bf16[2,40,1408]{2,1,0:T(8,128)(2,1)S(1)}, u32[]{:S(2)}, u32[]{:S(2)}) %collective-permute-start.10) | collective-permute-done | bytes 225312 | tf_op jit(solution)/shard_map/ppermute | solution.py:423
  36.1 2.1 %collective-permute-done.12.refs_13_ = bf16[2,40,2816]{2,1,0:T(8,128)(2,1)S(1)} collective-permute-done((bf16[2,40,2816]{2,1,0:T(8,128)(2,1)S(1)}, bf16[2,40,2816]{2,1,0:T(8,128)(2,1)S(1)}, u32[]{:S(2)}, u32[]{:S(2)}) %collective-permute-start.12) | collective-permute-done | bytes 450592 | tf_op jit(solution)/shard_map/ppermute | solution.py:423
  38.2 2.0 %collective-permute-start.13 = (bf16[2,40,2816]{2,1,0:T(8,128)(2,1)S(1)}, bf16[2,40,2816]{2,1,0:T(8,128)(2,1)S(1)}, u32[]{:S(2)}, u32[]{:S(2)}) collective-permute-start(bf16[2,40,2816]{2,1,0:T(8,128)(2,1)S(1)} %collective-permute-done.12.refs_13_), channel_id=1, source_target_pairs={{0,1},{1,0},{2,3},{3,2},{12,13},{13,12},{14,15},{15,14},{16,17},{1... | collective-permute-start | bytes 1351688 | tf_op jit(solution)/shard_map/ppermute | solution.py:423
  40.2 1.7 %collective-permute-done.13.refs_14_ = bf16[2,40,2816]{2,1,0:T(8,128)(2,1)S(1)} collective-permute-done((bf16[2,40,2816]{2,1,0:T(8,128)(2,1)S(1)}, bf16[2,40,2816]{2,1,0:T(8,128)(2,1)S(1)}, u32[]{:S(2)}, u32[]{:S(2)}) %collective-permute-start.13) | collective-permute-done | bytes 450592 | tf_op jit(solution)/shard_map/ppermute | solution.py:423
  41.9 8.3 %shard_map.52 = (f32[1,768,768]{2,1,0:T(8,128)}, f32[1,2048,2048]{2,1,0:T(8,128)}) custom-call(bf16[2,40,2816]{2,1,0:T(8,128)(2,1)S(1)} %get-tuple-element.16.refs_0_, bf16[40,2816]{1,0:T(8,128)(2,1)S(1)} %collective-permute-done.refs_1_, bf16[40,2816]{1,0:T(8,128)(2,1)S(1)} %collective-permute-done.1.refs_2_, ...), custom_call_target="tpu_custom_call" | custom-call | tf_op jit(solution)/shard_map/pallas_call | solution.py:370
  (8 shorter events, 0.1 us)
Async XLA Ops:
  3.4 13.7 %collective-permute-start.4 = (bf16[4,40,1408]{2,1,0:T(8,128)(2,1)S(1)}, bf16[4,40,1408]{2,1,0:T(8,128)(2,1)S(1)}, u32[]{:S(2)}, u32[]{:S(2)}) collective-permute-start(bf16[4,40,1408]{2,1,0:T(8,128)(2,1)S(1)} %get-tuple-element.20), channel_id=1, source_target_pairs={{0,8},{1,9},{2,10},{3,11},{4,0},{5,1},{6,2},{7,3},{8,12},{9,13},{1... | collective-permute-start | bytes 1351688 | tf_op jit(solution)/shard_map/ppermute | solution.py:423
  7.5 7.0 %collective-permute-start = (bf16[40,2816]{1,0:T(8,128)(2,1)S(1)}, bf16[40,2816]{1,0:T(8,128)(2,1)S(1)}, u32[]{:S(2)}, u32[]{:S(2)}) collective-permute-start(bf16[40,2816]{1,0:T(8,128)(2,1)S(1)} %get-tuple-element.17), channel_id=1, source_target_pairs={{0,2},{1,3},{2,0},{3,1},{4,6},{5,7},{6,4},{7,5},{8,10},{9,11},{10,... | collective-permute-start | bytes 675848 | tf_op jit(solution)/shard_map/ppermute | solution.py:423
  14.5 8.5 %collective-permute-start.2 = (bf16[2,40,2816]{2,1,0:T(8,128)(2,1)S(1)}, bf16[2,40,2816]{2,1,0:T(8,128)(2,1)S(1)}, u32[]{:S(2)}, u32[]{:S(2)}) collective-permute-start(bf16[2,40,2816]{2,1,0:T(8,128)(2,1)S(1)} %get-tuple-element.19), channel_id=1, source_target_pairs={{4,8},{5,11},{6,10},{7,9},{8,4},{9,7},{10,6},{11,5},{20,24},{21,27... | collective-permute-start | bytes 1351688 | tf_op jit(solution)/shard_map/ppermute | solution.py:423
  17.2 9.5 %collective-permute-start.6 = (bf16[3,40,1408]{2,1,0:T(8,128)(2,1)S(1)}, bf16[3,40,1408]{2,1,0:T(8,128)(2,1)S(1)}, u32[]{:S(2)}, u32[]{:S(2)}) collective-permute-start(bf16[3,40,1408]{2,1,0:T(8,128)(2,1)S(1)} %get-tuple-element.24), channel_id=1, source_target_pairs={{0,4},{1,5},{2,6},{3,7},{4,0},{5,1},{6,2},{7,3},{8,12},{9,13},{10,... | collective-permute-start | bytes 1013768 | tf_op jit(solution)/shard_map/ppermute | solution.py:423
  19.7 2.0 %collective-permute-start.1 = (bf16[40,2816]{1,0:T(8,128)(2,1)S(1)}, bf16[40,2816]{1,0:T(8,128)(2,1)S(1)}, u32[]{:S(2)}, u32[]{:S(2)}) collective-permute-start(bf16[40,2816]{1,0:T(8,128)(2,1)S(1)} %collective-permute-done.refs_1_), channel_id=1, source_target_pairs={{0,1},{1,0},{2,3},{3,2},{4,5},{5,4},{6,7},{7,6},{8,9},{9,8},{10,11... | collective-permute-start | bytes 675848 | tf_op jit(solution)/shard_map/ppermute | solution.py:423
  19.7 4.0 %collective-permute-start.5 = (bf16[2,40,1408]{2,1,0:T(8,128)(2,1)S(1)}, bf16[2,40,1408]{2,1,0:T(8,128)(2,1)S(1)}, u32[]{:S(2)}, u32[]{:S(2)}) collective-permute-start(bf16[2,40,1408]{2,1,0:T(8,128)(2,1)S(1)} %get-tuple-element.23.refs_5_), channel_id=1, source_target_pairs={{0,1},{1,0},{2,3},{3,2},{4,5},{5,4},{6,7},{7,6},{8,9},{9,8},{10,11... | collective-permute-start | bytes 675848 | tf_op jit(solution)/shard_map/ppermute | solution.py:423
  20.2 8.0 %collective-permute-start.8 = (bf16[2,40,1408]{2,1,0:T(8,128)(2,1)S(1)}, bf16[2,40,1408]{2,1,0:T(8,128)(2,1)S(1)}, u32[]{:S(2)}, u32[]{:S(2)}) collective-permute-start(bf16[2,40,1408]{2,1,0:T(8,128)(2,1)S(1)} %get-tuple-element.26), channel_id=1, source_target_pairs={{0,2},{1,3},{2,0},{3,1},{4,6},{5,7},{6,4},{7,5},{8,10},{9,11},{10,... | collective-permute-start | bytes 675848 | tf_op jit(solution)/shard_map/ppermute | solution.py:423
  21.7 16.5 %collective-permute-start.12 = (bf16[2,40,2816]{2,1,0:T(8,128)(2,1)S(1)}, bf16[2,40,2816]{2,1,0:T(8,128)(2,1)S(1)}, u32[]{:S(2)}, u32[]{:S(2)}) collective-permute-start(bf16[2,40,2816]{2,1,0:T(8,128)(2,1)S(1)} %get-tuple-element.28), channel_id=1, source_target_pairs={{4,12},{5,15},{6,14},{7,13},{8,0},{9,3},{10,2},{11,1},{20,28},{21,... | collective-permute-start | bytes 1351688 | tf_op jit(solution)/shard_map/ppermute | solution.py:423
  23.0 15.2 %collective-permute-start.3 = (bf16[2,40,2816]{2,1,0:T(8,128)(2,1)S(1)}, bf16[2,40,2816]{2,1,0:T(8,128)(2,1)S(1)}, u32[]{:S(2)}, u32[]{:S(2)}) collective-permute-start(bf16[2,40,2816]{2,1,0:T(8,128)(2,1)S(1)} %collective-permute-done.2.refs_3_), channel_id=1, source_target_pairs={{4,5},{5,4},{6,7},{7,6},{8,9},{9,8},{10,11},{11,10},{20,21},{21,20... | collective-permute-start | bytes 1351688 | tf_op jit(solution)/shard_map/ppermute | solution.py:423
  26.7 9.4 %collective-permute-start.10 = (bf16[2,40,1408]{2,1,0:T(8,128)(2,1)S(1)}, bf16[2,40,1408]{2,1,0:T(8,128)(2,1)S(1)}, u32[]{:S(2)}, u32[]{:S(2)}) collective-permute-start(bf16[2,40,1408]{2,1,0:T(8,128)(2,1)S(1)} %get-tuple-element.30), channel_id=1, source_target_pairs={{0,2},{1,3},{2,0},{3,1},{4,6},{5,7},{6,4},{7,5},{8,10},{9,11},{10,... | collective-permute-start | bytes 675848 | tf_op jit(solution)/shard_map/ppermute | solution.py:423
  28.3 7.8 %collective-permute-start.9 = (bf16[2,40,1408]{2,1,0:T(8,128)(2,1)S(1)}, bf16[2,40,1408]{2,1,0:T(8,128)(2,1)S(1)}, u32[]{:S(2)}, u32[]{:S(2)}) collective-permute-start(bf16[2,40,1408]{2,1,0:T(8,128)(2,1)S(1)} %collective-permute-done.8.refs_9_), channel_id=1, source_target_pairs={{0,1},{1,0},{2,3},{3,2},{4,5},{5,4},{6,7},{7,6},{8,9},{9,8},{10,11... | collective-permute-start | bytes 675848 | tf_op jit(solution)/shard_map/ppermute | solution.py:423
  28.3 10.0 %collective-permute-start.7 = (bf16[2,40,1408]{2,1,0:T(8,128)(2,1)S(1)}, bf16[2,40,1408]{2,1,0:T(8,128)(2,1)S(1)}, u32[]{:S(2)}, u32[]{:S(2)}) collective-permute-start(bf16[2,40,1408]{2,1,0:T(8,128)(2,1)S(1)} %get-tuple-element.31), channel_id=1, source_target_pairs={{0,1},{1,0},{2,3},{3,2},{4,5},{5,4},{6,7},{7,6},{8,9},{9,8},{10,11... | collective-permute-start | bytes 675848 | tf_op jit(solution)/shard_map/ppermute | solution.py:423
  36.1 2.1 %collective-permute-start.11 = (bf16[2,40,1408]{2,1,0:T(8,128)(2,1)S(1)}, bf16[2,40,1408]{2,1,0:T(8,128)(2,1)S(1)}, u32[]{:S(2)}, u32[]{:S(2)}) collective-permute-start(bf16[2,40,1408]{2,1,0:T(8,128)(2,1)S(1)} %collective-permute-done.10.refs_11_), channel_id=1, source_target_pairs={{0,1},{1,0},{2,3},{3,2},{4,5},{5,4},{6,7},{7,6},{8,9},{9,8},{10,11... | collective-permute-start | bytes 675848 | tf_op jit(solution)/shard_map/ppermute | solution.py:423
  38.2 3.7 %collective-permute-start.13 = (bf16[2,40,2816]{2,1,0:T(8,128)(2,1)S(1)}, bf16[2,40,2816]{2,1,0:T(8,128)(2,1)S(1)}, u32[]{:S(2)}, u32[]{:S(2)}) collective-permute-start(bf16[2,40,2816]{2,1,0:T(8,128)(2,1)S(1)} %collective-permute-done.12.refs_13_), channel_id=1, source_target_pairs={{0,1},{1,0},{2,3},{3,2},{12,13},{13,12},{14,15},{15,14},{16,17},{1... | collective-permute-start | bytes 1351688 | tf_op jit(solution)/shard_map/ppermute | solution.py:423

commit v5 on v4

--- a/solution.py
+++ b/solution.py
@@ -83,6 +83,8 @@
 N_X = 2
 N_Z = 4
 SLOTS = N_X * N_Z
+IN_ROWS = (256,) * 3
+GRAD_ROWS = (128,) * 2 + (256,) * 7
 SMEM = pl.BlockSpec(memory_space=pltpu.SMEM)
 VMEM = pl.BlockSpec(memory_space=pltpu.VMEM)
 ANY = pl.BlockSpec(memory_space=pl.ANY)
@@ -142,116 +144,150 @@
     return lax.div(chip, N_X), lax.rem(chip, N_X), lax.axis_index("hid").astype(jnp.int32)
 
 
-def block_at(plane, column, row):
-    return lookup(slot_table().reshape(-1, 3)[:, row], plane * N_X + column)
-
-
-def pack_kernel(far_routes, grads, inputs, *refs):
-    first_ref, second_ref, across_ref, out_ref, x0_ref, own_ref = refs[:6]
-    routes_ref, held, held_i, packed, sems = refs[6:]
-    plane, column, core = place()
-    capacity, total = x0_ref.shape
-    width = held.shape[2]
-    sources = [(grads, held), (inputs, held_i)]
+BF16 = jnp.bfloat16
+FAR = pl.BlockSpec(memory_space=pltpu.HBM)
+
+
+def half_copies(sources, buffers, sems, which):
     copies = []
-    for n, (source, buffer) in enumerate(sources):
-        size = buffer.shape[2]
+    for source, buffer in zip(sources, buffers):
+        half = buffer.shape[2]
         for block in range(4):
+            start = pl.multiple_of(block * 2 * half + which * half, 128)
             copies.append(
                 pltpu.make_async_copy(
-                    source.at[:, block * size : (block + 1) * size],
-                    buffer.at[block],
-                    sems.at[4 * n + block],
+                    source.at[:, pl.ds(start, half)], buffer.at[block], sems.at[len(copies)]
                 )
             )
+    return copies
+
+
+def choose(picker, empty, buffers, copies, packed, which):
+    low = 0
+    for n, buffer in enumerate(buffers):
+        half = buffer.shape[2]
+        for block in range(4):
+            copies[4 * n + block].wait()
+            got = jnp.dot(picker, buffer[block], preferred_element_type=jnp.float32)
+            if n == 1:
+                head = jnp.where(empty & (which == 0), jnp.inf, got[:, :128])
+                packed[block, :, low : low + 128] = head.astype(BF16)
+                packed[block, :, low + 128 :] = got[:, 128:].astype(BF16)
+            else:
+                packed[block, :, :half] = got.astype(BF16)
+        low += half
+
+
+def no_token(picker):
+    capacity = picker.shape[0]
+    return (jnp.sum(picker, axis=1, keepdims=True) == 0.0) & (
+        lax.broadcasted_iota(jnp.int32, (capacity, 128), 1) == 0
+    )
+
+
+def pack_kernel(far_routes, grads, inputs, *refs):
+    first_ref, second_ref, x0_ref, packed, picker_ref = refs[:5]
+    routes_ref, held, held_i, sems = refs[5:]
+    plane, column, core = place()
+    capacity = packed.shape[1]
     routes_copy = pltpu.make_async_copy(far_routes, routes_ref, sems.at[8])
     routes_copy.start()
+    copies = half_copies((grads, inputs), (held, held_i), sems, core)
     for copy in copies:
         copy.start()
-    routes_copy.wait()
-    chosen = (routes_ref[0:1, :] == 0) | (routes_ref[1:2, :] == 0)
-    tokens = chosen.shape[1]
-    flags = jnp.where(chosen, 1.0, 0.0)
+    tokens = routes_ref.shape[1]
     before = (
         lax.broadcasted_iota(jnp.int32, (tokens, tokens), 0)
         <= lax.broadcasted_iota(jnp.int32, (tokens, tokens), 1)
     )
-    rank = jnp.dot(
-        flags.astype(BF16),
-        jnp.where(before, 1.0, 0.0).astype(BF16),
-        preferred_element_type=jnp.float32,
-    )
+    before = jnp.where(before, 1.0, 0.0).astype(BF16)
     slot = lax.broadcasted_iota(jnp.int32, (capacity, tokens), 0).astype(jnp.float32) + 1.0
+    routes_copy.wait()
+    chosen = (routes_ref[0:1, :] == 0) | (routes_ref[1:2, :] == 0)
+    flags = jnp.where(chosen, 1.0, 0.0)
+    rank = jnp.dot(flags.astype(BF16), before, preferred_element_type=jnp.float32)
     picker = jnp.where((rank == slot) & chosen, 1.0, 0.0)
-    empty = (jnp.sum(picker, axis=1, keepdims=True) == 0.0) & (
-        lax.broadcasted_iota(jnp.int32, (capacity, 128), 1) == 0
-    )
+    empty = no_token(picker)
     picker = picker.astype(BF16)
-    for n, (_, buffer) in enumerate(sources):
-        for block in range(4):
-            copies[4 * n + block].wait()
-            got = jnp.dot(picker, buffer[block], preferred_element_type=jnp.float32)
-            if n == 0:
-                head = jnp.where(empty, jnp.inf, got[:, :128])
-                packed[block, :, :128] = head.astype(BF16)
-                packed[block, :, 128:width] = got[:, 128:].astype(BF16)
-            else:
-                packed[block, :, width:] = got.astype(BF16)
-    bounds = (0, width, total)
-
-    def put_half(ref, row, block):
-        for low, high in zip(bounds[:-1], bounds[1:]):
-            half = (high - low) // 2
-            start = pl.multiple_of(low + core * half, 128)
-            ref[row, :, low // 2 : high // 2] = packed[block, :, pl.ds(start, half)]
-
+    picker_ref[...] = picker
+    choose(picker, empty, (held, held_i), copies, packed, core)
     firsts = first_slots()
     to_plane = lookup(FIRST_HOP, plane)
     for row in range(4):
-        put_half(first_ref, row, lookup(firsts[:, row], to_plane * N_X + column))
+        first_ref[row] = packed[lookup(firsts[:, row], to_plane * N_X + column)]
     to_plane = lookup(SECOND_HOP, plane)
     for row in range(3):
-        put_half(second_ref, row, block_at(to_plane, column, row))
-    x0_block = jnp.where(
-        core == 0, block_at(plane, 1 - column, 1), block_at(plane, 1 - column, 0)
-    )
-    x0_ref[...] = packed[x0_block]
-    to_column = jnp.where(core == 0, column, 1 - column)
+        second_ref[row] = packed[block_at(to_plane, column, row)]
     for row in range(2):
-        own_ref[row] = packed[block_at(plane, column, row)]
-        across_ref[row] = packed[block_at(lookup((0, 2, 1, 0), plane), to_column, row)]
-        out_ref[row] = packed[block_at(lookup((0, 3, 0, 0), plane), to_column, row)]
-
-
-BF16 = jnp.bfloat16
+        x0_ref[row] = packed[block_at(plane, column, row + 1)]
+
+
+def block_at(plane, column, row):
+    return lookup(slot_table().reshape(-1, 3)[:, row], plane * N_X + column)
 
 
 def pack(routes_t, grads, inputs, capacity):
     tokens = routes_t.shape[1]
-    width, width_i = grads.shape[1] // 4, inputs.shape[1] // 4
-    total = width + width_i
-    shapes = [(4, capacity, total // 2), (3, capacity, total // 2), (2, capacity, total)]
-    shapes += [(2, capacity, total), (capacity, total), (2, capacity, total)]
+    halves = (grads.shape[1] // 8, inputs.shape[1] // 8)
+    shapes = [(n, capacity, sum(halves)) for n in (4, 3, 2, 4)] + [(capacity, tokens)]
     operands = [pltpu.with_memory_space_constraint(a, pltpu.HBM) for a in (routes_t, grads, inputs)]
     return pl.pallas_call(
         pack_kernel,
         out_shape=[jax.ShapeDtypeStruct(s, BF16) for s in shapes],
-        in_specs=[pl.BlockSpec(memory_space=pltpu.HBM)] * 3,
+        in_specs=[FAR] * 3,
         out_specs=[VMEM] * len(shapes),
-        scratch_shapes=[
-            pltpu.VMEM(routes_t.shape, jnp.int32),
-            pltpu.VMEM((4, tokens, width), BF16),
-            pltpu.VMEM((4, tokens, width_i), BF16),
-            pltpu.VMEM((4, capacity, total), BF16),
-            pltpu.SemaphoreType.DMA((9,)),
-        ],
+        scratch_shapes=[pltpu.VMEM(routes_t.shape, jnp.int32)]
+        + [pltpu.VMEM((4, tokens, half), BF16) for half in halves]
+        + [pltpu.SemaphoreType.DMA((9,))],
         compiler_params=pltpu.CompilerParams(vmem_limit_bytes=12 * 2**20),
-        cost_estimate=pl.CostEstimate(
-            flops=2 * 4 * capacity * tokens * total,
-            bytes_accessed=8 * tokens * total,
-            transcendentals=0,
-        ),
+        cost_estimate=NO_COST,
     )(*operands)
+
+
+def rest_kernel(grads, inputs, packed, picker_ref, *refs):
+    across_ref, out_ref, own_ref, held, held_i, other, whole, sems = refs
+    plane, column, core = place()
+    copies = half_copies((grads, inputs), (held, held_i), sems, 1 - core)
+    for copy in copies:
+        copy.start()
+    halves = (held.shape[2], held_i.shape[2])
+    spans = ((0, 0, halves[0]), (2 * halves[0], halves[0], halves[1]))
+    picker = picker_ref[...]
+    empty = no_token(picker.astype(jnp.float32))
+    choose(picker, empty, (held, held_i), copies, other, 1 - core)
+    for start, low, half in spans:
+        mine = pl.ds(pl.multiple_of(start + core * half, 128), half)
+        far = pl.ds(pl.multiple_of(start + (1 - core) * half, 128), half)
+        for block in range(4):
+            whole[block, :, mine] = packed[block, :, low : low + half]
+            whole[block, :, far] = other[block, :, low : low + half]
+    to_column = jnp.where(core == 0, column, 1 - column)
+    for row in range(2):
+        across_ref[row] = whole[block_at(lookup((0, 2, 1, 0), plane), to_column, row)]
+        out_ref[row] = whole[block_at(lookup((0, 3, 0, 0), plane), to_column, row)]
+        own_ref[row] = whole[block_at(plane, column, row)]
+
+
+def rest(grads, inputs, packed, picker):
+    _, capacity, half = packed.shape
+    tokens = picker.shape[1]
+    halves = (grads.shape[1] // 8, inputs.shape[1] // 8)
+    shapes = [(2, capacity, 2 * half)] * 3
+    operands = [pltpu.with_memory_space_constraint(a, pltpu.HBM) for a in (grads, inputs)]
+    return pl.pallas_call(
+        rest_kernel,
+        out_shape=[jax.ShapeDtypeStruct(s, BF16) for s in shapes],
+        in_specs=[FAR] * 2 + [VMEM] * 2,
+        out_specs=[VMEM] * len(shapes),
+        scratch_shapes=[pltpu.VMEM((4, tokens, h), BF16) for h in halves]
+        + [pltpu.VMEM((4, capacity, half), BF16), pltpu.VMEM((4, capacity, 2 * half), BF16)]
+        + [pltpu.SemaphoreType.DMA((8,))],
+        compiler_params=pltpu.CompilerParams(vmem_limit_bytes=12 * 2**20),
+        cost_estimate=NO_COST,
+    )(*operands, packed, picker)
+
+
+NO_COST = pl.CostEstimate(flops=0, bytes_accessed=0, transcendentals=0)
 
 
 def relay_kernel(got, own, keep_ref, forward_ref, second_ref):
@@ -274,12 +310,12 @@
         in_specs=[VMEM] * 2,
         out_specs=[VMEM] * 3,
         compiler_params=pltpu.CompilerParams(vmem_limit_bytes=4 * 2**20),
-        cost_estimate=cost(1, 1),
+        cost_estimate=NO_COST,
     )(got, own)
 
 
 def assemble(data, pieces, start):
-    own, x0, hx0, across, far_across, *halves, out, far_out = pieces
+    own, across, far_across, out, far_out, *halves = pieces
     plane, column, core = place()
     inner = (plane == 1) | (plane == 2)
     capacity = own.shape[1]
@@ -289,22 +325,36 @@
     half_span = pl.ds(start // 2, half)
     mine = pl.ds(pl.multiple_of(core * half, 128), half)
     far = pl.ds(pl.multiple_of((1 - core) * half, 128), half)
+
+    def rows(slot):
+        return pl.ds(slot * SLOT_ROWS, capacity)
+
+    def put(slot, block, n):
+        row = block if n % 2 else 1 - block
+        data[block, rows(slot), mine] = halves[2 * n][row, :, half_span]
+        data[block, rows(slot), far] = halves[2 * n + 1][row, :, half_span]
+
     for block in range(2):
-        whole = [own[block, :, span]]
-        whole.append(jnp.where((core == 0) == (block == 1), x0[:, span], hx0[:, span]))
-        whole.append(jnp.where(inner, across[block, :, span], out[block, :, span]))
-        whole.append(jnp.where(inner, far_across[block, :, span], far_out[block, :, span]))
         for slot in range(SLOTS):
             low = slot * SLOT_ROWS
             data[block, low + 32 : low + SLOT_ROWS, :] = jnp.zeros((SLOT_ROWS - 32, size), BF16)
-            if slot < len(whole):
-                data[block, low : low + capacity, :] = whole[slot]
-            else:
-                n = 2 * (slot - len(whole))
-                row = block if n < 4 else 1 - block
-                rows = pl.ds(low, capacity)
-                data[block, rows, mine] = halves[n][row, :, half_span]
-                data[block, rows, far] = halves[n + 1][row, :, half_span]
+        data[block, rows(0), :] = own[block, :, span]
+        for n in range(5):
+            put(1 + n, block, n)
+
+    def put_whole(slot, ref):
+        for block in range(2):
+            data[block, rows(slot), :] = ref[block, :, span]
+
+    @pl.when(inner)
+    def _():
+        put_whole(6, across)
+        put_whole(7, far_across)
+
+    @pl.when(jnp.logical_not(inner))
+    def _():
+        put_whole(6, out)
+        put_whole(7, far_out)
 
 
 def clear_marks(data, capacity, slots):
@@ -334,10 +384,6 @@
     )
 
 
-def cost(rows, width):
-    return pl.CostEstimate(flops=0, bytes_accessed=0, transcendentals=0)
-
-
 def tiles_kernel(*refs):
     pieces = refs[:15]
     out_i, out, data, data_i, stage, stage_i, sems = refs[15:]
@@ -349,18 +395,19 @@
         copies.append(pltpu.make_async_copy(source, target, sems.at[len(copies)]))
         copies[-1].start()
 
-    def multiply(data, stage, out, steps):
-        size = data.shape[2] // steps
-        for i in range(steps):
-            rows = pl.ds(i * size, size)
+    def multiply(data, stage, out, sizes):
+        low = 0
+        for size in sizes:
+            rows = pl.ds(low, size)
+            low += size
             stage[rows, :] = product(scale, data[left, :, rows], data[right])
             write(stage.at[rows], out.at[0, rows])
 
+    assemble(data_i, pieces, width)
+    scale = clear_marks(data_i, pieces[0].shape[1], SLOTS)
+    multiply(data_i, stage_i, out_i, IN_ROWS)
     assemble(data, pieces, 0)
-    scale = clear_marks(data, pieces[0].shape[1], SLOTS)
-    multiply(data, stage, out, 8)
-    assemble(data_i, pieces, width)
-    multiply(data_i, stage_i, out_i, 3)
+    multiply(data, stage, out, GRAD_ROWS)
     for copy in copies:
         copy.wait()
 
@@ -374,9 +421,9 @@
         out_specs=[ANY, ANY],
         scratch_shapes=[pltpu.VMEM((2, SLOTS * SLOT_ROWS, w), BF16) for w in (width, width_i)]
         + [pltpu.VMEM((w, w), jnp.float32) for w in (width, width_i)]
-        + [pltpu.SemaphoreType.DMA((11,))],
+        + [pltpu.SemaphoreType.DMA((len(IN_ROWS) + len(GRAD_ROWS),))],
         compiler_params=pltpu.CompilerParams(vmem_limit_bytes=32 * 2**20),
-        cost_estimate=cost(width, width),
+        cost_estimate=NO_COST,
     )(*pieces)
 
 
@@ -411,8 +458,6 @@
 ENDS = moves(OUTWARD, to_both_columns)
 ALONG_X = moves(STAY, to_neighbour)
 CORES = moves(STAY, to_other_core)
-INNER_CORES = moves((None, 1, 2, None), to_other_core)
-OUTER_CORES = moves((0, None, None, 3), to_other_core)
 
 
 def after(array, *done):
@@ -425,29 +470,29 @@
 
 def shards_eight(inputs, hidden_grads, routes):
     capacity = routes.shape[0] * 5 // 16
-    first, second, across, out, x0, own = pack(routes.T, hidden_grads, inputs, capacity)
+    first, second, x0, packed, picker = pack(routes.T, hidden_grads, inputs, capacity)
     first = send(first, FIRST)
     x0 = send(x0, ALONG_X)
-    hx0 = send(x0, CORES)
+    across, out, own = rest(hidden_grads, inputs, packed, picker)
+    far_x0 = send(x0, CORES)
     first = after(first, x0)
+    across = send(after(across, x0), MIDDLE)
     keep, forward, second = relay(first, second)
     second = send(second, SECOND)
-    across = send(after(across, x0), MIDDLE)
     out = send(after(out, keep), ENDS)
     x1 = send(forward, ALONG_X)
     far_keep = send(keep, CORES)
-    second = after(second, far_keep, hx0, across)
     far_x1 = send(x1, CORES)
+    second = after(second, far_keep, far_x0, across)
     x2 = send(second[1:], ALONG_X)
     far_second = send(second[:2], CORES)
-    far_across = send(across, INNER_CORES)
+    far_across = send(across, CORES)
     far_x2 = send(x2, CORES)
     out = after(out, far_x1, far_second, far_across, far_x2)
-    far_out = send(out, OUTER_CORES)
-    pieces = [own, x0, hx0, across, far_across, keep, far_keep, second, far_second]
-    pieces += [x1, far_x1, x2, far_x2, out, far_out]
-    input_tile, grad_tile = tiles(hidden_grads.shape[1] // 4, pieces)
-    return input_tile, grad_tile
+    far_out = send(out, CORES)
+    pieces = [own, across, far_across, out, far_out, x0, far_x0, keep, far_keep]
+    pieces += [x1, far_x1, second, far_second, x2, far_x2]
+    return tuple(tiles(hidden_grads.shape[1] // 4, pieces))
 
 
 def solution(mesh):

time: 50.5 us -> 47.8 us (0.947)
  starting transfers between devices: 16.9 us -> 14.4 us
  waiting for transfers between devices: 21.5 us -> 19.8 us
  Pallas kernels: 11.2 us -> 12.7 us
    ppermute x14, starting transfers between devices: 16.9 us -> 14.4 us  [send(): return lax.ppermute(array, ('tok', 'hid'), pairs)]
    pallas_call x0 -> x1, Pallas kernels: none -> 2.38 us  [rest(): pl.pallas_call(rest_kernel, out_shape=[jax.ShapeDtypeStruct(s, BF16) for...]
    ppermute x14, waiting for transfers between devices: 21.5 us -> 19.8 us  [send(): return lax.ppermute(array, ('tok', 'hid'), pairs)]
  transfers between devices with their start and end apart: 14 -> 14, of which waited for: 6 -> 6; matrix products, arithmetic and copies ran while one was open for 0% -> 0% of each run, Pallas kernels for 0% -> 5%
where the time goes in v5:
time: 47.8 us; the launch traced here: 47.6 us
  waiting for transfers between devices  19.8 us (41%)
  starting transfers between devices  14.4 us (30%)
  Pallas kernels  12.7 us (27%)
  between operations  0.7 us (1%)
    ppermute x14, waiting for transfers between devices, send(): return lax.ppermute(array, ('tok', 'hid'), pairs)  19.8 us
    ppermute x14, starting transfers between devices, send(): return lax.ppermute(array, ('tok', 'hid'), pairs)  14.4 us
    pallas_call x1, Pallas kernels, tiles(): pl.pallas_call(tiles_kernel, out_shape=[jax.ShapeDtypeStruct((1, w, w), j...  7.93 us
    pallas_call x1, Pallas kernels, rest(): pl.pallas_call(rest_kernel, out_shape=[jax.ShapeDtypeStruct(s, BF16) for...  2.38 us
    pallas_call x1, Pallas kernels, pack(): pl.pallas_call(pack_kernel, out_shape=[jax.ShapeDtypeStruct(s, BF16) for...  2.34 us
  transfers between devices with their start and end apart: 14, of which 6 were waited for; matrix products, arithmetic and copies ran while one was open for 0% of the time, Pallas kernels for 5%

profile of v5, /device:TPU:0, one launch (start us, length us, event | category | flops | bytes accessed | tf_op | source)
XLA Modules:
  0.0 47.6 jit_solution(16991495882035876314)
XLA Ops:
  0.6 2.3 %shard_map.50 = (bf16[4,40,1408]{2,1,0:T(8,128)(2,1)S(1)}, bf16[3,40,1408]{2,1,0:T(8,128)(2,1)S(1)}, bf16[2,40,1408]{2,1,0:T(8,128)(2,1)S(1)}, bf16[4,40,1408]{2,1,0:T(8,128)(2,1)S(1)}, bf16[40,128]{1,0:T(8,128)(2,1)S(1)}) custom-call(s32[2,128]{1,0:T(2,128)} %bitcast.1, bf16[128,8192]{1,0:T(8,128)(2,1)} %grads.3, bf16[128,3072]{1,0:T(8,128)(2,1)} %inputs.3), custom_call_target="tpu_custom_call" | custom-call | tf_op jit(solution)/shard_map/pallas_call | solution.py:234
  3.0 4.1 %collective-permute-start.3 = (bf16[4,40,1408]{2,1,0:T(8,128)(2,1)S(1)}, bf16[4,40,1408]{2,1,0:T(8,128)(2,1)S(1)}, u32[]{:S(2)}, u32[]{:S(2)}) collective-permute-start(bf16[4,40,1408]{2,1,0:T(8,128)(2,1)S(1)} %get-tuple-element.25), channel_id=1, source_target_pairs={{0,8},{1,9},{2,10},{3,11},{4,0},{5,1},{6,2},{7,3},{8,12},{9,13},{1... | collective-permute-start | bytes 1351688 | tf_op jit(solution)/shard_map/ppermute | solution.py:468
  7.1 1.5 %collective-permute-start = (bf16[2,40,1408]{2,1,0:T(8,128)(2,1)S(1)}, bf16[2,40,1408]{2,1,0:T(8,128)(2,1)S(1)}, u32[]{:S(2)}, u32[]{:S(2)}) collective-permute-start(bf16[2,40,1408]{2,1,0:T(8,128)(2,1)S(1)} %get-tuple-element.22), channel_id=1, source_target_pairs={{0,2},{1,3},{2,0},{3,1},{4,6},{5,7},{6,4},{7,5},{8,10},{9,11},{10,... | collective-permute-start | bytes 675848 | tf_op jit(solution)/shard_map/ppermute | solution.py:468
  8.6 2.4 %shard_map.51 = (bf16[2,40,2816]{2,1,0:T(8,128)(2,1)S(1)}, bf16[2,40,2816]{2,1,0:T(8,128)(2,1)S(1)}, bf16[2,40,2816]{2,1,0:T(8,128)(2,1)S(1)}) custom-call(bf16[128,8192]{1,0:T(8,128)(2,1)} %grads.3, bf16[128,3072]{1,0:T(8,128)(2,1)} %inputs.3, bf16[4,40,1408]{2,1,0:T(8,128)(2,1)S(1)} %get-tuple-element.18.packed, ...), custom_call_target="tpu_custom_call" | custom-call | tf_op jit(solution)/shard_map/pallas_call | solution.py:277
  11.0 3.1 %collective-permute-done.refs_5_ = bf16[2,40,1408]{2,1,0:T(8,128)(2,1)S(1)} collective-permute-done((bf16[2,40,1408]{2,1,0:T(8,128)(2,1)S(1)}, bf16[2,40,1408]{2,1,0:T(8,128)(2,1)S(1)}, u32[]{:S(2)}, u32[]{:S(2)}) %collective-permute-start) | collective-permute-done | bytes 225312 | tf_op jit(solution)/shard_map/ppermute | solution.py:468
  14.1 0.7 %collective-permute-start.1 = (bf16[2,40,2816]{2,1,0:T(8,128)(2,1)S(1)}, bf16[2,40,2816]{2,1,0:T(8,128)(2,1)S(1)}, u32[]{:S(2)}, u32[]{:S(2)}) collective-permute-start(bf16[2,40,2816]{2,1,0:T(8,128)(2,1)S(1)} %get-tuple-element.23), channel_id=1, source_target_pairs={{4,8},{5,11},{6,10},{7,9},{8,4},{9,7},{10,6},{11,5},{20,24},{21,27... | collective-permute-start | bytes 1351688 | tf_op jit(solution)/shard_map/ppermute | solution.py:468
  14.7 1.9 %collective-permute-done.3.got = bf16[4,40,1408]{2,1,0:T(8,128)(2,1)S(1)} collective-permute-done((bf16[4,40,1408]{2,1,0:T(8,128)(2,1)S(1)}, bf16[4,40,1408]{2,1,0:T(8,128)(2,1)S(1)}, u32[]{:S(2)}, u32[]{:S(2)}) %collective-permute-start.3) | collective-permute-done | bytes 450592 | tf_op jit(solution)/shard_map/ppermute | solution.py:468
  16.7 0.1 shard_map.52
  16.8 2.5 %collective-permute-start.7 = (bf16[3,40,1408]{2,1,0:T(8,128)(2,1)S(1)}, bf16[3,40,1408]{2,1,0:T(8,128)(2,1)S(1)}, u32[]{:S(2)}, u32[]{:S(2)}) collective-permute-start(bf16[3,40,1408]{2,1,0:T(8,128)(2,1)S(1)} %get-tuple-element.31), channel_id=1, source_target_pairs={{0,4},{1,5},{2,6},{3,7},{4,0},{5,1},{6,2},{7,3},{8,12},{9,13},{10,... | collective-permute-start | bytes 1013768 | tf_op jit(solution)/shard_map/ppermute | solution.py:468
  19.3 0.0 collective-permute-start.9
  19.3 0.5 %collective-permute-start.8 = (bf16[2,40,1408]{2,1,0:T(8,128)(2,1)S(1)}, bf16[2,40,1408]{2,1,0:T(8,128)(2,1)S(1)}, u32[]{:S(2)}, u32[]{:S(2)}) collective-permute-start(bf16[2,40,1408]{2,1,0:T(8,128)(2,1)S(1)} %get-tuple-element.28.refs_7_), channel_id=1, source_target_pairs={{0,1},{1,0},{2,3},{3,2},{4,5},{5,4},{6,7},{7,6},{8,9},{9,8},{10,11... | collective-permute-start | bytes 675848 | tf_op jit(solution)/shard_map/ppermute | solution.py:468
  19.8 1.5 %collective-permute-start.5 = (bf16[2,40,1408]{2,1,0:T(8,128)(2,1)S(1)}, bf16[2,40,1408]{2,1,0:T(8,128)(2,1)S(1)}, u32[]{:S(2)}, u32[]{:S(2)}) collective-permute-start(bf16[2,40,1408]{2,1,0:T(8,128)(2,1)S(1)} %get-tuple-element.30), channel_id=1, source_target_pairs={{0,2},{1,3},{2,0},{3,1},{4,6},{5,7},{6,4},{7,5},{8,10},{9,11},{10,... | collective-permute-start | bytes 675848 | tf_op jit(solution)/shard_map/ppermute | solution.py:468
  21.3 0.0 collective-permute-done.9.refs_6_
  21.3 1.3 %collective-permute-start.4 = (bf16[2,40,2816]{2,1,0:T(8,128)(2,1)S(1)}, bf16[2,40,2816]{2,1,0:T(8,128)(2,1)S(1)}, u32[]{:S(2)}, u32[]{:S(2)}) collective-permute-start(bf16[2,40,2816]{2,1,0:T(8,128)(2,1)S(1)} %get-tuple-element.29), channel_id=1, source_target_pairs={{4,12},{5,15},{6,14},{7,13},{8,0},{9,3},{10,2},{11,1},{20,28},{21,... | collective-permute-start | bytes 1351688 | tf_op jit(solution)/shard_map/ppermute | solution.py:468
  22.6 0.0 collective-permute-done.1.refs_1_
  22.6 0.1 collective-permute-start.2
  22.7 3.6 %collective-permute-done.7.refs_11_ = bf16[3,40,1408]{2,1,0:T(8,128)(2,1)S(1)} collective-permute-done((bf16[3,40,1408]{2,1,0:T(8,128)(2,1)S(1)}, bf16[3,40,1408]{2,1,0:T(8,128)(2,1)S(1)}, u32[]{:S(2)}, u32[]{:S(2)}) %collective-permute-start.7) | collective-permute-done | bytes 337952 | tf_op jit(solution)/shard_map/ppermute | solution.py:468
  26.3 1.6 %collective-permute-start.11 = (bf16[2,40,1408]{2,1,0:T(8,128)(2,1)S(1)}, bf16[2,40,1408]{2,1,0:T(8,128)(2,1)S(1)}, u32[]{:S(2)}, u32[]{:S(2)}) collective-permute-start(bf16[2,40,1408]{2,1,0:T(8,128)(2,1)S(1)} %get-tuple-element.34), channel_id=1, source_target_pairs={{0,2},{1,3},{2,0},{3,1},{4,6},{5,7},{6,4},{7,5},{8,10},{9,11},{10,... | collective-permute-start | bytes 675848 | tf_op jit(solution)/shard_map/ppermute | solution.py:468
  27.8 0.5 %collective-permute-start.10 = (bf16[2,40,1408]{2,1,0:T(8,128)(2,1)S(1)}, bf16[2,40,1408]{2,1,0:T(8,128)(2,1)S(1)}, u32[]{:S(2)}, u32[]{:S(2)}) collective-permute-start(bf16[2,40,1408]{2,1,0:T(8,128)(2,1)S(1)} %get-tuple-element.35), channel_id=1, source_target_pairs={{0,1},{1,0},{2,3},{3,2},{4,5},{5,4},{6,7},{7,6},{8,9},{9,8},{10,11... | collective-permute-start | bytes 675848 | tf_op jit(solution)/shard_map/ppermute | solution.py:468
  28.3 7.3 %collective-permute-done.11.refs_13_ = bf16[2,40,1408]{2,1,0:T(8,128)(2,1)S(1)} collective-permute-done((bf16[2,40,1408]{2,1,0:T(8,128)(2,1)S(1)}, bf16[2,40,1408]{2,1,0:T(8,128)(2,1)S(1)}, u32[]{:S(2)}, u32[]{:S(2)}) %collective-permute-start.11) | collective-permute-done | bytes 225312 | tf_op jit(solution)/shard_map/ppermute | solution.py:468
  35.7 2.1 %collective-permute-done.4.refs_3_ = bf16[2,40,2816]{2,1,0:T(8,128)(2,1)S(1)} collective-permute-done((bf16[2,40,2816]{2,1,0:T(8,128)(2,1)S(1)}, bf16[2,40,2816]{2,1,0:T(8,128)(2,1)S(1)}, u32[]{:S(2)}, u32[]{:S(2)}) %collective-permute-start.4) | collective-permute-done | bytes 450592 | tf_op jit(solution)/shard_map/ppermute | solution.py:468
  37.8 0.2 collective-permute-start.13
  38.0 1.7 %collective-permute-done.13.refs_4_ = bf16[2,40,2816]{2,1,0:T(8,128)(2,1)S(1)} collective-permute-done((bf16[2,40,2816]{2,1,0:T(8,128)(2,1)S(1)}, bf16[2,40,2816]{2,1,0:T(8,128)(2,1)S(1)}, u32[]{:S(2)}, u32[]{:S(2)}) %collective-permute-start.13) | collective-permute-done | bytes 450592 | tf_op jit(solution)/shard_map/ppermute | solution.py:468
  39.7 7.9 %shard_map.53 = (f32[1,768,768]{2,1,0:T(8,128)}, f32[1,2048,2048]{2,1,0:T(8,128)}) custom-call(bf16[2,40,2816]{2,1,0:T(8,128)(2,1)S(1)} %get-tuple-element.20.refs_0_, bf16[2,40,2816]{2,1,0:T(8,128)(2,1)S(1)} %collective-permute-done.1.refs_1_, bf16[2,40,2816]{2,1,0:T(8,128)(2,1)S(1)} %collective-permute-done.2.refs_2_, ...), custom_call_target="tpu_custom_call" | custom-call | tf_op jit(solution)/shard_map/pallas_call | solution.py:417
  (9 shorter events, 0.1 us)
Async XLA Ops:
  3.0 13.7 %collective-permute-start.3 = (bf16[4,40,1408]{2,1,0:T(8,128)(2,1)S(1)}, bf16[4,40,1408]{2,1,0:T(8,128)(2,1)S(1)}, u32[]{:S(2)}, u32[]{:S(2)}) collective-permute-start(bf16[4,40,1408]{2,1,0:T(8,128)(2,1)S(1)} %get-tuple-element.25), channel_id=1, source_target_pairs={{0,8},{1,9},{2,10},{3,11},{4,0},{5,1},{6,2},{7,3},{8,12},{9,13},{1... | collective-permute-start | bytes 1351688 | tf_op jit(solution)/shard_map/ppermute | solution.py:468
  7.1 7.0 %collective-permute-start = (bf16[2,40,1408]{2,1,0:T(8,128)(2,1)S(1)}, bf16[2,40,1408]{2,1,0:T(8,128)(2,1)S(1)}, u32[]{:S(2)}, u32[]{:S(2)}) collective-permute-start(bf16[2,40,1408]{2,1,0:T(8,128)(2,1)S(1)} %get-tuple-element.22), channel_id=1, source_target_pairs={{0,2},{1,3},{2,0},{3,1},{4,6},{5,7},{6,4},{7,5},{8,10},{9,11},{10,... | collective-permute-start | bytes 675848 | tf_op jit(solution)/shard_map/ppermute | solution.py:468
  14.1 8.5 %collective-permute-start.1 = (bf16[2,40,2816]{2,1,0:T(8,128)(2,1)S(1)}, bf16[2,40,2816]{2,1,0:T(8,128)(2,1)S(1)}, u32[]{:S(2)}, u32[]{:S(2)}) collective-permute-start(bf16[2,40,2816]{2,1,0:T(8,128)(2,1)S(1)} %get-tuple-element.23), channel_id=1, source_target_pairs={{4,8},{5,11},{6,10},{7,9},{8,4},{9,7},{10,6},{11,5},{20,24},{21,27... | collective-permute-start | bytes 1351688 | tf_op jit(solution)/shard_map/ppermute | solution.py:468
  16.8 9.5 %collective-permute-start.7 = (bf16[3,40,1408]{2,1,0:T(8,128)(2,1)S(1)}, bf16[3,40,1408]{2,1,0:T(8,128)(2,1)S(1)}, u32[]{:S(2)}, u32[]{:S(2)}) collective-permute-start(bf16[3,40,1408]{2,1,0:T(8,128)(2,1)S(1)} %get-tuple-element.31), channel_id=1, source_target_pairs={{0,4},{1,5},{2,6},{3,7},{4,0},{5,1},{6,2},{7,3},{8,12},{9,13},{10,... | collective-permute-start | bytes 1013768 | tf_op jit(solution)/shard_map/ppermute | solution.py:468
  19.3 2.0 %collective-permute-start.9 = (bf16[2,40,1408]{2,1,0:T(8,128)(2,1)S(1)}, bf16[2,40,1408]{2,1,0:T(8,128)(2,1)S(1)}, u32[]{:S(2)}, u32[]{:S(2)}) collective-permute-start(bf16[2,40,1408]{2,1,0:T(8,128)(2,1)S(1)} %collective-permute-done.refs_5_), channel_id=1, source_target_pairs={{0,1},{1,0},{2,3},{3,2},{4,5},{5,4},{6,7},{7,6},{8,9},{9,8},{10,11... | collective-permute-start | bytes 675848 | tf_op jit(solution)/shard_map/ppermute | solution.py:468
  19.3 3.4 %collective-permute-start.8 = (bf16[2,40,1408]{2,1,0:T(8,128)(2,1)S(1)}, bf16[2,40,1408]{2,1,0:T(8,128)(2,1)S(1)}, u32[]{:S(2)}, u32[]{:S(2)}) collective-permute-start(bf16[2,40,1408]{2,1,0:T(8,128)(2,1)S(1)} %get-tuple-element.28.refs_7_), channel_id=1, source_target_pairs={{0,1},{1,0},{2,3},{3,2},{4,5},{5,4},{6,7},{7,6},{8,9},{9,8},{10,11... | collective-permute-start | bytes 675848 | tf_op jit(solution)/shard_map/ppermute | solution.py:468
  19.8 8.0 %collective-permute-start.5 = (bf16[2,40,1408]{2,1,0:T(8,128)(2,1)S(1)}, bf16[2,40,1408]{2,1,0:T(8,128)(2,1)S(1)}, u32[]{:S(2)}, u32[]{:S(2)}) collective-permute-start(bf16[2,40,1408]{2,1,0:T(8,128)(2,1)S(1)} %get-tuple-element.30), channel_id=1, source_target_pairs={{0,2},{1,3},{2,0},{3,1},{4,6},{5,7},{6,4},{7,5},{8,10},{9,11},{10,... | collective-permute-start | bytes 675848 | tf_op jit(solution)/shard_map/ppermute | solution.py:468
  21.3 16.5 %collective-permute-start.4 = (bf16[2,40,2816]{2,1,0:T(8,128)(2,1)S(1)}, bf16[2,40,2816]{2,1,0:T(8,128)(2,1)S(1)}, u32[]{:S(2)}, u32[]{:S(2)}) collective-permute-start(bf16[2,40,2816]{2,1,0:T(8,128)(2,1)S(1)} %get-tuple-element.29), channel_id=1, source_target_pairs={{4,12},{5,15},{6,14},{7,13},{8,0},{9,3},{10,2},{11,1},{20,28},{21,... | collective-permute-start | bytes 1351688 | tf_op jit(solution)/shard_map/ppermute | solution.py:468
  22.6 15.2 %collective-permute-start.2 = (bf16[2,40,2816]{2,1,0:T(8,128)(2,1)S(1)}, bf16[2,40,2816]{2,1,0:T(8,128)(2,1)S(1)}, u32[]{:S(2)}, u32[]{:S(2)}) collective-permute-start(bf16[2,40,2816]{2,1,0:T(8,128)(2,1)S(1)} %collective-permute-done.1.refs_1_), channel_id=1, source_target_pairs={{0,1},{1,0},{2,3},{3,2},{4,5},{5,4},{6,7},{7,6},{8,9},{9,8},{10,11... | collective-permute-start | bytes 1351688 | tf_op jit(solution)/shard_map/ppermute | solution.py:468
  26.3 9.4 %collective-permute-start.11 = (bf16[2,40,1408]{2,1,0:T(8,128)(2,1)S(1)}, bf16[2,40,1408]{2,1,0:T(8,128)(2,1)S(1)}, u32[]{:S(2)}, u32[]{:S(2)}) collective-permute-start(bf16[2,40,1408]{2,1,0:T(8,128)(2,1)S(1)} %get-tuple-element.34), channel_id=1, source_target_pairs={{0,2},{1,3},{2,0},{3,1},{4,6},{5,7},{6,4},{7,5},{8,10},{9,11},{10,... | collective-permute-start | bytes 675848 | tf_op jit(solution)/shard_map/ppermute | solution.py:468
  27.8 7.8 %collective-permute-start.6 = (bf16[2,40,1408]{2,1,0:T(8,128)(2,1)S(1)}, bf16[2,40,1408]{2,1,0:T(8,128)(2,1)S(1)}, u32[]{:S(2)}, u32[]{:S(2)}) collective-permute-start(bf16[2,40,1408]{2,1,0:T(8,128)(2,1)S(1)} %collective-permute-done.5.refs_9_), channel_id=1, source_target_pairs={{0,1},{1,0},{2,3},{3,2},{4,5},{5,4},{6,7},{7,6},{8,9},{9,8},{10,11... | collective-permute-start | bytes 675848 | tf_op jit(solution)/shard_map/ppermute | solution.py:468
  27.8 10.0 %collective-permute-start.10 = (bf16[2,40,1408]{2,1,0:T(8,128)(2,1)S(1)}, bf16[2,40,1408]{2,1,0:T(8,128)(2,1)S(1)}, u32[]{:S(2)}, u32[]{:S(2)}) collective-permute-start(bf16[2,40,1408]{2,1,0:T(8,128)(2,1)S(1)} %get-tuple-element.35), channel_id=1, source_target_pairs={{0,1},{1,0},{2,3},{3,2},{4,5},{5,4},{6,7},{7,6},{8,9},{9,8},{10,11... | collective-permute-start | bytes 675848 | tf_op jit(solution)/shard_map/ppermute | solution.py:468
  35.7 2.1 %collective-permute-start.12 = (bf16[2,40,1408]{2,1,0:T(8,128)(2,1)S(1)}, bf16[2,40,1408]{2,1,0:T(8,128)(2,1)S(1)}, u32[]{:S(2)}, u32[]{:S(2)}) collective-permute-start(bf16[2,40,1408]{2,1,0:T(8,128)(2,1)S(1)} %collective-permute-done.11.refs_13_), channel_id=1, source_target_pairs={{0,1},{1,0},{2,3},{3,2},{4,5},{5,4},{6,7},{7,6},{8,9},{9,8},{10,11... | collective-permute-start | bytes 675848 | tf_op jit(solution)/shard_map/ppermute | solution.py:468
  37.8 1.9 %collective-permute-start.13 = (bf16[2,40,2816]{2,1,0:T(8,128)(2,1)S(1)}, bf16[2,40,2816]{2,1,0:T(8,128)(2,1)S(1)}, u32[]{:S(2)}, u32[]{:S(2)}) collective-permute-start(bf16[2,40,2816]{2,1,0:T(8,128)(2,1)S(1)} %collective-permute-done.4.refs_3_), channel_id=1, source_target_pairs={{0,1},{1,0},{2,3},{3,2},{4,5},{5,4},{6,7},{7,6},{8,9},{9,8},{10,11... | collective-permute-start | bytes 1351688 | tf_op jit(solution)/shard_map/ppermute | solution.py:468

commit v6 on v5

--- a/solution.py
+++ b/solution.py
@@ -83,8 +83,8 @@
 N_X = 2
 N_Z = 4
 SLOTS = N_X * N_Z
-IN_ROWS = (256,) * 3
-GRAD_ROWS = (128,) * 2 + (256,) * 7
+IN_ROWS = (128,) * 6
+GRAD_ROWS = (128,) * 4 + (256,) * 6
 SMEM = pl.BlockSpec(memory_space=pltpu.SMEM)
 VMEM = pl.BlockSpec(memory_space=pltpu.VMEM)
 ANY = pl.BlockSpec(memory_space=pl.ANY)
@@ -479,16 +479,16 @@
     across = send(after(across, x0), MIDDLE)
     keep, forward, second = relay(first, second)
     second = send(second, SECOND)
-    out = send(after(out, keep), ENDS)
+    out = send(after(out, far_x0), ENDS)
+    far_keep = send(keep, CORES)
     x1 = send(forward, ALONG_X)
-    far_keep = send(keep, CORES)
     far_x1 = send(x1, CORES)
     second = after(second, far_keep, far_x0, across)
     x2 = send(second[1:], ALONG_X)
     far_second = send(second[:2], CORES)
-    far_across = send(across, CORES)
+    far_across = send(after(across, x2), CORES)
     far_x2 = send(x2, CORES)
-    out = after(out, far_x1, far_second, far_across, far_x2)
+    out = after(out, far_x1, far_second, far_x2)
     far_out = send(out, CORES)
     pieces = [own, across, far_across, out, far_out, x0, far_x0, keep, far_keep]
     pieces += [x1, far_x1, second, far_second, x2, far_x2]

time: 47.8 us -> 47.5 us (level)
  waiting for transfers between devices: 19.8 us -> 19.3 us
where the time goes in v6:
time: 47.5 us; the launch traced here: 47.3 us
  waiting for transfers between devices  19.3 us (41%)
  starting transfers between devices  14.7 us (31%)
  Pallas kernels  12.5 us (26%)
  between operations  0.69 us (1%)
    ppermute x14, waiting for transfers between devices, send(): return lax.ppermute(array, ('tok', 'hid'), pairs)  19.3 us
    ppermute x14, starting transfers between devices, send(): return lax.ppermute(array, ('tok', 'hid'), pairs)  14.7 us
    pallas_call x1, Pallas kernels, tiles(): pl.pallas_call(tiles_kernel, out_shape=[jax.ShapeDtypeStruct((1, w, w), j...  7.73 us
    pallas_call x1, Pallas kernels, rest(): pl.pallas_call(rest_kernel, out_shape=[jax.ShapeDtypeStruct(s, BF16) for...  2.38 us
    pallas_call x1, Pallas kernels, pack(): pl.pallas_call(pack_kernel, out_shape=[jax.ShapeDtypeStruct(s, BF16) for...  2.34 us
  transfers between devices with their start and end apart: 14, of which 6 were waited for; matrix products, arithmetic and copies ran while one was open for 0% of the time, Pallas kernels for 5%

profile of v6, /device:TPU:0, one launch (start us, length us, event | category | flops | bytes accessed | tf_op | source)
XLA Modules:
  0.0 47.3 jit_solution(10704349816394430341)
XLA Ops:
  0.6 2.3 %shard_map.50 = (bf16[4,40,1408]{2,1,0:T(8,128)(2,1)S(1)}, bf16[3,40,1408]{2,1,0:T(8,128)(2,1)S(1)}, bf16[2,40,1408]{2,1,0:T(8,128)(2,1)S(1)}, bf16[4,40,1408]{2,1,0:T(8,128)(2,1)S(1)}, bf16[40,128]{1,0:T(8,128)(2,1)S(1)}) custom-call(s32[2,128]{1,0:T(2,128)} %bitcast.1, bf16[128,8192]{1,0:T(8,128)(2,1)} %grads.3, bf16[128,3072]{1,0:T(8,128)(2,1)} %inputs.3), custom_call_target="tpu_custom_call" | custom-call | tf_op jit(solution)/shard_map/pallas_call | solution.py:234
  3.0 4.1 %collective-permute-start.2 = (bf16[4,40,1408]{2,1,0:T(8,128)(2,1)S(1)}, bf16[4,40,1408]{2,1,0:T(8,128)(2,1)S(1)}, u32[]{:S(2)}, u32[]{:S(2)}) collective-permute-start(bf16[4,40,1408]{2,1,0:T(8,128)(2,1)S(1)} %get-tuple-element.25), channel_id=1, source_target_pairs={{0,8},{1,9},{2,10},{3,11},{4,0},{5,1},{6,2},{7,3},{8,12},{9,13},{1... | collective-permute-start | bytes 1351688 | tf_op jit(solution)/shard_map/ppermute | solution.py:468
  7.1 1.5 %collective-permute-start = (bf16[2,40,1408]{2,1,0:T(8,128)(2,1)S(1)}, bf16[2,40,1408]{2,1,0:T(8,128)(2,1)S(1)}, u32[]{:S(2)}, u32[]{:S(2)}) collective-permute-start(bf16[2,40,1408]{2,1,0:T(8,128)(2,1)S(1)} %get-tuple-element.23), channel_id=1, source_target_pairs={{0,2},{1,3},{2,0},{3,1},{4,6},{5,7},{6,4},{7,5},{8,10},{9,11},{10,... | collective-permute-start | bytes 675848 | tf_op jit(solution)/shard_map/ppermute | solution.py:468
  8.6 2.4 %shard_map.51 = (bf16[2,40,2816]{2,1,0:T(8,128)(2,1)S(1)}, bf16[2,40,2816]{2,1,0:T(8,128)(2,1)S(1)}, bf16[2,40,2816]{2,1,0:T(8,128)(2,1)S(1)}) custom-call(bf16[128,8192]{1,0:T(8,128)(2,1)} %grads.3, bf16[128,3072]{1,0:T(8,128)(2,1)} %inputs.3, bf16[4,40,1408]{2,1,0:T(8,128)(2,1)S(1)} %get-tuple-element.19.packed, ...), custom_call_target="tpu_custom_call" | custom-call | tf_op jit(solution)/shard_map/pallas_call | solution.py:277
  11.0 3.1 %collective-permute-done.refs_5_ = bf16[2,40,1408]{2,1,0:T(8,128)(2,1)S(1)} collective-permute-done((bf16[2,40,1408]{2,1,0:T(8,128)(2,1)S(1)}, bf16[2,40,1408]{2,1,0:T(8,128)(2,1)S(1)}, u32[]{:S(2)}, u32[]{:S(2)}) %collective-permute-start) | collective-permute-done | bytes 225312 | tf_op jit(solution)/shard_map/ppermute | solution.py:468
  14.1 0.7 %collective-permute-start.1 = (bf16[2,40,2816]{2,1,0:T(8,128)(2,1)S(1)}, bf16[2,40,2816]{2,1,0:T(8,128)(2,1)S(1)}, u32[]{:S(2)}, u32[]{:S(2)}) collective-permute-start(bf16[2,40,2816]{2,1,0:T(8,128)(2,1)S(1)} %get-tuple-element.24), channel_id=1, source_target_pairs={{4,8},{5,11},{6,10},{7,9},{8,4},{9,7},{10,6},{11,5},{20,24},{21,27... | collective-permute-start | bytes 1351688 | tf_op jit(solution)/shard_map/ppermute | solution.py:468
  14.7 1.9 %collective-permute-done.2.got = bf16[4,40,1408]{2,1,0:T(8,128)(2,1)S(1)} collective-permute-done((bf16[4,40,1408]{2,1,0:T(8,128)(2,1)S(1)}, bf16[4,40,1408]{2,1,0:T(8,128)(2,1)S(1)}, u32[]{:S(2)}, u32[]{:S(2)}) %collective-permute-start.2) | collective-permute-done | bytes 450592 | tf_op jit(solution)/shard_map/ppermute | solution.py:468
  16.7 0.1 shard_map.52
  16.8 2.5 %collective-permute-start.3 = (bf16[3,40,1408]{2,1,0:T(8,128)(2,1)S(1)}, bf16[3,40,1408]{2,1,0:T(8,128)(2,1)S(1)}, u32[]{:S(2)}, u32[]{:S(2)}) collective-permute-start(bf16[3,40,1408]{2,1,0:T(8,128)(2,1)S(1)} %get-tuple-element.28), channel_id=1, source_target_pairs={{0,4},{1,5},{2,6},{3,7},{4,0},{5,1},{6,2},{7,3},{8,12},{9,13},{10,... | collective-permute-start | bytes 1013768 | tf_op jit(solution)/shard_map/ppermute | solution.py:468
  19.3 0.0 collective-permute-start.5
  19.3 0.5 %collective-permute-start.4 = (bf16[2,40,1408]{2,1,0:T(8,128)(2,1)S(1)}, bf16[2,40,1408]{2,1,0:T(8,128)(2,1)S(1)}, u32[]{:S(2)}, u32[]{:S(2)}) collective-permute-start(bf16[2,40,1408]{2,1,0:T(8,128)(2,1)S(1)} %get-tuple-element.29.refs_7_), channel_id=1, source_target_pairs={{0,1},{1,0},{2,3},{3,2},{4,5},{5,4},{6,7},{7,6},{8,9},{9,8},{10,11... | collective-permute-start | bytes 675848 | tf_op jit(solution)/shard_map/ppermute | solution.py:468
  19.8 1.5 %collective-permute-start.9 = (bf16[2,40,1408]{2,1,0:T(8,128)(2,1)S(1)}, bf16[2,40,1408]{2,1,0:T(8,128)(2,1)S(1)}, u32[]{:S(2)}, u32[]{:S(2)}) collective-permute-start(bf16[2,40,1408]{2,1,0:T(8,128)(2,1)S(1)} %get-tuple-element.34), channel_id=1, source_target_pairs={{0,2},{1,3},{2,0},{3,1},{4,6},{5,7},{6,4},{7,5},{8,10},{9,11},{10,... | collective-permute-start | bytes 675848 | tf_op jit(solution)/shard_map/ppermute | solution.py:468
  21.3 0.0 collective-permute-done.5.refs_6_
  21.3 1.3 %collective-permute-start.8 = (bf16[2,40,2816]{2,1,0:T(8,128)(2,1)S(1)}, bf16[2,40,2816]{2,1,0:T(8,128)(2,1)S(1)}, u32[]{:S(2)}, u32[]{:S(2)}) collective-permute-start(bf16[2,40,2816]{2,1,0:T(8,128)(2,1)S(1)} %get-tuple-element.33), channel_id=1, source_target_pairs={{4,12},{5,15},{6,14},{7,13},{8,0},{9,3},{10,2},{11,1},{20,28},{21,... | collective-permute-start | bytes 1351688 | tf_op jit(solution)/shard_map/ppermute | solution.py:468
  22.6 0.0 collective-permute-done.4.refs_8_
  22.6 3.6 %collective-permute-done.3.refs_11_ = bf16[3,40,1408]{2,1,0:T(8,128)(2,1)S(1)} collective-permute-done((bf16[3,40,1408]{2,1,0:T(8,128)(2,1)S(1)}, bf16[3,40,1408]{2,1,0:T(8,128)(2,1)S(1)}, u32[]{:S(2)}, u32[]{:S(2)}) %collective-permute-start.3) | collective-permute-done | bytes 337952 | tf_op jit(solution)/shard_map/ppermute | solution.py:468
  26.3 1.6 %collective-permute-start.6 = (bf16[2,40,1408]{2,1,0:T(8,128)(2,1)S(1)}, bf16[2,40,1408]{2,1,0:T(8,128)(2,1)S(1)}, u32[]{:S(2)}, u32[]{:S(2)}) collective-permute-start(bf16[2,40,1408]{2,1,0:T(8,128)(2,1)S(1)} %get-tuple-element.37), channel_id=1, source_target_pairs={{0,2},{1,3},{2,0},{3,1},{4,6},{5,7},{6,4},{7,5},{8,10},{9,11},{10,... | collective-permute-start | bytes 675848 | tf_op jit(solution)/shard_map/ppermute | solution.py:468
  27.8 0.5 %collective-permute-start.11 = (bf16[2,40,1408]{2,1,0:T(8,128)(2,1)S(1)}, bf16[2,40,1408]{2,1,0:T(8,128)(2,1)S(1)}, u32[]{:S(2)}, u32[]{:S(2)}) collective-permute-start(bf16[2,40,1408]{2,1,0:T(8,128)(2,1)S(1)} %get-tuple-element.36), channel_id=1, source_target_pairs={{0,1},{1,0},{2,3},{3,2},{4,5},{5,4},{6,7},{7,6},{8,9},{9,8},{10,11... | collective-permute-start | bytes 675848 | tf_op jit(solution)/shard_map/ppermute | solution.py:468
  28.3 7.3 %collective-permute-done.6.refs_13_ = bf16[2,40,1408]{2,1,0:T(8,128)(2,1)S(1)} collective-permute-done((bf16[2,40,1408]{2,1,0:T(8,128)(2,1)S(1)}, bf16[2,40,1408]{2,1,0:T(8,128)(2,1)S(1)}, u32[]{:S(2)}, u32[]{:S(2)}) %collective-permute-start.6) | collective-permute-done | bytes 225312 | tf_op jit(solution)/shard_map/ppermute | solution.py:468
  35.7 0.5 %collective-permute-start.7 = (bf16[2,40,2816]{2,1,0:T(8,128)(2,1)S(1)}, bf16[2,40,2816]{2,1,0:T(8,128)(2,1)S(1)}, u32[]{:S(2)}, u32[]{:S(2)}) collective-permute-start(bf16[2,40,2816]{2,1,0:T(8,128)(2,1)S(1)} %collective-permute-done.1.refs_1_), channel_id=1, source_target_pairs={{0,1},{1,0},{2,3},{3,2},{4,5},{5,4},{6,7},{7,6},{8,9},{9,8},{10,11... | collective-permute-start | bytes 1351688 | tf_op jit(solution)/shard_map/ppermute | solution.py:468
  36.2 1.6 %collective-permute-done.8.refs_3_ = bf16[2,40,2816]{2,1,0:T(8,128)(2,1)S(1)} collective-permute-done((bf16[2,40,2816]{2,1,0:T(8,128)(2,1)S(1)}, bf16[2,40,2816]{2,1,0:T(8,128)(2,1)S(1)}, u32[]{:S(2)}, u32[]{:S(2)}) %collective-permute-start.8) | collective-permute-done | bytes 450592 | tf_op jit(solution)/shard_map/ppermute | solution.py:468
  37.8 0.1 collective-permute-start.13
  37.9 1.7 %collective-permute-done.13.refs_4_ = bf16[2,40,2816]{2,1,0:T(8,128)(2,1)S(1)} collective-permute-done((bf16[2,40,2816]{2,1,0:T(8,128)(2,1)S(1)}, bf16[2,40,2816]{2,1,0:T(8,128)(2,1)S(1)}, u32[]{:S(2)}, u32[]{:S(2)}) %collective-permute-start.13) | collective-permute-done | bytes 450592 | tf_op jit(solution)/shard_map/ppermute | solution.py:468
  39.6 7.7 %shard_map.53 = (f32[1,768,768]{2,1,0:T(8,128)}, f32[1,2048,2048]{2,1,0:T(8,128)}) custom-call(bf16[2,40,2816]{2,1,0:T(8,128)(2,1)S(1)} %get-tuple-element.21.refs_0_, bf16[2,40,2816]{2,1,0:T(8,128)(2,1)S(1)} %collective-permute-done.1.refs_1_, bf16[2,40,2816]{2,1,0:T(8,128)(2,1)S(1)} %collective-permute-done.7.refs_2_, ...), custom_call_target="tpu_custom_call" | custom-call | tf_op jit(solution)/shard_map/pallas_call | solution.py:417
  (9 shorter events, 0.1 us)
Async XLA Ops:
  3.0 13.7 %collective-permute-start.2 = (bf16[4,40,1408]{2,1,0:T(8,128)(2,1)S(1)}, bf16[4,40,1408]{2,1,0:T(8,128)(2,1)S(1)}, u32[]{:S(2)}, u32[]{:S(2)}) collective-permute-start(bf16[4,40,1408]{2,1,0:T(8,128)(2,1)S(1)} %get-tuple-element.25), channel_id=1, source_target_pairs={{0,8},{1,9},{2,10},{3,11},{4,0},{5,1},{6,2},{7,3},{8,12},{9,13},{1... | collective-permute-start | bytes 1351688 | tf_op jit(solution)/shard_map/ppermute | solution.py:468
  7.1 7.0 %collective-permute-start = (bf16[2,40,1408]{2,1,0:T(8,128)(2,1)S(1)}, bf16[2,40,1408]{2,1,0:T(8,128)(2,1)S(1)}, u32[]{:S(2)}, u32[]{:S(2)}) collective-permute-start(bf16[2,40,1408]{2,1,0:T(8,128)(2,1)S(1)} %get-tuple-element.23), channel_id=1, source_target_pairs={{0,2},{1,3},{2,0},{3,1},{4,6},{5,7},{6,4},{7,5},{8,10},{9,11},{10,... | collective-permute-start | bytes 675848 | tf_op jit(solution)/shard_map/ppermute | solution.py:468
  14.1 8.5 %collective-permute-start.1 = (bf16[2,40,2816]{2,1,0:T(8,128)(2,1)S(1)}, bf16[2,40,2816]{2,1,0:T(8,128)(2,1)S(1)}, u32[]{:S(2)}, u32[]{:S(2)}) collective-permute-start(bf16[2,40,2816]{2,1,0:T(8,128)(2,1)S(1)} %get-tuple-element.24), channel_id=1, source_target_pairs={{4,8},{5,11},{6,10},{7,9},{8,4},{9,7},{10,6},{11,5},{20,24},{21,27... | collective-permute-start | bytes 1351688 | tf_op jit(solution)/shard_map/ppermute | solution.py:468
  16.8 9.5 %collective-permute-start.3 = (bf16[3,40,1408]{2,1,0:T(8,128)(2,1)S(1)}, bf16[3,40,1408]{2,1,0:T(8,128)(2,1)S(1)}, u32[]{:S(2)}, u32[]{:S(2)}) collective-permute-start(bf16[3,40,1408]{2,1,0:T(8,128)(2,1)S(1)} %get-tuple-element.28), channel_id=1, source_target_pairs={{0,4},{1,5},{2,6},{3,7},{4,0},{5,1},{6,2},{7,3},{8,12},{9,13},{10,... | collective-permute-start | bytes 1013768 | tf_op jit(solution)/shard_map/ppermute | solution.py:468
  19.3 2.0 %collective-permute-start.5 = (bf16[2,40,1408]{2,1,0:T(8,128)(2,1)S(1)}, bf16[2,40,1408]{2,1,0:T(8,128)(2,1)S(1)}, u32[]{:S(2)}, u32[]{:S(2)}) collective-permute-start(bf16[2,40,1408]{2,1,0:T(8,128)(2,1)S(1)} %collective-permute-done.refs_5_), channel_id=1, source_target_pairs={{0,1},{1,0},{2,3},{3,2},{4,5},{5,4},{6,7},{7,6},{8,9},{9,8},{10,11... | collective-permute-start | bytes 675848 | tf_op jit(solution)/shard_map/ppermute | solution.py:468
  19.3 3.3 %collective-permute-start.4 = (bf16[2,40,1408]{2,1,0:T(8,128)(2,1)S(1)}, bf16[2,40,1408]{2,1,0:T(8,128)(2,1)S(1)}, u32[]{:S(2)}, u32[]{:S(2)}) collective-permute-start(bf16[2,40,1408]{2,1,0:T(8,128)(2,1)S(1)} %get-tuple-element.29.refs_7_), channel_id=1, source_target_pairs={{0,1},{1,0},{2,3},{3,2},{4,5},{5,4},{6,7},{7,6},{8,9},{9,8},{10,11... | collective-permute-start | bytes 675848 | tf_op jit(solution)/shard_map/ppermute | solution.py:468
  19.8 8.0 %collective-permute-start.9 = (bf16[2,40,1408]{2,1,0:T(8,128)(2,1)S(1)}, bf16[2,40,1408]{2,1,0:T(8,128)(2,1)S(1)}, u32[]{:S(2)}, u32[]{:S(2)}) collective-permute-start(bf16[2,40,1408]{2,1,0:T(8,128)(2,1)S(1)} %get-tuple-element.34), channel_id=1, source_target_pairs={{0,2},{1,3},{2,0},{3,1},{4,6},{5,7},{6,4},{7,5},{8,10},{9,11},{10,... | collective-permute-start | bytes 675848 | tf_op jit(solution)/shard_map/ppermute | solution.py:468
  21.3 16.5 %collective-permute-start.8 = (bf16[2,40,2816]{2,1,0:T(8,128)(2,1)S(1)}, bf16[2,40,2816]{2,1,0:T(8,128)(2,1)S(1)}, u32[]{:S(2)}, u32[]{:S(2)}) collective-permute-start(bf16[2,40,2816]{2,1,0:T(8,128)(2,1)S(1)} %get-tuple-element.33), channel_id=1, source_target_pairs={{4,12},{5,15},{6,14},{7,13},{8,0},{9,3},{10,2},{11,1},{20,28},{21,... | collective-permute-start | bytes 1351688 | tf_op jit(solution)/shard_map/ppermute | solution.py:468
  26.3 9.4 %collective-permute-start.6 = (bf16[2,40,1408]{2,1,0:T(8,128)(2,1)S(1)}, bf16[2,40,1408]{2,1,0:T(8,128)(2,1)S(1)}, u32[]{:S(2)}, u32[]{:S(2)}) collective-permute-start(bf16[2,40,1408]{2,1,0:T(8,128)(2,1)S(1)} %get-tuple-element.37), channel_id=1, source_target_pairs={{0,2},{1,3},{2,0},{3,1},{4,6},{5,7},{6,4},{7,5},{8,10},{9,11},{10,... | collective-permute-start | bytes 675848 | tf_op jit(solution)/shard_map/ppermute | solution.py:468
  27.8 8.3 %collective-permute-start.10 = (bf16[2,40,1408]{2,1,0:T(8,128)(2,1)S(1)}, bf16[2,40,1408]{2,1,0:T(8,128)(2,1)S(1)}, u32[]{:S(2)}, u32[]{:S(2)}) collective-permute-start(bf16[2,40,1408]{2,1,0:T(8,128)(2,1)S(1)} %collective-permute-done.9.refs_9_), channel_id=1, source_target_pairs={{0,1},{1,0},{2,3},{3,2},{4,5},{5,4},{6,7},{7,6},{8,9},{9,8},{10,11... | collective-permute-start | bytes 675848 | tf_op jit(solution)/shard_map/ppermute | solution.py:468
  27.8 10.0 %collective-permute-start.11 = (bf16[2,40,1408]{2,1,0:T(8,128)(2,1)S(1)}, bf16[2,40,1408]{2,1,0:T(8,128)(2,1)S(1)}, u32[]{:S(2)}, u32[]{:S(2)}) collective-permute-start(bf16[2,40,1408]{2,1,0:T(8,128)(2,1)S(1)} %get-tuple-element.36), channel_id=1, source_target_pairs={{0,1},{1,0},{2,3},{3,2},{4,5},{5,4},{6,7},{7,6},{8,9},{9,8},{10,11... | collective-permute-start | bytes 675848 | tf_op jit(solution)/shard_map/ppermute | solution.py:468
  35.7 2.1 %collective-permute-start.12 = (bf16[2,40,1408]{2,1,0:T(8,128)(2,1)S(1)}, bf16[2,40,1408]{2,1,0:T(8,128)(2,1)S(1)}, u32[]{:S(2)}, u32[]{:S(2)}) collective-permute-start(bf16[2,40,1408]{2,1,0:T(8,128)(2,1)S(1)} %collective-permute-done.6.refs_13_), channel_id=1, source_target_pairs={{0,1},{1,0},{2,3},{3,2},{4,5},{5,4},{6,7},{7,6},{8,9},{9,8},{10,11... | collective-permute-start | bytes 675848 | tf_op jit(solution)/shard_map/ppermute | solution.py:468
  35.7 2.2 %collective-permute-start.7 = (bf16[2,40,2816]{2,1,0:T(8,128)(2,1)S(1)}, bf16[2,40,2816]{2,1,0:T(8,128)(2,1)S(1)}, u32[]{:S(2)}, u32[]{:S(2)}) collective-permute-start(bf16[2,40,2816]{2,1,0:T(8,128)(2,1)S(1)} %collective-permute-done.1.refs_1_), channel_id=1, source_target_pairs={{0,1},{1,0},{2,3},{3,2},{4,5},{5,4},{6,7},{7,6},{8,9},{9,8},{10,11... | collective-permute-start | bytes 1351688 | tf_op jit(solution)/shard_map/ppermute | solution.py:468
  37.8 1.8 %collective-permute-start.13 = (bf16[2,40,2816]{2,1,0:T(8,128)(2,1)S(1)}, bf16[2,40,2816]{2,1,0:T(8,128)(2,1)S(1)}, u32[]{:S(2)}, u32[]{:S(2)}) collective-permute-start(bf16[2,40,2816]{2,1,0:T(8,128)(2,1)S(1)} %collective-permute-done.8.refs_3_), channel_id=1, source_target_pairs={{0,1},{1,0},{2,3},{3,2},{4,5},{5,4},{6,7},{7,6},{8,9},{9,8},{10,11... | collective-permute-start | bytes 1351688 | tf_op jit(solution)/shard_map/ppermute | solution.py:468

commit v7 on v6

--- a/solution.py
+++ b/solution.py
@@ -84,7 +84,7 @@
 N_Z = 4
 SLOTS = N_X * N_Z
 IN_ROWS = (128,) * 6
-GRAD_ROWS = (128,) * 4 + (256,) * 6
+GRAD_ROWS = (128,) * 8 + (256,) * 4
 SMEM = pl.BlockSpec(memory_space=pltpu.SMEM)
 VMEM = pl.BlockSpec(memory_space=pltpu.VMEM)
 ANY = pl.BlockSpec(memory_space=pl.ANY)

time: 47.5 us -> 47.5 us (level)
  no operation moved by 1% of the time
where the time goes in v7:
time: 47.5 us; the launch traced here: 47.3 us
  waiting for transfers between devices  19.3 us (41%)
  starting transfers between devices  14.7 us (31%)
  Pallas kernels  12.5 us (26%)
  between operations  0.69 us (1%)
    ppermute x14, waiting for transfers between devices, send(): return lax.ppermute(array, ('tok', 'hid'), pairs)  19.3 us
    ppermute x14, starting transfers between devices, send(): return lax.ppermute(array, ('tok', 'hid'), pairs)  14.7 us
    pallas_call x1, Pallas kernels, tiles(): pl.pallas_call(tiles_kernel, out_shape=[jax.ShapeDtypeStruct((1, w, w), j...  7.71 us
    pallas_call x1, Pallas kernels, rest(): pl.pallas_call(rest_kernel, out_shape=[jax.ShapeDtypeStruct(s, BF16) for...  2.38 us
    pallas_call x1, Pallas kernels, pack(): pl.pallas_call(pack_kernel, out_shape=[jax.ShapeDtypeStruct(s, BF16) for...  2.34 us
  transfers between devices with their start and end apart: 14, of which 6 were waited for; matrix products, arithmetic and copies ran while one was open for 0% of the time, Pallas kernels for 5%

profile of v7, /device:TPU:0, one launch (start us, length us, event | category | flops | bytes accessed | tf_op | source)
XLA Modules:
  0.0 47.3 jit_solution(14708910992970720438)
XLA Ops:
  0.6 2.3 %shard_map.50 = (bf16[4,40,1408]{2,1,0:T(8,128)(2,1)S(1)}, bf16[3,40,1408]{2,1,0:T(8,128)(2,1)S(1)}, bf16[2,40,1408]{2,1,0:T(8,128)(2,1)S(1)}, bf16[4,40,1408]{2,1,0:T(8,128)(2,1)S(1)}, bf16[40,128]{1,0:T(8,128)(2,1)S(1)}) custom-call(s32[2,128]{1,0:T(2,128)} %bitcast.1, bf16[128,8192]{1,0:T(8,128)(2,1)} %grads.3, bf16[128,3072]{1,0:T(8,128)(2,1)} %inputs.3), custom_call_target="tpu_custom_call" | custom-call | tf_op jit(solution)/shard_map/pallas_call | solution.py:234
  3.0 4.1 %collective-permute-start.2 = (bf16[4,40,1408]{2,1,0:T(8,128)(2,1)S(1)}, bf16[4,40,1408]{2,1,0:T(8,128)(2,1)S(1)}, u32[]{:S(2)}, u32[]{:S(2)}) collective-permute-start(bf16[4,40,1408]{2,1,0:T(8,128)(2,1)S(1)} %get-tuple-element.25), channel_id=1, source_target_pairs={{0,8},{1,9},{2,10},{3,11},{4,0},{5,1},{6,2},{7,3},{8,12},{9,13},{1... | collective-permute-start | bytes 1351688 | tf_op jit(solution)/shard_map/ppermute | solution.py:468
  7.1 1.5 %collective-permute-start = (bf16[2,40,1408]{2,1,0:T(8,128)(2,1)S(1)}, bf16[2,40,1408]{2,1,0:T(8,128)(2,1)S(1)}, u32[]{:S(2)}, u32[]{:S(2)}) collective-permute-start(bf16[2,40,1408]{2,1,0:T(8,128)(2,1)S(1)} %get-tuple-element.23), channel_id=1, source_target_pairs={{0,2},{1,3},{2,0},{3,1},{4,6},{5,7},{6,4},{7,5},{8,10},{9,11},{10,... | collective-permute-start | bytes 675848 | tf_op jit(solution)/shard_map/ppermute | solution.py:468
  8.6 2.4 %shard_map.51 = (bf16[2,40,2816]{2,1,0:T(8,128)(2,1)S(1)}, bf16[2,40,2816]{2,1,0:T(8,128)(2,1)S(1)}, bf16[2,40,2816]{2,1,0:T(8,128)(2,1)S(1)}) custom-call(bf16[128,8192]{1,0:T(8,128)(2,1)} %grads.3, bf16[128,3072]{1,0:T(8,128)(2,1)} %inputs.3, bf16[4,40,1408]{2,1,0:T(8,128)(2,1)S(1)} %get-tuple-element.19.packed, ...), custom_call_target="tpu_custom_call" | custom-call | tf_op jit(solution)/shard_map/pallas_call | solution.py:277
  11.0 3.1 %collective-permute-done.refs_5_ = bf16[2,40,1408]{2,1,0:T(8,128)(2,1)S(1)} collective-permute-done((bf16[2,40,1408]{2,1,0:T(8,128)(2,1)S(1)}, bf16[2,40,1408]{2,1,0:T(8,128)(2,1)S(1)}, u32[]{:S(2)}, u32[]{:S(2)}) %collective-permute-start) | collective-permute-done | bytes 225312 | tf_op jit(solution)/shard_map/ppermute | solution.py:468
  14.1 0.7 %collective-permute-start.1 = (bf16[2,40,2816]{2,1,0:T(8,128)(2,1)S(1)}, bf16[2,40,2816]{2,1,0:T(8,128)(2,1)S(1)}, u32[]{:S(2)}, u32[]{:S(2)}) collective-permute-start(bf16[2,40,2816]{2,1,0:T(8,128)(2,1)S(1)} %get-tuple-element.24), channel_id=1, source_target_pairs={{4,8},{5,11},{6,10},{7,9},{8,4},{9,7},{10,6},{11,5},{20,24},{21,27... | collective-permute-start | bytes 1351688 | tf_op jit(solution)/shard_map/ppermute | solution.py:468
  14.7 1.9 %collective-permute-done.2.got = bf16[4,40,1408]{2,1,0:T(8,128)(2,1)S(1)} collective-permute-done((bf16[4,40,1408]{2,1,0:T(8,128)(2,1)S(1)}, bf16[4,40,1408]{2,1,0:T(8,128)(2,1)S(1)}, u32[]{:S(2)}, u32[]{:S(2)}) %collective-permute-start.2) | collective-permute-done | bytes 450592 | tf_op jit(solution)/shard_map/ppermute | solution.py:468
  16.7 0.1 shard_map.52
  16.8 2.5 %collective-permute-start.3 = (bf16[3,40,1408]{2,1,0:T(8,128)(2,1)S(1)}, bf16[3,40,1408]{2,1,0:T(8,128)(2,1)S(1)}, u32[]{:S(2)}, u32[]{:S(2)}) collective-permute-start(bf16[3,40,1408]{2,1,0:T(8,128)(2,1)S(1)} %get-tuple-element.28), channel_id=1, source_target_pairs={{0,4},{1,5},{2,6},{3,7},{4,0},{5,1},{6,2},{7,3},{8,12},{9,13},{10,... | collective-permute-start | bytes 1013768 | tf_op jit(solution)/shard_map/ppermute | solution.py:468
  19.3 0.0 collective-permute-start.5
  19.3 0.5 %collective-permute-start.4 = (bf16[2,40,1408]{2,1,0:T(8,128)(2,1)S(1)}, bf16[2,40,1408]{2,1,0:T(8,128)(2,1)S(1)}, u32[]{:S(2)}, u32[]{:S(2)}) collective-permute-start(bf16[2,40,1408]{2,1,0:T(8,128)(2,1)S(1)} %get-tuple-element.29.refs_7_), channel_id=1, source_target_pairs={{0,1},{1,0},{2,3},{3,2},{4,5},{5,4},{6,7},{7,6},{8,9},{9,8},{10,11... | collective-permute-start | bytes 675848 | tf_op jit(solution)/shard_map/ppermute | solution.py:468
  19.8 1.5 %collective-permute-start.9 = (bf16[2,40,1408]{2,1,0:T(8,128)(2,1)S(1)}, bf16[2,40,1408]{2,1,0:T(8,128)(2,1)S(1)}, u32[]{:S(2)}, u32[]{:S(2)}) collective-permute-start(bf16[2,40,1408]{2,1,0:T(8,128)(2,1)S(1)} %get-tuple-element.34), channel_id=1, source_target_pairs={{0,2},{1,3},{2,0},{3,1},{4,6},{5,7},{6,4},{7,5},{8,10},{9,11},{10,... | collective-permute-start | bytes 675848 | tf_op jit(solution)/shard_map/ppermute | solution.py:468
  21.3 0.0 collective-permute-done.5.refs_6_
  21.3 1.3 %collective-permute-start.8 = (bf16[2,40,2816]{2,1,0:T(8,128)(2,1)S(1)}, bf16[2,40,2816]{2,1,0:T(8,128)(2,1)S(1)}, u32[]{:S(2)}, u32[]{:S(2)}) collective-permute-start(bf16[2,40,2816]{2,1,0:T(8,128)(2,1)S(1)} %get-tuple-element.33), channel_id=1, source_target_pairs={{4,12},{5,15},{6,14},{7,13},{8,0},{9,3},{10,2},{11,1},{20,28},{21,... | collective-permute-start | bytes 1351688 | tf_op jit(solution)/shard_map/ppermute | solution.py:468
  22.6 0.0 collective-permute-done.4.refs_8_
  22.6 3.6 %collective-permute-done.3.refs_11_ = bf16[3,40,1408]{2,1,0:T(8,128)(2,1)S(1)} collective-permute-done((bf16[3,40,1408]{2,1,0:T(8,128)(2,1)S(1)}, bf16[3,40,1408]{2,1,0:T(8,128)(2,1)S(1)}, u32[]{:S(2)}, u32[]{:S(2)}) %collective-permute-start.3) | collective-permute-done | bytes 337952 | tf_op jit(solution)/shard_map/ppermute | solution.py:468
  26.3 1.6 %collective-permute-start.6 = (bf16[2,40,1408]{2,1,0:T(8,128)(2,1)S(1)}, bf16[2,40,1408]{2,1,0:T(8,128)(2,1)S(1)}, u32[]{:S(2)}, u32[]{:S(2)}) collective-permute-start(bf16[2,40,1408]{2,1,0:T(8,128)(2,1)S(1)} %get-tuple-element.37), channel_id=1, source_target_pairs={{0,2},{1,3},{2,0},{3,1},{4,6},{5,7},{6,4},{7,5},{8,10},{9,11},{10,... | collective-permute-start | bytes 675848 | tf_op jit(solution)/shard_map/ppermute | solution.py:468
  27.8 0.5 %collective-permute-start.11 = (bf16[2,40,1408]{2,1,0:T(8,128)(2,1)S(1)}, bf16[2,40,1408]{2,1,0:T(8,128)(2,1)S(1)}, u32[]{:S(2)}, u32[]{:S(2)}) collective-permute-start(bf16[2,40,1408]{2,1,0:T(8,128)(2,1)S(1)} %get-tuple-element.36), channel_id=1, source_target_pairs={{0,1},{1,0},{2,3},{3,2},{4,5},{5,4},{6,7},{7,6},{8,9},{9,8},{10,11... | collective-permute-start | bytes 675848 | tf_op jit(solution)/shard_map/ppermute | solution.py:468
  28.3 7.3 %collective-permute-done.6.refs_13_ = bf16[2,40,1408]{2,1,0:T(8,128)(2,1)S(1)} collective-permute-done((bf16[2,40,1408]{2,1,0:T(8,128)(2,1)S(1)}, bf16[2,40,1408]{2,1,0:T(8,128)(2,1)S(1)}, u32[]{:S(2)}, u32[]{:S(2)}) %collective-permute-start.6) | collective-permute-done | bytes 225312 | tf_op jit(solution)/shard_map/ppermute | solution.py:468
  35.7 0.5 %collective-permute-start.7 = (bf16[2,40,2816]{2,1,0:T(8,128)(2,1)S(1)}, bf16[2,40,2816]{2,1,0:T(8,128)(2,1)S(1)}, u32[]{:S(2)}, u32[]{:S(2)}) collective-permute-start(bf16[2,40,2816]{2,1,0:T(8,128)(2,1)S(1)} %collective-permute-done.1.refs_1_), channel_id=1, source_target_pairs={{0,1},{1,0},{2,3},{3,2},{4,5},{5,4},{6,7},{7,6},{8,9},{9,8},{10,11... | collective-permute-start | bytes 1351688 | tf_op jit(solution)/shard_map/ppermute | solution.py:468
  36.2 1.6 %collective-permute-done.8.refs_3_ = bf16[2,40,2816]{2,1,0:T(8,128)(2,1)S(1)} collective-permute-done((bf16[2,40,2816]{2,1,0:T(8,128)(2,1)S(1)}, bf16[2,40,2816]{2,1,0:T(8,128)(2,1)S(1)}, u32[]{:S(2)}, u32[]{:S(2)}) %collective-permute-start.8) | collective-permute-done | bytes 450592 | tf_op jit(solution)/shard_map/ppermute | solution.py:468
  37.8 0.1 collective-permute-start.13
  37.9 1.7 %collective-permute-done.13.refs_4_ = bf16[2,40,2816]{2,1,0:T(8,128)(2,1)S(1)} collective-permute-done((bf16[2,40,2816]{2,1,0:T(8,128)(2,1)S(1)}, bf16[2,40,2816]{2,1,0:T(8,128)(2,1)S(1)}, u32[]{:S(2)}, u32[]{:S(2)}) %collective-permute-start.13) | collective-permute-done | bytes 450592 | tf_op jit(solution)/shard_map/ppermute | solution.py:468
  39.6 7.7 %shard_map.53 = (f32[1,768,768]{2,1,0:T(8,128)}, f32[1,2048,2048]{2,1,0:T(8,128)}) custom-call(bf16[2,40,2816]{2,1,0:T(8,128)(2,1)S(1)} %get-tuple-element.21.refs_0_, bf16[2,40,2816]{2,1,0:T(8,128)(2,1)S(1)} %collective-permute-done.1.refs_1_, bf16[2,40,2816]{2,1,0:T(8,128)(2,1)S(1)} %collective-permute-done.7.refs_2_, ...), custom_call_target="tpu_custom_call" | custom-call | tf_op jit(solution)/shard_map/pallas_call | solution.py:417
  (9 shorter events, 0.1 us)
Async XLA Ops:
  3.0 13.7 %collective-permute-start.2 = (bf16[4,40,1408]{2,1,0:T(8,128)(2,1)S(1)}, bf16[4,40,1408]{2,1,0:T(8,128)(2,1)S(1)}, u32[]{:S(2)}, u32[]{:S(2)}) collective-permute-start(bf16[4,40,1408]{2,1,0:T(8,128)(2,1)S(1)} %get-tuple-element.25), channel_id=1, source_target_pairs={{0,8},{1,9},{2,10},{3,11},{4,0},{5,1},{6,2},{7,3},{8,12},{9,13},{1... | collective-permute-start | bytes 1351688 | tf_op jit(solution)/shard_map/ppermute | solution.py:468
  7.1 7.0 %collective-permute-start = (bf16[2,40,1408]{2,1,0:T(8,128)(2,1)S(1)}, bf16[2,40,1408]{2,1,0:T(8,128)(2,1)S(1)}, u32[]{:S(2)}, u32[]{:S(2)}) collective-permute-start(bf16[2,40,1408]{2,1,0:T(8,128)(2,1)S(1)} %get-tuple-element.23), channel_id=1, source_target_pairs={{0,2},{1,3},{2,0},{3,1},{4,6},{5,7},{6,4},{7,5},{8,10},{9,11},{10,... | collective-permute-start | bytes 675848 | tf_op jit(solution)/shard_map/ppermute | solution.py:468
  14.1 8.5 %collective-permute-start.1 = (bf16[2,40,2816]{2,1,0:T(8,128)(2,1)S(1)}, bf16[2,40,2816]{2,1,0:T(8,128)(2,1)S(1)}, u32[]{:S(2)}, u32[]{:S(2)}) collective-permute-start(bf16[2,40,2816]{2,1,0:T(8,128)(2,1)S(1)} %get-tuple-element.24), channel_id=1, source_target_pairs={{4,8},{5,11},{6,10},{7,9},{8,4},{9,7},{10,6},{11,5},{20,24},{21,27... | collective-permute-start | bytes 1351688 | tf_op jit(solution)/shard_map/ppermute | solution.py:468
  16.8 9.5 %collective-permute-start.3 = (bf16[3,40,1408]{2,1,0:T(8,128)(2,1)S(1)}, bf16[3,40,1408]{2,1,0:T(8,128)(2,1)S(1)}, u32[]{:S(2)}, u32[]{:S(2)}) collective-permute-start(bf16[3,40,1408]{2,1,0:T(8,128)(2,1)S(1)} %get-tuple-element.28), channel_id=1, source_target_pairs={{0,4},{1,5},{2,6},{3,7},{4,0},{5,1},{6,2},{7,3},{8,12},{9,13},{10,... | collective-permute-start | bytes 1013768 | tf_op jit(solution)/shard_map/ppermute | solution.py:468
  19.3 2.0 %collective-permute-start.5 = (bf16[2,40,1408]{2,1,0:T(8,128)(2,1)S(1)}, bf16[2,40,1408]{2,1,0:T(8,128)(2,1)S(1)}, u32[]{:S(2)}, u32[]{:S(2)}) collective-permute-start(bf16[2,40,1408]{2,1,0:T(8,128)(2,1)S(1)} %collective-permute-done.refs_5_), channel_id=1, source_target_pairs={{0,1},{1,0},{2,3},{3,2},{4,5},{5,4},{6,7},{7,6},{8,9},{9,8},{10,11... | collective-permute-start | bytes 675848 | tf_op jit(solution)/shard_map/ppermute | solution.py:468
  19.3 3.3 %collective-permute-start.4 = (bf16[2,40,1408]{2,1,0:T(8,128)(2,1)S(1)}, bf16[2,40,1408]{2,1,0:T(8,128)(2,1)S(1)}, u32[]{:S(2)}, u32[]{:S(2)}) collective-permute-start(bf16[2,40,1408]{2,1,0:T(8,128)(2,1)S(1)} %get-tuple-element.29.refs_7_), channel_id=1, source_target_pairs={{0,1},{1,0},{2,3},{3,2},{4,5},{5,4},{6,7},{7,6},{8,9},{9,8},{10,11... | collective-permute-start | bytes 675848 | tf_op jit(solution)/shard_map/ppermute | solution.py:468
  19.8 8.0 %collective-permute-start.9 = (bf16[2,40,1408]{2,1,0:T(8,128)(2,1)S(1)}, bf16[2,40,1408]{2,1,0:T(8,128)(2,1)S(1)}, u32[]{:S(2)}, u32[]{:S(2)}) collective-permute-start(bf16[2,40,1408]{2,1,0:T(8,128)(2,1)S(1)} %get-tuple-element.34), channel_id=1, source_target_pairs={{0,2},{1,3},{2,0},{3,1},{4,6},{5,7},{6,4},{7,5},{8,10},{9,11},{10,... | collective-permute-start | bytes 675848 | tf_op jit(solution)/shard_map/ppermute | solution.py:468
  21.3 16.5 %collective-permute-start.8 = (bf16[2,40,2816]{2,1,0:T(8,128)(2,1)S(1)}, bf16[2,40,2816]{2,1,0:T(8,128)(2,1)S(1)}, u32[]{:S(2)}, u32[]{:S(2)}) collective-permute-start(bf16[2,40,2816]{2,1,0:T(8,128)(2,1)S(1)} %get-tuple-element.33), channel_id=1, source_target_pairs={{4,12},{5,15},{6,14},{7,13},{8,0},{9,3},{10,2},{11,1},{20,28},{21,... | collective-permute-start | bytes 1351688 | tf_op jit(solution)/shard_map/ppermute | solution.py:468
  26.3 9.4 %collective-permute-start.6 = (bf16[2,40,1408]{2,1,0:T(8,128)(2,1)S(1)}, bf16[2,40,1408]{2,1,0:T(8,128)(2,1)S(1)}, u32[]{:S(2)}, u32[]{:S(2)}) collective-permute-start(bf16[2,40,1408]{2,1,0:T(8,128)(2,1)S(1)} %get-tuple-element.37), channel_id=1, source_target_pairs={{0,2},{1,3},{2,0},{3,1},{4,6},{5,7},{6,4},{7,5},{8,10},{9,11},{10,... | collective-permute-start | bytes 675848 | tf_op jit(solution)/shard_map/ppermute | solution.py:468
  27.8 8.3 %collective-permute-start.10 = (bf16[2,40,1408]{2,1,0:T(8,128)(2,1)S(1)}, bf16[2,40,1408]{2,1,0:T(8,128)(2,1)S(1)}, u32[]{:S(2)}, u32[]{:S(2)}) collective-permute-start(bf16[2,40,1408]{2,1,0:T(8,128)(2,1)S(1)} %collective-permute-done.9.refs_9_), channel_id=1, source_target_pairs={{0,1},{1,0},{2,3},{3,2},{4,5},{5,4},{6,7},{7,6},{8,9},{9,8},{10,11... | collective-permute-start | bytes 675848 | tf_op jit(solution)/shard_map/ppermute | solution.py:468
  27.8 10.0 %collective-permute-start.11 = (bf16[2,40,1408]{2,1,0:T(8,128)(2,1)S(1)}, bf16[2,40,1408]{2,1,0:T(8,128)(2,1)S(1)}, u32[]{:S(2)}, u32[]{:S(2)}) collective-permute-start(bf16[2,40,1408]{2,1,0:T(8,128)(2,1)S(1)} %get-tuple-element.36), channel_id=1, source_target_pairs={{0,1},{1,0},{2,3},{3,2},{4,5},{5,4},{6,7},{7,6},{8,9},{9,8},{10,11... | collective-permute-start | bytes 675848 | tf_op jit(solution)/shard_map/ppermute | solution.py:468
  35.7 2.1 %collective-permute-start.12 = (bf16[2,40,1408]{2,1,0:T(8,128)(2,1)S(1)}, bf16[2,40,1408]{2,1,0:T(8,128)(2,1)S(1)}, u32[]{:S(2)}, u32[]{:S(2)}) collective-permute-start(bf16[2,40,1408]{2,1,0:T(8,128)(2,1)S(1)} %collective-permute-done.6.refs_13_), channel_id=1, source_target_pairs={{0,1},{1,0},{2,3},{3,2},{4,5},{5,4},{6,7},{7,6},{8,9},{9,8},{10,11... | collective-permute-start | bytes 675848 | tf_op jit(solution)/shard_map/ppermute | solution.py:468
  35.7 2.2 %collective-permute-start.7 = (bf16[2,40,2816]{2,1,0:T(8,128)(2,1)S(1)}, bf16[2,40,2816]{2,1,0:T(8,128)(2,1)S(1)}, u32[]{:S(2)}, u32[]{:S(2)}) collective-permute-start(bf16[2,40,2816]{2,1,0:T(8,128)(2,1)S(1)} %collective-permute-done.1.refs_1_), channel_id=1, source_target_pairs={{0,1},{1,0},{2,3},{3,2},{4,5},{5,4},{6,7},{7,6},{8,9},{9,8},{10,11... | collective-permute-start | bytes 1351688 | tf_op jit(solution)/shard_map/ppermute | solution.py:468
  37.8 1.8 %collective-permute-start.13 = (bf16[2,40,2816]{2,1,0:T(8,128)(2,1)S(1)}, bf16[2,40,2816]{2,1,0:T(8,128)(2,1)S(1)}, u32[]{:S(2)}, u32[]{:S(2)}) collective-permute-start(bf16[2,40,2816]{2,1,0:T(8,128)(2,1)S(1)} %collective-permute-done.8.refs_3_), channel_id=1, source_target_pairs={{0,1},{1,0},{2,3},{3,2},{4,5},{5,4},{6,7},{7,6},{8,9},{9,8},{10,11... | collective-permute-start | bytes 1351688 | tf_op jit(solution)/shard_map/ppermute | solution.py:468
